TPU v7x, 256 devices: a whole 4x4x8 slice. The times are simulated.
256 devices in a mesh: expert: 64 (over z_lo, x, y, core), tensor: 4 (over z_hi).
Axes of the slice: x: 4, y: 4, z: 8 (z_hi: 4, z_lo: 2; z = z_hi * 2 + z_lo), core: 2. Of those that a mesh axis runs over, the one named last changes fastest.
Arguments:
- tokens: bfloat16 [8192, 7168], P('expert', 'tensor'), may hold values from -6 to 6
- route: int32 [8192, 2], P('expert'), may hold values from 0 to 31, all different within a row; in each aligned block of 128 rows (0 to 127, 128 to 255, ...) at most 12 rows name the same one
- probs: float32 [8192, 2], P('expert'), may hold values from 0.2 to 1
- cotangent: bfloat16 [8192, 7168], P('expert', 'tensor'), may hold values from -6 to 6
- gate_weight: bfloat16 [64, 7168, 512], P('expert', 'tensor'), may hold values from -0.0625 to 0.0625
- up_weight: bfloat16 [64, 7168, 512], P('expert', 'tensor'), may hold values from -0.0625 to 0.0625
- down_weight: bfloat16 [64, 512, 7168], P('expert', None, 'tensor'), may hold values from -0.1875 to 0.1875
Outputs:
- moe_out: bfloat16 [8192, 7168], P('expert', 'tensor')
- grad_probs: float32 [8192, 2], P('expert')
- grad_tokens: bfloat16 [8192, 7168], P('expert', 'tensor')
- grad_gate: bfloat16 [64, 7168, 512], P('expert', 'tensor')
- grad_up: bfloat16 [64, 7168, 512], P('expert', 'tensor')
- grad_down: bfloat16 [64, 512, 7168], P('expert', None, 'tensor')
Inputs may be any that keep to these rules, and one draw needn't show every extreme that they name: `route`: within each aligned block of 128 rows (the rows of one device) no expert is named more than 12 times, and in some blocks some expert exactly 12 times; the 2 entries of a row differ and every expert is named somewhere.
All inputs are finite; a program needn't handle non-finite values.
Results may differ from a plain program's by a relative error of at most 0.0064.
Values may be sent and summed in bfloat16 or wider, within the bound.
No kernel may reach another device: no remote copies, remote signals or barrier semaphores. Data moves between devices by JAX's collectives and lax.ppermute only.
A program may use at most 128 MiB of HBM per device.

v0:
```python
import jax
import jax.numpy as jnp
from jax import lax
from jax.sharding import PartitionSpec as P


def dispatch(buffer, experts, capacity):
    width = buffer.shape[1]
    doubled = jnp.repeat(buffer.reshape(experts, 1, capacity, width), 2, axis=1)
    return lax.all_to_all(
        doubled.reshape(2 * experts * capacity, width),
        "expert",
        split_axis=0,
        concat_axis=0,
        tiled=True,
    )


def select_halves(chooser, returned, experts, capacity, quarter):
    halves = returned.reshape(experts, 2, capacity, quarter)
    first_rows = halves[:, 0].reshape(experts * capacity, quarter)
    second_rows = halves[:, 1].reshape(experts * capacity, quarter)
    return jnp.dot(chooser, first_rows, preferred_element_type=jnp.float32) + jnp.dot(
        chooser, second_rows, preferred_element_type=jnp.float32
    )


def on_device(tokens, route, probs, cotangent, gate_weight, up_weight, down_weight):
    tok_rows, quarter = tokens.shape
    top_count = route.shape[1]
    devices = lax.axis_size("expert")
    experts = devices // 2
    capacity = 3 * tok_rows * top_count // (2 * experts)
    flat_route = route.reshape(tok_rows * top_count)
    onehot = (flat_route[:, None] == jnp.arange(experts, dtype=jnp.int32)[None, :]).astype(
        jnp.int32
    )
    before = jnp.cumsum(onehot, axis=0) - onehot
    slot_rank = jnp.sum(before * onehot, axis=1)
    target = flat_route * capacity + slot_rank
    selector = (target[:, None] == jnp.arange(experts * capacity, dtype=jnp.int32)[None, :]).astype(
        jnp.float32
    )
    selector_grid = selector.reshape(tok_rows, top_count, experts * capacity)
    assign = jnp.sum(selector_grid, axis=1).astype(jnp.bfloat16)
    slot_prob = jnp.sum(selector_grid * probs[:, :, None], axis=(0, 1))
    selector_bf = selector.astype(jnp.bfloat16)
    w_gate = gate_weight[0]
    w_up = up_weight[0]
    w_down = down_weight[0]
    send_rows = jnp.dot(assign.T, tokens, preferred_element_type=jnp.float32).astype(jnp.bfloat16)
    expert_in = dispatch(send_rows, experts, capacity)
    gate_part = jnp.dot(expert_in, w_gate, preferred_element_type=jnp.float32)
    up_part = jnp.dot(expert_in, w_up, preferred_element_type=jnp.float32)
    gate_val, up_val = lax.psum((gate_part, up_part), "tensor")
    hidden_full = (jax.nn.silu(gate_val) * up_val).astype(jnp.bfloat16)
    part_out = jnp.dot(hidden_full, w_down, preferred_element_type=jnp.float32).astype(jnp.bfloat16)
    returned = lax.all_to_all(part_out, "expert", split_axis=0, concat_axis=0, tiled=True)
    picked = select_halves(selector_bf, returned, experts, capacity, quarter).reshape(
        tok_rows, top_count, quarter
    )
    moe_out = jnp.sum(probs[:, :, None] * picked, axis=1).astype(jnp.bfloat16)
    cot_float = cotangent.astype(jnp.float32)
    grad_probs = lax.psum(jnp.sum(picked * cot_float[:, None, :], axis=2), "tensor")
    cot_slots = jnp.dot(assign.T, cotangent, preferred_element_type=jnp.float32)
    cot_rows = (slot_prob[:, None] * cot_slots).astype(jnp.bfloat16)
    expert_cot = dispatch(cot_rows, experts, capacity)
    hidden_part = jnp.einsum("rd,hd->rh", expert_cot, w_down, preferred_element_type=jnp.float32)
    hidden_cot = lax.psum(hidden_part, "tensor")
    gate_sig = jax.nn.sigmoid(gate_val)
    gate_cot = (hidden_cot * up_val * gate_sig * (1.0 + gate_val * (1.0 - gate_sig))).astype(
        jnp.bfloat16
    )
    up_cot = (hidden_cot * gate_val * gate_sig).astype(jnp.bfloat16)
    gate_full, up_full = (gate_cot, up_cot)
    part_in = (
        jnp.einsum("rh,dh->rd", gate_full, w_gate, preferred_element_type=jnp.float32)
        + jnp.einsum("rh,dh->rd", up_full, w_up, preferred_element_type=jnp.float32)
    ).astype(jnp.bfloat16)
    returned_in = lax.all_to_all(part_in, "expert", split_axis=0, concat_axis=0, tiled=True)
    grad_tokens = select_halves(assign, returned_in, experts, capacity, quarter).astype(
        jnp.bfloat16
    )
    grad_gate = jnp.einsum(
        "rd,rh->dh", expert_in, gate_full, preferred_element_type=jnp.float32
    ).astype(jnp.bfloat16)
    grad_up = jnp.einsum(
        "rd,rh->dh", expert_in, up_full, preferred_element_type=jnp.float32
    ).astype(jnp.bfloat16)
    grad_down = jnp.einsum(
        "rh,rd->hd", hidden_full, expert_cot, preferred_element_type=jnp.float32
    ).astype(jnp.bfloat16)
    return (moe_out, grad_probs, grad_tokens, grad_gate[None], grad_up[None], grad_down[None])


def solution(mesh):
    placed = (
        P("expert", "tensor"),
        P("expert", None),
        P("expert", None),
        P("expert", "tensor"),
        P("expert", "tensor", None),
        P("expert", "tensor", None),
        P("expert", None, "tensor"),
    )
    return jax.shard_map(
        on_device,
        mesh=mesh,
        in_specs=placed,
        out_specs=(
            P("expert", "tensor"),
            P("expert", None),
            P("expert", "tensor"),
            P("expert", "tensor", None),
            P("expert", "tensor", None),
            P("expert", None, "tensor"),
        ),
        check_vma=False,
    )
```

profile of v0, /device:TPU:32, one launch (start us, length us, event | category | flops | bytes accessed | tf_op | source)
XLA Modules:
  0.0 499.8 jit_solution(15265794373857320928)
XLA Ops:
  14.0 3.6 broadcast_in_dim.10
  17.7 9.2 %all-to-all-start = ((bf16[64,12,1792]{2,1,0:T(8,128)(2,1)}), bf16[64,12,1792]{2,1,0:T(8,128)(2,1)}, u32[]{:S(2)}, u32[]{:S(2)}) async-start(bf16[64,12,1792]{2,1,0:T(8,128)(2,1)} %bitcast.83), calls=%async_computation | async-start | bytes 7340032 | tf_op jit(solution)/shard_map/all_to_all | solution.py:10
  29.9 43.5 %all-to-all-done = bf16[64,12,1792]{2,1,0:T(8,128)(2,1)} async-done(((bf16[64,12,1792]{2,1,0:T(8,128)(2,1)}), bf16[64,12,1792]{2,1,0:T(8,128)(2,1)}, u32[]{:S(2)}, u32[]{:S(2)}) %all-to-all-start) | async-done | bytes 2752544 | tf_op jit(solution)/shard_map/all_to_all | solution.py:10
  73.4 3.7 broadcast_in_dim.11
  77.1 7.9 %all-to-all-start.2 = ((bf16[64,12,1792]{2,1,0:T(8,128)(2,1)}), bf16[64,12,1792]{2,1,0:T(8,128)(2,1)}, u32[]{:S(2)}, u32[]{:S(2)}) async-start(bf16[64,12,1792]{2,1,0:T(8,128)(2,1)} %bitcast.82), calls=%async_computation.2 | async-start | bytes 7340032 | tf_op jit(solution)/shard_map/all_to_all | solution.py:10
  85.0 5.4 %all_to_all.30 = bf16[768,1792]{1,0:T(8,128)(2,1)} reshape(bf16[64,12,1792]{2,1,0:T(8,128)(2,1)} %all-to-all-done) | data formatting | bytes 5505024 | tf_op jit(solution)/shard_map/all_to_all | solution.py:10
  90.4 4.6 fusion.13
  97.8 33.7 %all-to-all-done.2 = bf16[64,12,1792]{2,1,0:T(8,128)(2,1)} async-done(((bf16[64,12,1792]{2,1,0:T(8,128)(2,1)}), bf16[64,12,1792]{2,1,0:T(8,128)(2,1)}, u32[]{:S(2)}, u32[]{:S(2)}) %all-to-all-start.2) | async-done | bytes 2752544 | tf_op jit(solution)/shard_map/all_to_all | solution.py:10
  131.5 5.3 %all_to_all.35 = bf16[768,1792]{1,0:T(8,128)(2,1)} reshape(bf16[64,12,1792]{2,1,0:T(8,128)(2,1)} %all-to-all-done.2) | data formatting | bytes 5505024 | tf_op jit(solution)/shard_map/all_to_all | solution.py:10
  136.8 5.1 %fusion.5 = f32[768,512]{1,0:T(8,128)} fusion(bf16[768,1792]{1,0:T(8,128)(2,1)} %all_to_all.35, bf16[1,512,1792]{2,1,0:T(8,128)(2,1)} %param.13), kind=kOutput, calls=%fused_computation.18 | convolution fusion | flops 1409286144 | bytes 6160384 | tf_op jit(solution)/shard_map/rd,hd->rh/dot_general | solution.py:68
  141.9 186.2 %all-reduce.3.cloned.1.call-done = (f32[768,512]{1,0:T(8,128)}, f32[768,512]{1,0:T(8,128)}, f32[768,512]{1,0:T(8,128)}) async-done(((f32[768,512]{1,0:T(8,128)}, f32[768,512]{1,0:T(8,128)}, f32[768,512]{1,0:T(8,128)}), (f32[768,512]{1,0:T(8,128)}, f32[768,512]{1,0:T(8,128)}, f32[768,512]{1,0:T(8,128)})) %all-reduce.3.cloned.1.call-update) | async-done | bytes 4718608 | tf_op jit(solution)/shard_map/psum | solution.py:55
  336.5 5.3 %all_to_all.36 = bf16[64,12,1792]{2,1,0:T(8,128)(2,1)} reshape(bf16[768,1792]{1,0:T(8,128)(2,1)} %add_convert_fusion) | data formatting | bytes 5505024 | tf_op jit(solution)/shard_map/all_to_all | solution.py:80
  341.8 9.1 %all-to-all-start.3 = ((bf16[64,12,1792]{2,1,0:T(8,128)(2,1)}), bf16[64,12,1792]{2,1,0:T(8,128)(2,1)}, u32[]{:S(2)}, u32[]{:S(2)}) async-start(bf16[64,12,1792]{2,1,0:T(8,128)(2,1)} %all_to_all.36), calls=%async_computation.3 | async-start | bytes 7340032 | tf_op jit(solution)/shard_map/all_to_all | solution.py:80
  354.0 5.3 %all_to_all.31 = bf16[64,12,1792]{2,1,0:T(8,128)(2,1)} reshape(bf16[768,1792]{1,0:T(8,128)(2,1)} %convolution_convert_fusion) | data formatting | bytes 5505024 | tf_op jit(solution)/shard_map/all_to_all | solution.py:58
  359.3 38.1 %all-to-all-done.3 = bf16[64,12,1792]{2,1,0:T(8,128)(2,1)} async-done(((bf16[64,12,1792]{2,1,0:T(8,128)(2,1)}), bf16[64,12,1792]{2,1,0:T(8,128)(2,1)}, u32[]{:S(2)}, u32[]{:S(2)}) %all-to-all-start.3) | async-done | bytes 2752544 | tf_op jit(solution)/shard_map/all_to_all | solution.py:80
  397.4 7.9 %all-to-all-start.1 = ((bf16[64,12,1792]{2,1,0:T(8,128)(2,1)}), bf16[64,12,1792]{2,1,0:T(8,128)(2,1)}, u32[]{:S(2)}, u32[]{:S(2)}) async-start(bf16[64,12,1792]{2,1,0:T(8,128)(2,1)} %all_to_all.31), calls=%async_computation.1 | async-start | bytes 7340032 | tf_op jit(solution)/shard_map/all_to_all | solution.py:58
  410.1 4.8 fusion.3
  420.6 3.6 slice_bitcast_fusion
  424.1 3.4 reshape_squeeze.14
  430.7 21.1 %all-to-all-done.1 = bf16[64,12,1792]{2,1,0:T(8,128)(2,1)} async-done(((bf16[64,12,1792]{2,1,0:T(8,128)(2,1)}), bf16[64,12,1792]{2,1,0:T(8,128)(2,1)}, u32[]{:S(2)}, u32[]{:S(2)}) %all-to-all-start.1) | async-done | bytes 2752544 | tf_op jit(solution)/shard_map/all_to_all | solution.py:58
  451.8 3.6 slice_bitcast_fusion.2
  455.3 3.4 reshape_squeeze.12
  467.7 18.6 %psum.30 = f32[128,2]{1,0:T(8,128)S(1)} all-reduce(f32[128,2]{1,0:T(8,128)S(1)} %reduce_sum.54), channel_id=1, replica_groups=mesh['expert'=64,'tensor'=4] {'tensor'}, use_global_device_ids=true, to_apply=%region_8.9 | all-reduce | flops 256 | bytes 2048 | tf_op jit(solution)/shard_map/psum | solution.py:64
  489.5 3.4 multiply_reduce_fusion.1
  (67 shorter events, 49.7 us)
Async XLA Ops:
  7.2 83.2 %copy-start = (bf16[1,1792,512]{2,1,0:T(8,128)(2,1)S(1)}, bf16[1,1792,512]{2,1,0:T(8,128)(2,1)}, u32[]{:S(2)}) copy-start(bf16[1,1792,512]{2,1,0:T(8,128)(2,1)} %param.11) | copy-start | bytes 5505028
  17.7 55.7 %all-to-all-start = ((bf16[64,12,1792]{2,1,0:T(8,128)(2,1)}), bf16[64,12,1792]{2,1,0:T(8,128)(2,1)}, u32[]{:S(2)}, u32[]{:S(2)}) async-start(bf16[64,12,1792]{2,1,0:T(8,128)(2,1)} %bitcast.83), calls=%async_computation | async-start | bytes 7340032 | tf_op jit(solution)/shard_map/all_to_all | solution.py:10
  77.1 54.4 %all-to-all-start.2 = ((bf16[64,12,1792]{2,1,0:T(8,128)(2,1)}), bf16[64,12,1792]{2,1,0:T(8,128)(2,1)}, u32[]{:S(2)}, u32[]{:S(2)}) async-start(bf16[64,12,1792]{2,1,0:T(8,128)(2,1)} %bitcast.82), calls=%async_computation.2 | async-start | bytes 7340032 | tf_op jit(solution)/shard_map/all_to_all | solution.py:10
  85.0 243.1 %all-reduce.3.cloned.1.call-start = ((), (), s32[]{:S(2)}) async-start(), calls=%async_computation.4 | async-start | bytes 9437184 | tf_op jit(solution)/shard_map/psum | solution.py:55
  90.4 4.7 copy-start.5
  90.4 4.7 copy-start.7
  331.5 1.7 copy-start.9
  331.5 1.8 copy-start.8
  341.8 9.1 %copy-start.13 = (bf16[1,512,1792]{2,1,0:T(8,128)(2,1)S(1)}, bf16[1,512,1792]{2,1,0:T(8,128)(2,1)}, u32[]{:S(2)}) copy-start(bf16[1,512,1792]{2,1,0:T(8,128)(2,1)} %param.13) | copy-start | bytes 5505028
  341.8 55.6 %all-to-all-start.3 = ((bf16[64,12,1792]{2,1,0:T(8,128)(2,1)}), bf16[64,12,1792]{2,1,0:T(8,128)(2,1)}, u32[]{:S(2)}, u32[]{:S(2)}) async-start(bf16[64,12,1792]{2,1,0:T(8,128)(2,1)} %all_to_all.36), calls=%async_computation.3 | async-start | bytes 7340032 | tf_op jit(solution)/shard_map/all_to_all | solution.py:80
  359.3 46.0 %copy-start.12 = (f32[128,2]{0,1:T(2,128)S(1)}, f32[128,2]{0,1:T(2,128)}, u32[]{:S(2)}) copy-start(f32[128,2]{0,1:T(2,128)} %param.9) | copy-start | bytes 3076
  397.4 54.4 %all-to-all-start.1 = ((bf16[64,12,1792]{2,1,0:T(8,128)(2,1)}), bf16[64,12,1792]{2,1,0:T(8,128)(2,1)}, u32[]{:S(2)}, u32[]{:S(2)}) async-start(bf16[64,12,1792]{2,1,0:T(8,128)(2,1)} %all_to_all.31), calls=%async_computation.1 | async-start | bytes 7340032 | tf_op jit(solution)/shard_map/all_to_all | solution.py:58
  410.1 4.8 copy-start.6
  410.1 4.8 copy-start.10
  460.0 2.2 copy-start.3
  460.0 2.3 copy-start.4
  467.6 21.9 %copy-start.11 = (f32[128,2]{1,0:T(8,128)S(1)}, f32[128,2]{1,0:T(8,128)}, u32[]{:S(2)}) copy-start(f32[128,2]{1,0:T(8,128)} %copy.40) | copy-start | bytes 3076
  487.0 2.5 copy-start.2
  487.0 5.9 %copy-start.1 = (bf16[1,1792,512]{2,1,0:T(8,128)(2,1)S(1)}, bf16[1,1792,512]{2,1,0:T(8,128)(2,1)}, u32[]{:S(2)}) copy-start(bf16[1,1792,512]{2,1,0:T(8,128)(2,1)} %param.11) | copy-start | bytes 5505028
Sparse Core Ops, SparseCore 0:
  142.1 186.0 all-reduce.2
where the time goes:
time: 501 us; the launch traced here: 500 us
  waiting for transfers between devices  323 us (64%)
  local copies, waits for them, and re-layouts  57.7 us (12%)
  matrix products  43.5 us (9%)
  starting transfers between devices  34.2 us (7%)
  blocking collectives  18.6 us (4%)
  between operations  14.2 us (3%)
  other arithmetic  9.01 us (2%)
    psum x1, waiting for transfers between devices, on_device(): gate_val, up_val = lax.psum((gate_part, up_part), 'tensor')  186 us
    all_to_all x2, waiting for transfers between devices, dispatch(): lax.all_to_all(doubled.reshape(2 * experts * capacity, width), 'expert',...  77.2 us
    all_to_all x1, waiting for transfers between devices, on_device(): lax.all_to_all(part_in, 'expert', split_axis=0, concat_axis=0, tiled=True)  38.1 us
    all_to_all x1, waiting for transfers between devices, on_device(): lax.all_to_all(part_out, 'expert', split_axis=0, concat_axis=0, tiled=True)  21.1 us
    psum x1, blocking collectives, on_device(): lax.psum(jnp.sum(picked * cot_float[:, None, :], axis=2), 'tensor')  18.6 us
    all_to_all x2, starting transfers between devices, dispatch(): lax.all_to_all(doubled.reshape(2 * experts * capacity, width), 'expert',...  17.1 us
    all_to_all x2, local copies, waits for them, and re-layouts, dispatch(): lax.all_to_all(doubled.reshape(2 * experts * capacity, width), 'expert',...  10.7 us
  transfers between devices with their start and end apart: 5, of which 5 were waited for; matrix products, arithmetic and copies ran while one was open for 8% of the time, Pallas kernels for 0%

commit v1 on v0

v1 whole, which is shorter than its diff:
```python
import jax
import jax.numpy as jnp
from jax import lax
from jax.sharding import Mesh, PartitionSpec as P

BF = jnp.bfloat16
F32 = jnp.float32
PAIR = [(0, 1), (1, 0)]
EDGE_A = [(0, 1), (1, 0), (2, 3), (3, 2)]
EDGE_B = [(0, 3), (3, 0), (1, 2), (2, 1)]


def swap(value, axis):
    return lax.ppermute(value, axis, PAIR)


def cross(value, edge):
    return lax.ppermute(value, "tensor", edge)


def pick_block(value, index):
    return lax.dynamic_index_in_dim(value, index, 0, keepdims=False)


def scatter_sum(value, first_bit, second_bit, first_edge, second_edge):
    rows, width = value.shape
    blocks = value.reshape(2, 2, rows // 4, width)
    away = pick_block(blocks, 1 - first_bit).astype(BF)
    mine = pick_block(blocks, first_bit) + cross(away, first_edge).astype(F32)
    away = pick_block(mine, 1 - second_bit).astype(BF)
    return pick_block(mine, second_bit) + cross(away, second_edge).astype(F32)


def in_order(mine, other, bit):
    return jnp.where(
        bit == 0, jnp.concatenate([mine, other], 0), jnp.concatenate([other, mine], 0)
    )


def gather_rows(value, first_bit, second_bit, first_edge, second_edge):
    pair = in_order(value, cross(value, second_edge), second_bit)
    return in_order(pair, cross(pair, first_edge), first_bit)


def dot(a, b, dims):
    return lax.dot_general(a, b, (dims, ((), ())), preferred_element_type=F32)


NN = ((1,), (0,))
NT = ((1,), (1,))
TN = ((0,), (0,))


def on_device(tokens, route, probs, cotangent, gate_weight, up_weight, down_weight):
    tok_rows, quarter = tokens.shape
    top_count = route.shape[1]
    planes = lax.axis_size("z")
    chips = lax.axis_size("x") * lax.axis_size("y")
    experts = planes * chips
    capacity = 3 * tok_rows * top_count // (2 * experts)
    slots = chips * planes * capacity
    z_index = lax.axis_index("z")
    t_index = lax.axis_index("tensor")
    bit_b = t_index // 2
    bit_a = (t_index + 1) // 2 % 2
    w_gate, w_up, w_down = gate_weight[0], up_weight[0], down_weight[0]

    tok_peer = swap(tokens, "z")
    cot_peer = swap(cotangent, "z")

    flat_route = route.reshape(tok_rows * top_count)
    onehot = flat_route[:, None] == jnp.arange(experts, dtype=jnp.int32)[None, :]
    picks = tok_rows * top_count
    earlier = (jnp.arange(picks)[:, None] > jnp.arange(picks)[None, :]).astype(BF)
    before = dot(earlier, onehot.astype(BF), NN)
    rank = jnp.sum(jnp.where(onehot, before, 0.0), axis=1).astype(jnp.int32)
    slot = flat_route // chips * slots + flat_route % chips * (planes * capacity) + rank
    packed = jnp.concatenate(
        [slot.reshape(tok_rows, top_count).T.astype(F32), probs.T], 0
    )
    packed_peer = swap(packed, "z")

    def seen(pack, place):
        local = pack[:top_count].astype(jnp.int32) - z_index * slots + place * capacity
        inside = (pack[:top_count] >= (z_index * slots).astype(F32)) & (
            pack[:top_count] < ((z_index + 1) * slots).astype(F32)
        )
        return jnp.where(inside, local, -1)

    local = jnp.concatenate([seen(packed, 0), seen(packed_peer, 1)], 1)
    prob = jnp.concatenate([packed[top_count:], packed_peer[top_count:]], 1)
    selector = local[:, None, :] == jnp.arange(slots, dtype=jnp.int32)[None, :, None]
    assign = jnp.any(selector, axis=0).astype(BF)
    slot_prob = jnp.sum(jnp.where(selector, prob[:, None, :], 0.0), axis=(0, 2))

    def dispatch(rows):
        sent = lax.all_to_all(
            rows.reshape(chips, planes * capacity, quarter),
            ("x", "y"),
            split_axis=0,
            concat_axis=0,
            tiled=True,
        ).reshape(slots, quarter)
        return sent, swap(sent, "core")

    tok_all = jnp.concatenate([tokens, tok_peer], 0)
    cot_all = jnp.concatenate([cotangent, cot_peer], 0)
    in_mine, in_other = dispatch(dot(assign, tok_all, NN).astype(BF))
    cot_mine, cot_other = dispatch((slot_prob[:, None] * dot(assign, cot_all, NN)).astype(BF))

    first = (bit_a, bit_b, EDGE_A, EDGE_B)
    second = (bit_b, bit_a, EDGE_B, EDGE_A)

    def gate_up(rows):
        return jnp.concatenate([dot(rows, w_gate, NN), dot(rows, w_up, NN)], 1)

    gu_mine = scatter_sum(gate_up(in_mine), *first)
    gu_other = scatter_sum(gate_up(in_other), *second)
    hc_mine = scatter_sum(dot(cot_mine, w_down, NT), *first)
    hc_other = scatter_sum(dot(cot_other, w_down, NT), *second)
    half = w_gate.shape[1]

    def forward(gu):
        gate, up = gu[:, :half], gu[:, half:]
        return (jax.nn.silu(gate) * up).astype(BF)

    def backward(gu, hc):
        gate, up = gu[:, :half], gu[:, half:]
        sig = jax.nn.sigmoid(gate)
        gate_cot = (hc * up * sig * (1.0 + gate * (1.0 - sig))).astype(BF)
        up_cot = (hc * gate * sig).astype(BF)
        return jnp.concatenate([gate_cot, up_cot], 1)

    hid_mine = gather_rows(forward(gu_mine), *first)
    hid_other = gather_rows(forward(gu_other), *second)
    gc_mine = gather_rows(backward(gu_mine, hc_mine), *first)
    gc_other = gather_rows(backward(gu_other, hc_other), *second)

    def send_back(product, mine, other):
        theirs = swap(product(other).astype(BF), "core")
        rows = (product(mine) + theirs.astype(F32)).astype(BF)
        return lax.all_to_all(
            rows.reshape(chips, planes * capacity, quarter),
            ("x", "y"),
            split_axis=0,
            concat_axis=0,
            tiled=True,
        ).reshape(slots, quarter)

    def out_rows(rows):
        return dot(rows, w_down, NN)

    def in_rows(rows):
        return dot(rows[:, :half], w_gate, NT) + dot(rows[:, half:], w_up, NT)

    returned = send_back(out_rows, hid_mine, hid_other)
    returned_in = send_back(in_rows, gc_mine, gc_other)

    picked = [dot(selector[k].astype(BF), returned, TN) for k in range(top_count)]
    partial = sum(prob[k][:, None] * picked[k] for k in range(top_count))
    cot_float = cot_all.astype(F32)
    grad_p = jnp.stack([jnp.sum(picked[k] * cot_float, axis=1) for k in range(top_count)])
    moe_out = (partial[:tok_rows] + swap(partial[tok_rows:].astype(BF), "z").astype(F32)).astype(BF)
    grad_p = grad_p[:, :tok_rows] + swap(grad_p[:, tok_rows:], "z")
    grad_p = grad_p + cross(grad_p, EDGE_A)
    grad_p = grad_p + cross(grad_p, EDGE_B)

    tok_part = dot(assign, returned_in, TN)
    grad_tokens = (tok_part[:tok_rows] + swap(tok_part[tok_rows:].astype(BF), "z").astype(F32)).astype(BF)

    rows_in = jnp.concatenate([in_mine, in_other], 0)
    rows_cot = jnp.concatenate([cot_mine, cot_other], 0)
    hidden = jnp.concatenate([hid_mine, hid_other], 0)
    cots = jnp.concatenate([gc_mine, gc_other], 0)
    grad_gate = dot(rows_in, cots[:, :half], TN).astype(BF)
    grad_up = dot(rows_in, cots[:, half:], TN).astype(BF)
    grad_down = dot(hidden, rows_cot, TN).astype(BF)
    return (moe_out, grad_p.T, grad_tokens, grad_gate[None], grad_up[None], grad_down[None])


def solution(mesh):
    lanes = ("z", "x", "y", "core")
    fine = Mesh(mesh.devices.reshape(2, 4, 4, 2, 4), lanes + ("tensor",))
    placed = (
        P(lanes, "tensor"),
        P(lanes, None),
        P(lanes, None),
        P(lanes, "tensor"),
        P(lanes, "tensor", None),
        P(lanes, "tensor", None),
        P(lanes, None, "tensor"),
    )
    return jax.shard_map(
        on_device,
        mesh=fine,
        in_specs=placed,
        out_specs=(
            P(lanes, "tensor"),
            P(lanes, None),
            P(lanes, "tensor"),
            P(lanes, "tensor", None),
            P(lanes, "tensor", None),
            P(lanes, None, "tensor"),
        ),
        check_vma=False,
    )
```

time: 501 us -> 282 us (0.56)
  waiting for transfers between devices: 323 us -> 146 us
  local copies, waits for them, and re-layouts: 57.7 us -> 6.07 us
  starting transfers between devices: 34.2 us -> 69.7 us
  blocking collectives: 18.6 us -> 0 us
  between operations: 14.2 us -> 1.37 us
    psum x1 -> x0, waiting for transfers between devices: 186 us -> none  [on_device(): gate_val, up_val = lax.psum((gate_part, up_part), 'tensor')]
    ppermute x0 -> x28, waiting for transfers between devices: none -> 119 us  [the longest x18 88.4 us: cross(): return lax.ppermute(value, 'tensor', edge)]
    all_to_all x4, waiting for transfers between devices: 136 us -> 26.7 us  [the longest x2 22 us: dispatch(): lax.all_to_all(rows.reshape(chips, planes * capacity, quarter), ('x', 'y'...]
    ppermute x0 -> x28, starting transfers between devices: none -> 49.7 us  [the longest x18 39.9 us: cross(): return lax.ppermute(value, 'tensor', edge)]
    all_to_all x4 -> x0, local copies, waits for them, and re-layouts: 21.3 us -> none  [the longest x2 10.7 us: dispatch(): lax.all_to_all(doubled.reshape(2 * experts * capacity, width), 'expert',...]
    psum x1 -> x0, blocking collectives: 18.6 us -> none  [on_device(): lax.psum(jnp.sum(picked * cot_float[:, None, :], axis=2), 'tensor')]
    all_to_all x4, starting transfers between devices: 34.1 us -> 19.9 us  [the longest x2 11.6 us: dispatch(): lax.all_to_all(rows.reshape(chips, planes * capacity, quarter), ('x', 'y'...]
    another operation x5 -> x0, local copies, waits for them, and re-layouts: 8.46 us -> none  [the longest x2 6.87 us: select_halves(): first_rows = halves[:, 0].reshape(experts * capacity, quarter)]
  transfers between devices with their start and end apart: 5 -> 32, of which waited for: 5 -> 19; matrix products, arithmetic and copies ran while one was open for 8% -> 20% of each run, Pallas kernels for 0% -> 0%
where the time goes in v1:
time: 282 us; the launch traced here: 280 us
  waiting for transfers between devices  146 us (52%)
  starting transfers between devices  69.7 us (25%)
  matrix products  46.5 us (16%)
  other arithmetic  10.8 us (4%)
  local copies, waits for them, and re-layouts  6.07 us (2%)
    ppermute x18, waiting for transfers between devices, cross(): return lax.ppermute(value, 'tensor', edge)  88.4 us
    dot_general x21, matrix products, dot(): return lax.dot_general(a, b, (dims, ((), ())), preferred_element_type=F32)  46.5 us
    ppermute x18, starting transfers between devices, cross(): return lax.ppermute(value, 'tensor', edge)  39.9 us
    ppermute x10, waiting for transfers between devices, swap(): return lax.ppermute(value, axis, PAIR)  30.9 us
    all_to_all x2, waiting for transfers between devices, dispatch(): lax.all_to_all(rows.reshape(chips, planes * capacity, quarter), ('x', 'y'...  22 us
    all_to_all x2, starting transfers between devices, dispatch(): lax.all_to_all(rows.reshape(chips, planes * capacity, quarter), ('x', 'y'...  11.6 us
    ppermute x10, starting transfers between devices, swap(): return lax.ppermute(value, axis, PAIR)  9.8 us
    all_to_all x2, starting transfers between devices, send_back(): lax.all_to_all(rows.reshape(chips, planes * capacity, quarter), ('x', 'y'...  8.32 us
  transfers between devices with their start and end apart: 32, of which 19 were waited for; matrix products, arithmetic and copies ran while one was open for 20% of the time, Pallas kernels for 0%

profile of v1, /device:TPU:32, one launch (start us, length us, event | category | flops | bytes accessed | tf_op | source)
XLA Modules:
  0.0 280.4 jit_solution(2885338589030127595)
XLA Ops:
  10.0 7.7 %collective-permute-done.1 = bf16[128,1792]{1,0:T(8,128)(2,1)S(1)} collective-permute-done((bf16[128,1792]{1,0:T(8,128)(2,1)}, bf16[128,1792]{1,0:T(8,128)(2,1)S(1)}, u32[]{:S(2)}, u32[]{:S(2)}) %collective-permute-start.1) | collective-permute-done | bytes 458784 | tf_op jit(solution)/shard_map/ppermute | solution.py:14
  20.3 7.2 %all-to-all-start = ((bf16[16,24,1792]{2,1,0:T(8,128)(2,1)}), bf16[16,24,1792]{2,1,0:T(8,128)(2,1)}, u32[]{:S(2)}, u32[]{:S(2)}) async-start(bf16[16,24,1792]{2,1,0:T(8,128)(2,1)} %bitcast.130), calls=%async_computation | async-start | bytes 2752512 | tf_op jit(solution)/shard_map/all_to_all | solution.py:97
  28.6 10.2 %collective-permute-done.13 = bf16[128,1792]{1,0:T(8,128)(2,1)} collective-permute-done((bf16[128,1792]{1,0:T(8,128)(2,1)S(1)}, bf16[128,1792]{1,0:T(8,128)(2,1)}, u32[]{:S(2)}, u32[]{:S(2)}) %collective-permute-start.13) | collective-permute-done | bytes 458784 | tf_op jit(solution)/shard_map/ppermute | solution.py:14
  41.5 6.5 %all-to-all-done = bf16[16,24,1792]{2,1,0:T(8,128)(2,1)} async-done(((bf16[16,24,1792]{2,1,0:T(8,128)(2,1)}), bf16[16,24,1792]{2,1,0:T(8,128)(2,1)}, u32[]{:S(2)}, u32[]{:S(2)}) %all-to-all-start) | async-done | bytes 1376288 | tf_op jit(solution)/shard_map/all_to_all | solution.py:97
  48.0 4.4 %all-to-all-start.2 = ((bf16[16,24,1792]{2,1,0:T(8,128)(2,1)}), bf16[16,24,1792]{2,1,0:T(8,128)(2,1)}, u32[]{:S(2)}, u32[]{:S(2)}) async-start(bf16[16,24,1792]{2,1,0:T(8,128)(2,1)} %bitcast.124), calls=%async_computation.2 | async-start | bytes 2752512 | tf_op jit(solution)/shard_map/all_to_all | solution.py:97
  55.3 15.5 %all-to-all-done.2 = bf16[16,24,1792]{2,1,0:T(8,128)(2,1)} async-done(((bf16[16,24,1792]{2,1,0:T(8,128)(2,1)}), bf16[16,24,1792]{2,1,0:T(8,128)(2,1)}, u32[]{:S(2)}, u32[]{:S(2)}) %all-to-all-start.2) | async-done | bytes 1376288 | tf_op jit(solution)/shard_map/all_to_all | solution.py:97
  81.2 10.4 %collective-permute-done.17 = bf16[2,96,512]{2,1,0:T(8,128)(2,1)} collective-permute-done((bf16[2,96,512]{2,1,0:T(8,128)(2,1)}, bf16[2,96,512]{2,1,0:T(8,128)(2,1)}, u32[]{:S(2)}, u32[]{:S(2)}) %collective-permute-start.17) | collective-permute-done | bytes 196640 | tf_op jit(solution)/shard_map/ppermute | solution.py:18
  92.8 7.7 %collective-permute-start.18 = (bf16[96,512]{1,0:T(8,128)(2,1)S(1)}, bf16[96,512]{1,0:T(8,128)(2,1)S(1)}, u32[]{:S(2)}, u32[]{:S(2)}) collective-permute-start(bf16[96,512]{1,0:T(8,128)(2,1)S(1)} %fusion.60), channel_id=1, source_target_pairs={{0,3},{3,0},{1,2},{2,1},{4,7},{7,4},{5,6},{6,5},{8,11},{11,8},{9,1... | collective-permute-start | bytes 294920 | tf_op jit(solution)/shard_map/ppermute | solution.py:18
  101.8 4.5 %collective-permute-start.3 = (bf16[96,1024]{1,0:T(8,128)(2,1)S(1)}, bf16[96,1024]{1,0:T(8,128)(2,1)S(1)}, u32[]{:S(2)}, u32[]{:S(2)}) collective-permute-start(bf16[96,1024]{1,0:T(8,128)(2,1)S(1)} %fusion.56), channel_id=1, source_target_pairs={{0,3},{3,0},{1,2},{2,1},{4,7},{7,4},{5,6},{6,5},{8,11},{11,8},{9,1... | collective-permute-start | bytes 589832 | tf_op jit(solution)/shard_map/ppermute | solution.py:18
  112.3 4.3 %collective-permute-start.22 = (bf16[2,96,512]{2,1,0:T(8,128)(2,1)S(1)}, bf16[2,96,512]{2,1,0:T(8,128)(2,1)S(1)}, u32[]{:S(2)}, u32[]{:S(2)}) collective-permute-start(bf16[2,96,512]{2,1,0:T(8,128)(2,1)S(1)} %fusion.59), channel_id=1, source_target_pairs={{0,3},{3,0},{1,2},{2,1},{4,7},{7,4},{5,6},{6,5},{8,11},{11,8},{9,1... | collective-permute-start | bytes 589832 | tf_op jit(solution)/shard_map/ppermute | solution.py:18
  116.6 18.4 %collective-permute-done.7 = bf16[2,96,1024]{2,1,0:T(8,128)(2,1)S(1)} collective-permute-done((bf16[2,96,1024]{2,1,0:T(8,128)(2,1)S(1)}, bf16[2,96,1024]{2,1,0:T(8,128)(2,1)S(1)}, u32[]{:S(2)}, u32[]{:S(2)}) %collective-permute-start.7) | collective-permute-done | bytes 393248 | tf_op jit(solution)/shard_map/ppermute | solution.py:18
  139.2 7.6 %collective-permute-done.8 = bf16[96,1024]{1,0:T(8,128)(2,1)S(1)} collective-permute-done((bf16[96,1024]{1,0:T(8,128)(2,1)S(1)}, bf16[96,1024]{1,0:T(8,128)(2,1)S(1)}, u32[]{:S(2)}, u32[]{:S(2)}) %collective-permute-start.8) | collective-permute-done | bytes 196640 | tf_op jit(solution)/shard_map/ppermute | solution.py:18
  151.9 8.4 %collective-permute-done.9 = bf16[96,512]{1,0:T(8,128)(2,1)S(1)} collective-permute-done((bf16[96,512]{1,0:T(8,128)(2,1)S(1)}, bf16[96,512]{1,0:T(8,128)(2,1)S(1)}, u32[]{:S(2)}, u32[]{:S(2)}) %collective-permute-start.9) | collective-permute-done | bytes 98336 | tf_op jit(solution)/shard_map/ppermute | solution.py:18
  166.7 15.6 %collective-permute-done.10 = bf16[192,512]{1,0:T(8,128)(2,1)S(1)} collective-permute-done((bf16[192,512]{1,0:T(8,128)(2,1)S(1)}, bf16[192,512]{1,0:T(8,128)(2,1)S(1)}, u32[]{:S(2)}, u32[]{:S(2)}) %collective-permute-start.10) | collective-permute-done | bytes 196640 | tf_op jit(solution)/shard_map/ppermute | solution.py:18
  183.8 4.2 %collective-permute-start.19 = (bf16[96,1024]{1,0:T(8,128)(2,1)S(1)}, bf16[96,1024]{1,0:T(8,128)(2,1)S(1)}, u32[]{:S(2)}, u32[]{:S(2)}) collective-permute-start(bf16[96,1024]{1,0:T(8,128)(2,1)S(1)} %pad_maximum_fusion.7), channel_id=1, source_target_pairs={{0,3},{3,0},{1,2},{2,1},{4,7},{7,4},{5,6},{6,5},{8,11},{11,8},{9,1... | collective-permute-start | bytes 589832 | tf_op jit(solution)/shard_map/ppermute | solution.py:18
  188.0 11.2 %collective-permute-done.4 = bf16[96,512]{1,0:T(8,128)(2,1)S(1)} collective-permute-done((bf16[96,512]{1,0:T(8,128)(2,1)S(1)}, bf16[96,512]{1,0:T(8,128)(2,1)S(1)}, u32[]{:S(2)}, u32[]{:S(2)}) %collective-permute-start.4) | collective-permute-done | bytes 98336 | tf_op jit(solution)/shard_map/ppermute | solution.py:18
  206.4 9.2 %collective-permute-done.5 = bf16[192,512]{1,0:T(8,128)(2,1)S(1)} collective-permute-done((bf16[192,512]{1,0:T(8,128)(2,1)S(1)}, bf16[192,512]{1,0:T(8,128)(2,1)S(1)}, u32[]{:S(2)}, u32[]{:S(2)}) %collective-permute-start.5) | collective-permute-done | bytes 196640 | tf_op jit(solution)/shard_map/ppermute | solution.py:18
  231.7 4.7 %all-to-all-done.1 = bf16[16,24,1792]{2,1,0:T(8,128)(2,1)S(1)} async-done(((bf16[16,24,1792]{2,1,0:T(8,128)(2,1)}), bf16[16,24,1792]{2,1,0:T(8,128)(2,1)S(1)}, u32[]{:S(2)}, u32[]{:S(2)}) %all-to-all-start.1) | async-done | bytes 1376288 | tf_op jit(solution)/shard_map/all_to_all | solution.py:142
  236.4 4.4 %all-to-all-start.3 = ((bf16[16,24,1792]{2,1,0:T(8,128)(2,1)}), bf16[16,24,1792]{2,1,0:T(8,128)(2,1)}, u32[]{:S(2)}, u32[]{:S(2)}) async-start(bf16[16,24,1792]{2,1,0:T(8,128)(2,1)} %bitcast.125), calls=%async_computation.3 | async-start | bytes 2752512 | tf_op jit(solution)/shard_map/all_to_all | solution.py:142
  242.7 4.6 %collective-permute-start.14 = (f32[2,128]{1,0:T(2,128)S(1)}, f32[2,128]{1,0:T(2,128)S(1)}, u32[]{:S(2)}, u32[]{:S(2)}) collective-permute-start(f32[2,128]{1,0:T(2,128)S(1)} %pad_maximum_fusion.11), channel_id=1, source_target_pairs={{0,128},{128,0},{1,129},{129,1},{2,130},{130,2},{3,131},{131,3},{4... | collective-permute-start | bytes 3080 | tf_op jit(solution)/shard_map/ppermute | solution.py:14
  247.2 4.2 %fusion.10 = bf16[1,512,1792]{2,1,0:T(8,128)(2,1)} fusion(bf16[384,1792]{1,0:T(8,128)(2,1)S(1)} %copy-done.21, bf16[384,1792]{1,0:T(8,128)(2,1)} %bitcast.34, bf16[384,512]{1,0:T(8,128)(2,1)S(1)} %copy-done.17, bf16[384,512]{1,0:T(8,128)(2,1)S(1)} %copy-done.19), kind=kOutput, calls=%fused_computation.20 | convolution fusion | flops 1417281536 | bytes 5373952 | tf_op jit(solution)/shard_map/dot_general | solution.py:46
  252.6 4.6 %fusion.8 = bf16[1,1792,512]{2,1,0:T(8,128)(2,1)} fusion(bf16[384,1792]{1,0:T(8,128)(2,1)} %collective-permute-done.6, bf16[384,1792]{1,0:T(8,128)(2,1)} %bitcast.5, bf16[384,1024]{1,0:T(8,128)(2,1)S(1)} %copy-done.10, bf16[384,1024]{1,0:T(8,128)(2,1)S(1)} %maximum_select_fusion.1), kind=kOutput, calls=%fused_computation.18 | convolution fusion | flops 1417281536 | bytes 6160384 | tf_op jit(solution)/shard_map/dot_general | solution.py:46
  259.0 4.6 %fusion.9 = bf16[1,1792,512]{2,1,0:T(8,128)(2,1)} fusion(bf16[384,1792]{1,0:T(8,128)(2,1)} %collective-permute-done.6, bf16[384,1792]{1,0:T(8,128)(2,1)} %bitcast.5, bf16[384,1024]{1,0:T(8,128)(2,1)S(1)} %maximum_select_fusion.1, bf16[384,1024]{1,0:T(8,128)(2,1)S(1)} %copy-done.10), kind=kOutput, calls=%fused_computation.19 | convolution fusion | flops 1417281536 | bytes 6160384 | tf_op jit(solution)/shard_map/dot_general | solution.py:46
  268.7 6.0 %collective-permute-done.12 = bf16[128,1792]{1,0:T(8,128)(2,1)S(1)} collective-permute-done((bf16[128,1792]{1,0:T(8,128)(2,1)S(1)}, bf16[128,1792]{1,0:T(8,128)(2,1)S(1)}, u32[]{:S(2)}, u32[]{:S(2)}) %collective-permute-start.12) | collective-permute-done | bytes 458784 | tf_op jit(solution)/shard_map/ppermute | solution.py:14
  (163 shorter events, 93.0 us)
Async XLA Ops:
  5.8 11.8 %collective-permute-start.1 = (bf16[128,1792]{1,0:T(8,128)(2,1)}, bf16[128,1792]{1,0:T(8,128)(2,1)S(1)}, u32[]{:S(2)}, u32[]{:S(2)}) collective-permute-start(bf16[128,1792]{1,0:T(8,128)(2,1)} %param.7), channel_id=1, source_target_pairs={{0,128},{128,0},{1,129},{129,1},{2,130},{130,2},{3,131},{131,3},{4... | collective-permute-start | bytes 1376264 | tf_op jit(solution)/shard_map/ppermute | solution.py:14
  20.3 27.7 %all-to-all-start = ((bf16[16,24,1792]{2,1,0:T(8,128)(2,1)}), bf16[16,24,1792]{2,1,0:T(8,128)(2,1)}, u32[]{:S(2)}, u32[]{:S(2)}) async-start(bf16[16,24,1792]{2,1,0:T(8,128)(2,1)} %bitcast.130), calls=%async_computation | async-start | bytes 2752512 | tf_op jit(solution)/shard_map/all_to_all | solution.py:97
  48.0 22.8 %all-to-all-start.2 = ((bf16[16,24,1792]{2,1,0:T(8,128)(2,1)}), bf16[16,24,1792]{2,1,0:T(8,128)(2,1)}, u32[]{:S(2)}, u32[]{:S(2)}) async-start(bf16[16,24,1792]{2,1,0:T(8,128)(2,1)} %bitcast.124), calls=%async_computation.2 | async-start | bytes 2752512 | tf_op jit(solution)/shard_map/all_to_all | solution.py:97
  52.4 53.9 %collective-permute-start.6 = (bf16[384,1792]{1,0:T(8,128)(2,1)}, bf16[384,1792]{1,0:T(8,128)(2,1)}, u32[]{:S(2)}, u32[]{:S(2)}) collective-permute-start(bf16[384,1792]{1,0:T(8,128)(2,1)} %bitcast.5), channel_id=1, source_target_pairs={{0,4},{4,0},{1,5},{5,1},{2,6},{6,2},{3,7},{7,3},{8,12},{12,8},{9,1... | collective-permute-start | bytes 4128776 | tf_op jit(solution)/shard_map/ppermute | solution.py:14
  74.2 17.5 %collective-permute-start.17 = (bf16[2,96,512]{2,1,0:T(8,128)(2,1)}, bf16[2,96,512]{2,1,0:T(8,128)(2,1)}, u32[]{:S(2)}, u32[]{:S(2)}) collective-permute-start(bf16[2,96,512]{2,1,0:T(8,128)(2,1)} %fusion.58), channel_id=1, source_target_pairs={{0,1},{1,0},{2,3},{3,2},{4,5},{5,4},{6,7},{7,6},{8,9},{9,8},{10,11... | collective-permute-start | bytes 589832 | tf_op jit(solution)/shard_map/ppermute | solution.py:18
  81.0 19.6 %collective-permute-start.2 = (bf16[2,96,1024]{2,1,0:T(8,128)(2,1)S(1)}, bf16[2,96,1024]{2,1,0:T(8,128)(2,1)S(1)}, u32[]{:S(2)}, u32[]{:S(2)}) collective-permute-start(bf16[2,96,1024]{2,1,0:T(8,128)(2,1)S(1)} %fusion.48), channel_id=1, source_target_pairs={{0,1},{1,0},{2,3},{3,2},{4,5},{5,4},{6,7},{7,6},{8,9},{9,8},{10,11... | collective-permute-start | bytes 1179656 | tf_op jit(solution)/shard_map/ppermute | solution.py:18
  81.1 30.1 %collective-permute-start.21 = (bf16[384,1792]{1,0:T(8,128)(2,1)}, bf16[384,1792]{1,0:T(8,128)(2,1)S(1)}, u32[]{:S(2)}, u32[]{:S(2)}) collective-permute-start(bf16[384,1792]{1,0:T(8,128)(2,1)} %bitcast.34), channel_id=1, source_target_pairs={{0,4},{4,0},{1,5},{5,1},{2,6},{6,2},{3,7},{7,3},{8,12},{12,8},{9,1... | collective-permute-start | bytes 4128776 | tf_op jit(solution)/shard_map/ppermute | solution.py:14
  92.8 90.7 %collective-permute-start.18 = (bf16[96,512]{1,0:T(8,128)(2,1)S(1)}, bf16[96,512]{1,0:T(8,128)(2,1)S(1)}, u32[]{:S(2)}, u32[]{:S(2)}) collective-permute-start(bf16[96,512]{1,0:T(8,128)(2,1)S(1)} %fusion.60), channel_id=1, source_target_pairs={{0,3},{3,0},{1,2},{2,1},{4,7},{7,4},{5,6},{6,5},{8,11},{11,8},{9,1... | collective-permute-start | bytes 294920 | tf_op jit(solution)/shard_map/ppermute | solution.py:18
  101.8 61.6 %collective-permute-start.3 = (bf16[96,1024]{1,0:T(8,128)(2,1)S(1)}, bf16[96,1024]{1,0:T(8,128)(2,1)S(1)}, u32[]{:S(2)}, u32[]{:S(2)}) collective-permute-start(bf16[96,1024]{1,0:T(8,128)(2,1)S(1)} %fusion.56), channel_id=1, source_target_pairs={{0,3},{3,0},{1,2},{2,1},{4,7},{7,4},{5,6},{6,5},{8,11},{11,8},{9,1... | collective-permute-start | bytes 589832 | tf_op jit(solution)/shard_map/ppermute | solution.py:18
  111.0 24.0 %collective-permute-start.7 = (bf16[2,96,1024]{2,1,0:T(8,128)(2,1)S(1)}, bf16[2,96,1024]{2,1,0:T(8,128)(2,1)S(1)}, u32[]{:S(2)}, u32[]{:S(2)}) collective-permute-start(bf16[2,96,1024]{2,1,0:T(8,128)(2,1)S(1)} %fusion.49), channel_id=1, source_target_pairs={{0,3},{3,0},{1,2},{2,1},{4,7},{7,4},{5,6},{6,5},{8,11},{11,8},{9,1... | collective-permute-start | bytes 1179656 | tf_op jit(solution)/shard_map/ppermute | solution.py:18
  112.3 26.8 %collective-permute-start.22 = (bf16[2,96,512]{2,1,0:T(8,128)(2,1)S(1)}, bf16[2,96,512]{2,1,0:T(8,128)(2,1)S(1)}, u32[]{:S(2)}, u32[]{:S(2)}) collective-permute-start(bf16[2,96,512]{2,1,0:T(8,128)(2,1)S(1)} %fusion.59), channel_id=1, source_target_pairs={{0,3},{3,0},{1,2},{2,1},{4,7},{7,4},{5,6},{6,5},{8,11},{11,8},{9,1... | collective-permute-start | bytes 589832 | tf_op jit(solution)/shard_map/ppermute | solution.py:18
  148.3 12.0 %collective-permute-start.9 = (bf16[96,512]{1,0:T(8,128)(2,1)S(1)}, bf16[96,512]{1,0:T(8,128)(2,1)S(1)}, u32[]{:S(2)}, u32[]{:S(2)}) collective-permute-start(bf16[96,512]{1,0:T(8,128)(2,1)S(1)} %get-tuple-element.15), channel_id=1, source_target_pairs={{0,1},{1,0},{2,3},{3,2},{4,5},{5,4},{6,7},{7,6},{8,9},{9,8},{10,11... | collective-permute-start | bytes 294920 | tf_op jit(solution)/shard_map/ppermute | solution.py:18
  151.8 12.1 %collective-permute-start.24 = (bf16[96,1024]{1,0:T(8,128)(2,1)S(1)}, bf16[96,1024]{1,0:T(8,128)(2,1)S(1)}, u32[]{:S(2)}, u32[]{:S(2)}) collective-permute-start(bf16[96,1024]{1,0:T(8,128)(2,1)S(1)} %pad_maximum_fusion.8), channel_id=1, source_target_pairs={{0,1},{1,0},{2,3},{3,2},{4,5},{5,4},{6,7},{7,6},{8,9},{9,8},{10,11... | collective-permute-start | bytes 589832 | tf_op jit(solution)/shard_map/ppermute | solution.py:18
  160.3 22.1 %collective-permute-start.10 = (bf16[192,512]{1,0:T(8,128)(2,1)S(1)}, bf16[192,512]{1,0:T(8,128)(2,1)S(1)}, u32[]{:S(2)}, u32[]{:S(2)}) collective-permute-start(bf16[192,512]{1,0:T(8,128)(2,1)S(1)} %maximum_select_fusion.7), channel_id=1, source_target_pairs={{0,3},{3,0},{1,2},{2,1},{4,7},{7,4},{5,6},{6,5},{8,11},{11,8},{9,1... | collective-permute-start | bytes 589832 | tf_op jit(solution)/shard_map/ppermute | solution.py:18
  163.9 35.4 %collective-permute-start.25 = (bf16[192,1024]{1,0:T(8,128)(2,1)S(1)}, bf16[192,1024]{1,0:T(8,128)(2,1)S(1)}, u32[]{:S(2)}, u32[]{:S(2)}) collective-permute-start(bf16[192,1024]{1,0:T(8,128)(2,1)S(1)} %maximum_select_fusion.5), channel_id=1, source_target_pairs={{0,3},{3,0},{1,2},{2,1},{4,7},{7,4},{5,6},{6,5},{8,11},{11,8},{9,1... | collective-permute-start | bytes 1179656 | tf_op jit(solution)/shard_map/ppermute | solution.py:18
  183.4 32.3 %collective-permute-start.11 = (bf16[384,1792]{1,0:T(8,128)(2,1)S(1)}, bf16[384,1792]{1,0:T(8,128)(2,1)S(1)}, u32[]{:S(2)}, u32[]{:S(2)}) collective-permute-start(bf16[384,1792]{1,0:T(8,128)(2,1)S(1)} %convolution_convert_fusion.3), channel_id=1, source_target_pairs={{0,4},{4,0},{1,5},{5,1},{2,6},{6,2},{3,7},{7,3},{8,12},{12,8},{9,1... | collective-permute-start | bytes 4128776 | tf_op jit(solution)/shard_map/ppermute | solution.py:14
  183.7 15.6 %collective-permute-start.4 = (bf16[96,512]{1,0:T(8,128)(2,1)S(1)}, bf16[96,512]{1,0:T(8,128)(2,1)S(1)}, u32[]{:S(2)}, u32[]{:S(2)}) collective-permute-start(bf16[96,512]{1,0:T(8,128)(2,1)S(1)} %get-tuple-element.16), channel_id=1, source_target_pairs={{0,3},{3,0},{1,2},{2,1},{4,7},{7,4},{5,6},{6,5},{8,11},{11,8},{9,1... | collective-permute-start | bytes 294920 | tf_op jit(solution)/shard_map/ppermute | solution.py:18
  183.8 18.8 %collective-permute-start.19 = (bf16[96,1024]{1,0:T(8,128)(2,1)S(1)}, bf16[96,1024]{1,0:T(8,128)(2,1)S(1)}, u32[]{:S(2)}, u32[]{:S(2)}) collective-permute-start(bf16[96,1024]{1,0:T(8,128)(2,1)S(1)} %pad_maximum_fusion.7), channel_id=1, source_target_pairs={{0,3},{3,0},{1,2},{2,1},{4,7},{7,4},{5,6},{6,5},{8,11},{11,8},{9,1... | collective-permute-start | bytes 589832 | tf_op jit(solution)/shard_map/ppermute | solution.py:18
  199.3 16.3 %collective-permute-start.5 = (bf16[192,512]{1,0:T(8,128)(2,1)S(1)}, bf16[192,512]{1,0:T(8,128)(2,1)S(1)}, u32[]{:S(2)}, u32[]{:S(2)}) collective-permute-start(bf16[192,512]{1,0:T(8,128)(2,1)S(1)} %maximum_select_fusion.6), channel_id=1, source_target_pairs={{0,1},{1,0},{2,3},{3,2},{4,5},{5,4},{6,7},{7,6},{8,9},{9,8},{10,11... | collective-permute-start | bytes 589832 | tf_op jit(solution)/shard_map/ppermute | solution.py:18
  202.6 25.5 %collective-permute-start.26 = (bf16[384,1792]{1,0:T(8,128)(2,1)}, bf16[384,1792]{1,0:T(8,128)(2,1)}, u32[]{:S(2)}, u32[]{:S(2)}) collective-permute-start(bf16[384,1792]{1,0:T(8,128)(2,1)} %fusion.4), channel_id=1, source_target_pairs={{0,4},{4,0},{1,5},{5,1},{2,6},{6,2},{3,7},{7,3},{8,12},{12,8},{9,1... | collective-permute-start | bytes 4128776 | tf_op jit(solution)/shard_map/ppermute | solution.py:14
  203.5 20.2 %collective-permute-start.20 = (bf16[192,1024]{1,0:T(8,128)(2,1)}, bf16[192,1024]{1,0:T(8,128)(2,1)}, u32[]{:S(2)}, u32[]{:S(2)}) collective-permute-start(bf16[192,1024]{1,0:T(8,128)(2,1)} %maximum_select_fusion.4), channel_id=1, source_target_pairs={{0,1},{1,0},{2,3},{3,2},{4,5},{5,4},{6,7},{7,6},{8,9},{9,8},{10,11... | collective-permute-start | bytes 1179656 | tf_op jit(solution)/shard_map/ppermute | solution.py:18
  217.7 18.7 %all-to-all-start.1 = ((bf16[16,24,1792]{2,1,0:T(8,128)(2,1)}), bf16[16,24,1792]{2,1,0:T(8,128)(2,1)S(1)}, u32[]{:S(2)}, u32[]{:S(2)}) async-start(bf16[16,24,1792]{2,1,0:T(8,128)(2,1)} %bitcast.131), calls=%async_computation.1 | async-start | bytes 2752512 | tf_op jit(solution)/shard_map/all_to_all | solution.py:142
  236.4 28.7 %all-to-all-start.3 = ((bf16[16,24,1792]{2,1,0:T(8,128)(2,1)}), bf16[16,24,1792]{2,1,0:T(8,128)(2,1)}, u32[]{:S(2)}, u32[]{:S(2)}) async-start(bf16[16,24,1792]{2,1,0:T(8,128)(2,1)} %bitcast.125), calls=%async_computation.3 | async-start | bytes 2752512 | tf_op jit(solution)/shard_map/all_to_all | solution.py:142
  267.3 12.3 %collective-permute-start.27 = (bf16[128,1792]{1,0:T(8,128)(2,1)S(1)}, bf16[128,1792]{1,0:T(8,128)(2,1)S(1)}, u32[]{:S(2)}, u32[]{:S(2)}) collective-permute-start(bf16[128,1792]{1,0:T(8,128)(2,1)S(1)} %slice.179), channel_id=1, source_target_pairs={{0,128},{128,0},{1,129},{129,1},{2,130},{130,2},{3,131},{131,3},{4... | collective-permute-start | bytes 1376264 | tf_op jit(solution)/shard_map/ppermute | solution.py:14
  (30 other events, 315.3 us)

commit v2 on v1

v2 whole, which is shorter than its diff:
```python
import jax
import jax.numpy as jnp
from jax import lax
from jax.experimental import pallas as pl
from jax.experimental.pallas import tpu as pltpu
from jax.sharding import Mesh, PartitionSpec as P

BF = jnp.bfloat16
F32 = jnp.float32
PAIR = [(0, 1), (1, 0)]
EDGE_A = [(0, 1), (1, 0), (2, 3), (3, 2)]
EDGE_B = [(0, 3), (3, 0), (1, 2), (2, 1)]


def swap(value, axis):
    return lax.ppermute(value, axis, PAIR)


FIRST = [(i, j) for i, j in EDGE_A] + [(4 + i, 4 + j) for i, j in EDGE_B]
SECOND = [(i, j) for i, j in EDGE_B] + [(4 + i, 4 + j) for i, j in EDGE_A]


def cross(value, step):
    return lax.ppermute(value, ("core", "tensor"), step)


def tie(value, after):
    return lax.optimization_barrier((value, after))[0]


def dot(a, b, dims):
    return lax.dot_general(a, b, (dims, ((), ())), preferred_element_type=F32)


NN = ((1,), (0,))
NT = ((1,), (1,))
TN = ((0,), (0,))


def local_call(kernel, out_shape, code, *args):
    vmem = pl.BlockSpec(memory_space=pltpu.VMEM)
    return pl.pallas_call(
        kernel,
        in_specs=[pl.BlockSpec(memory_space=pltpu.SMEM)] + [vmem] * len(args),
        out_specs=jax.tree.map(lambda _: vmem, out_shape),
        out_shape=out_shape,
        compiler_params=pltpu.CompilerParams(vmem_limit_bytes=20 * 1024 * 1024),
        cost_estimate=pl.CostEstimate(flops=1000, bytes_accessed=1000, transcendentals=0),
    )(code, *args)


def shuffled(value, bit):
    half = value.shape[0] // 2
    return [(part ^ bit, value[part * half : (part + 1) * half]) for part in range(2)]


def first_kernel(product, count, code, mine, top, bottom, *refs):
    weights, (keep, away, rel) = refs[:count], refs[count:]

    def half_of_rows(step, rows):
        for place, part in shuffled(rows, code[1]):
            rel[step, place] = part
        column = 0
        for weight in weights:
            value = product(rows, weight[...])
            width = value.shape[1]
            for place, part in shuffled(value, code[1]):

                @pl.when(step == 0)
                def _():
                    keep[place, :, column : column + width] = part

                @pl.when(step == 1)
                def _():
                    away[place, :, column : column + width] = part.astype(BF)

            column += width

    @pl.loop(0, 2)
    def _(step):
        other = jnp.concatenate([top[...], bottom[...]], 0)
        half_of_rows(step, jnp.where((step ^ code[0]) == 0, mine[...], other))


def first_products(product, code, mine, other, weights, width):
    rows, quarter = mine.shape
    block = rows // 2
    return local_call(
        lambda *refs: first_kernel(product, len(weights), *refs),
        [
            jax.ShapeDtypeStruct((2, block, width), F32),
            jax.ShapeDtypeStruct((2, block, width), BF),
            jax.ShapeDtypeStruct((2, 2, block, quarter), BF),
        ],
        code,
        mine,
        *other,
        *weights,
    )


def finish(value, theirs, outs):
    half = value.shape[0] // 2
    for j in range(2):
        part = value[j * half : (j + 1) * half]
        if theirs:
            outs[0][j * half : (j + 1) * half, :] = (part + theirs[j][...].astype(F32)).astype(BF)
        else:
            outs[j][...] = part.astype(BF)


def out_rows_kernel(side, code, hidden, w_down, *refs):
    theirs, outs = refs[:2], refs[2:]
    if side == 1:
        theirs, outs = (), refs
    parts = [hidden[2 * (side ^ code[0]) + (j ^ code[1])] for j in range(2)]
    value = dot(jnp.concatenate(parts, 0), w_down[...], NN)
    finish(value, theirs, outs)


def in_rows_kernel(side, code, near, far, w_gate, w_up, *refs):
    theirs, outs = refs[:2], refs[2:]
    if side == 1:
        theirs, outs = (), refs
    place = side ^ code[0]
    value = None
    for kind, weight in ((0, w_gate), (1, w_up)):
        pair = near[2 * place + kind], far[2 * place + kind]
        parts = [jnp.where((j ^ code[1]) == 0, *pair) for j in range(2)]
        term = dot(jnp.concatenate(parts, 0), weight[...], NT)
        value = term if value is None else value + term
    finish(value, theirs, outs)


def last_products(kernel, code, pieces, weights, quarter, theirs):
    side = 1 if theirs is None else 0
    rows = pieces[0].shape[1]
    whole_shape = jax.ShapeDtypeStruct((2 * rows, quarter), BF)
    half_shape = jax.ShapeDtypeStruct((rows, quarter), BF)
    return local_call(
        lambda *refs: kernel(side, *refs),
        [half_shape] * 2 if theirs is None else whole_shape,
        code,
        *pieces,
        *weights,
        *([] if theirs is None else theirs),
    )


def slots_kernel(chips, capacity, planes, z_ref, route_mine, route_peer, local, assign):
    tokens = route_mine.shape[0]
    slots = assign.shape[1]
    lanes = lax.broadcasted_iota(jnp.int32, (tokens, 128), 1)
    earlier = lax.broadcasted_iota(jnp.int32, (tokens, tokens), 0) > lax.broadcasted_iota(
        jnp.int32, (tokens, tokens), 1
    )
    places = lax.broadcasted_iota(jnp.int32, (tokens, slots), 1)
    for block, route in enumerate((route_mine, route_peer)):
        named = [route[:, k : k + 1] for k in range(2)]
        onehot = [(named[k] == lanes).astype(F32) for k in range(2)]
        before = dot(earlier.astype(BF), (onehot[0] + onehot[1]).astype(BF), NN)
        chosen = jnp.zeros((tokens, slots), F32)
        for k in range(2):
            rank = jnp.sum(before * onehot[k], axis=1, keepdims=True).astype(jnp.int32)
            expert = named[k] - z_ref[0] * chips
            inside = (expert >= 0) & (expert < chips)
            slot = jnp.where(inside, expert * (planes * capacity) + block * capacity + rank, -1)
            local[block * tokens : (block + 1) * tokens, k : k + 1] = slot
            chosen = chosen + (slot == places).astype(F32)
        assign[block * tokens : (block + 1) * tokens, :] = chosen.astype(BF)


def rows_kernel(_, assign, mine, peer, out):
    tokens = mine.shape[0]
    rows = dot(assign[:tokens], mine[...], TN) + dot(assign[tokens:], peer[...], TN)
    out[...] = rows.astype(BF)


def picks_of(local, k, first, last, slots):
    places = lax.broadcasted_iota(jnp.int32, (last - first, slots), 1)
    return (local[first:last, k : k + 1] == places).astype(F32).astype(BF)


def cot_rows_kernel(_, local, prob, mine, peer, out):
    tokens = mine.shape[0]
    slots = out.shape[0]
    total = None
    for block, cot in enumerate((mine, peer)):
        first, last = block * tokens, (block + 1) * tokens
        value = cot[...].astype(F32)
        for k in range(2):
            scaled = (prob[first:last, k : k + 1] * value).astype(BF)
            term = dot(picks_of(local, k, first, last, slots), scaled, TN)
            total = term if total is None else total + term
    out[...] = total.astype(BF)


def combine_kernel(_, local, prob, rows, mine, peer, out_mine, out_peer, grad_p):
    tokens = mine.shape[0]
    slots = rows.shape[0]
    for block, (cot, out) in enumerate(((mine, out_mine), (peer, out_peer))):
        first, last = block * tokens, (block + 1) * tokens
        total = None
        for k in range(2):
            picked = dot(picks_of(local, k, first, last, slots), rows[...], NN)
            term = prob[first:last, k : k + 1] * picked
            total = term if total is None else total + term
            grad = jnp.sum(picked * cot[...].astype(F32), axis=1, keepdims=True)
            grad_p[first:last, k : k + 1] = grad
        out[...] = total.astype(out.dtype)


def on_device(tokens, route, probs, cotangent, gate_weight, up_weight, down_weight):
    tok_rows, quarter = tokens.shape
    top_count = route.shape[1]
    planes = lax.axis_size("z")
    chips = lax.axis_size("x") * lax.axis_size("y")
    experts = planes * chips
    capacity = 3 * tok_rows * top_count // (2 * experts)
    slots = chips * planes * capacity
    z_index = lax.axis_index("z")
    t_index = lax.axis_index("tensor")
    bit_b = t_index // 2
    bit_a = (t_index + 1) // 2 % 2
    core = lax.axis_index("core")
    code = jnp.stack(
        [jnp.where(core == 0, bit_a, bit_b), jnp.where(core == 0, bit_b, bit_a)]
    ).astype(jnp.int32)
    w_gate, w_up, w_down = gate_weight[0], up_weight[0], down_weight[0]

    route_peer, probs_peer = swap(route, "z"), swap(probs, "z")
    tok_peer = swap(tokens, "z")
    cot_peer = swap(tie(cotangent, tok_peer), "z")
    prob = jnp.concatenate([probs, probs_peer], 0)
    local, assign = local_call(
        lambda *refs: slots_kernel(chips, capacity, planes, *refs),
        [
            jax.ShapeDtypeStruct((planes * tok_rows, top_count), jnp.int32),
            jax.ShapeDtypeStruct((planes * tok_rows, slots), BF),
        ],
        z_index.astype(jnp.int32)[None],
        route,
        route_peer,
    )
    rows_shape = jax.ShapeDtypeStruct((slots, quarter), BF)

    def exchange(rows):
        return lax.all_to_all(
            rows.reshape(chips, planes * capacity, quarter),
            ("x", "y"),
            split_axis=0,
            concat_axis=0,
            tiled=True,
        ).reshape(slots, quarter)

    def collect(sent):
        return sent, [swap(sent[: slots // 2], "core"), swap(sent[slots // 2 :], "core")]

    tok_sent = exchange(local_call(rows_kernel, rows_shape, code, assign, tokens, tok_peer))
    cot_rows = local_call(cot_rows_kernel, rows_shape, code, local, prob, cotangent, cot_peer)
    cot_sent = exchange(tie(cot_rows, tok_sent))
    in_mine, in_other = collect(tie(tok_sent, cot_rows))
    half = w_gate.shape[1]

    def nn(rows, weight):
        return dot(rows, weight, NN)

    def nt(rows, weight):
        return dot(rows, weight, NT)

    keep, away, rows_in = first_products(nn, code, in_mine, in_other, (w_gate, w_up), 2 * half)
    got = cross(away, FIRST)
    cot_mine, cot_other = collect(tie(cot_sent, away))
    keep_c, away_c, rows_cot = first_products(nt, code, cot_mine, cot_other, (w_down,), half)
    got_c = cross(away_c, FIRST)
    gate_up = keep + tie(got, away_c).astype(F32)
    got = cross(gate_up[1].astype(BF), SECOND)

    gate_up = gate_up[0] + got.astype(F32)
    gate, up = gate_up[:, :half], gate_up[:, half:]
    hidden = (jax.nn.silu(gate) * up).astype(BF)

    hidden_cot = keep_c + got_c.astype(F32)
    got = cross(jnp.stack([hidden_cot[1].astype(BF), hidden]), SECOND)
    hidden_cot = hidden_cot[0] + got[0].astype(F32)
    hidden = jnp.stack([hidden, got[1]])
    sig = jax.nn.sigmoid(gate)
    gate_cot = (hidden_cot * up * sig * (1.0 + gate * (1.0 - sig))).astype(BF)
    up_cot = (hidden_cot * gate * sig).astype(BF)

    own = jnp.stack([gate_cot, up_cot])
    hidden = jnp.concatenate([hidden, cross(hidden, FIRST)], 0)
    got = cross(own, FIRST)

    def send_back(kernel, pieces, weights, after=None):
        away = last_products(kernel, code, pieces, weights, quarter, None)
        theirs = [swap(part, "core") for part in away]
        if after is not None:
            theirs = tie(theirs, after)
        return last_products(kernel, code, pieces, weights, quarter, theirs)

    out_back = send_back(out_rows_kernel, (hidden,), (w_down,))
    returned = exchange(out_back)
    near = jnp.concatenate([own, got], 0)
    far = cross(near, SECOND)
    hidden, rows_cot = tie((hidden, rows_cot), out_back)
    grad_down = dot(hidden.reshape(2 * slots, half), rows_cot.reshape(2 * slots, quarter), TN).astype(BF)
    out_mine, out_peer, grad_p = local_call(
        combine_kernel,
        [
            jax.ShapeDtypeStruct((tok_rows, quarter), F32),
            jax.ShapeDtypeStruct((tok_rows, quarter), BF),
            jax.ShapeDtypeStruct((planes * tok_rows, top_count), F32),
        ],
        code,
        local,
        prob,
        returned,
        cotangent,
        cot_peer,
    )
    in_back = send_back(in_rows_kernel, (near, far), (w_gate, w_up), (out_peer, grad_down))
    returned_in = exchange(in_back)
    near, far, out_mine, grad_p = tie((near, far, out_mine, grad_p), in_back)

    moe_out = (out_mine + swap(out_peer, "z").astype(F32)).astype(BF)
    grad_p = grad_p.T
    grad_p = grad_p[:, :tok_rows] + swap(grad_p[:, tok_rows:], "z")
    grad_p = grad_p + cross(grad_p, FIRST)
    grad_p = grad_p + cross(grad_p, SECOND)

    tok_part = dot(assign, returned_in, NN)
    grad_tokens = (tok_part[:tok_rows] + swap(tok_part[tok_rows:].astype(BF), "z").astype(F32)).astype(BF)

    rows_in = rows_in.reshape(2 * slots, quarter)

    def all_rows(kind):
        parts = [near[kind], far[kind], near[2 + kind], far[2 + kind]]
        return jnp.concatenate(parts, 0)

    grad_gate = dot(rows_in, all_rows(0), TN).astype(BF)
    grad_up = dot(rows_in, all_rows(1), TN).astype(BF)
    return (moe_out, grad_p.T, grad_tokens, grad_gate[None], grad_up[None], grad_down[None])


def solution(mesh):
    lanes = ("z", "x", "y", "core")
    fine = Mesh(mesh.devices.reshape(2, 4, 4, 2, 4), lanes + ("tensor",))
    placed = (
        P(lanes, "tensor"),
        P(lanes, None),
        P(lanes, None),
        P(lanes, "tensor"),
        P(lanes, "tensor", None),
        P(lanes, "tensor", None),
        P(lanes, None, "tensor"),
    )
    return jax.shard_map(
        on_device,
        mesh=fine,
        in_specs=placed,
        out_specs=(
            P(lanes, "tensor"),
            P(lanes, None),
            P(lanes, "tensor"),
            P(lanes, "tensor", None),
            P(lanes, "tensor", None),
            P(lanes, None, "tensor"),
        ),
        check_vma=False,
    )
```

time: 282 us -> 241 us (0.85)
  waiting for transfers between devices: 146 us -> 98.1 us
  matrix products: 46.5 us -> 10.7 us
  Pallas kernels: 0 us -> 26.8 us
  local copies, waits for them, and re-layouts: 6.07 us -> 17.7 us
  starting transfers between devices: 69.7 us -> 80.5 us
  other arithmetic: 10.8 us -> 4.97 us
    ppermute x18 -> x9, waiting for transfers between devices: 88.4 us -> 45.5 us  [cross(): return lax.ppermute(value, ('core', 'tensor'), step)]
    dot_general x21 -> x4, matrix products: 46.5 us -> 10.7 us  [dot(): return lax.dot_general(a, b, (dims, ((), ())), preferred_element_type=F32)]
    all_to_all x4, starting transfers between devices: 19.9 us -> 46.7 us  [exchange(): lax.all_to_all(rows.reshape(chips, planes * capacity, quarter), ('x', 'y'...]
    pallas_call x0 -> x10, Pallas kernels: none -> 26.8 us  [local_call(): pl.pallas_call(kernel, in_specs=[pl.BlockSpec(memory_space=pltpu.SMEM)] +...]
    ppermute x18 -> x9, starting transfers between devices: 39.9 us -> 23.2 us  [cross(): return lax.ppermute(value, ('core', 'tensor'), step)]
    unnamed x47 -> x56, local copies, waits for them, and re-layouts: 3.2 us -> 14.6 us
    all_to_all x4, waiting for transfers between devices: 26.7 us -> 20.7 us  [exchange(): lax.all_to_all(rows.reshape(chips, planes * capacity, quarter), ('x', 'y'...]
    select_n x10 -> x0, other arithmetic: 3.39 us -> none  [the longest x8 3.28 us: in_order(): jnp.where(bit == 0, jnp.concatenate([mine, other], 0), jnp.concatenate([o...]
  transfers between devices with their start and end apart: 32 -> 28, of which waited for: 19 -> 20; matrix products, arithmetic and copies ran while one was open for 20% -> 8% of each run, Pallas kernels for 0% -> 10%
where the time goes in v2:
time: 241 us; the launch traced here: 240 us
  waiting for transfers between devices  98.1 us (41%)
  starting transfers between devices  80.5 us (33%)
  Pallas kernels  26.8 us (11%)
  local copies, waits for them, and re-layouts  17.7 us (7%)
  matrix products  10.7 us (4%)
  other arithmetic  4.97 us (2%)
    all_to_all x4, starting transfers between devices, exchange(): lax.all_to_all(rows.reshape(chips, planes * capacity, quarter), ('x', 'y'...  46.7 us
    ppermute x9, waiting for transfers between devices, cross(): return lax.ppermute(value, ('core', 'tensor'), step)  45.5 us
    ppermute x15, waiting for transfers between devices, swap(): return lax.ppermute(value, axis, PAIR)  31.9 us
    pallas_call x10, Pallas kernels, local_call(): pl.pallas_call(kernel, in_specs=[pl.BlockSpec(memory_space=pltpu.SMEM)] +...  26.8 us
    ppermute x9, starting transfers between devices, cross(): return lax.ppermute(value, ('core', 'tensor'), step)  23.2 us
    all_to_all x4, waiting for transfers between devices, exchange(): lax.all_to_all(rows.reshape(chips, planes * capacity, quarter), ('x', 'y'...  20.7 us
    unnamed x56, local copies, waits for them, and re-layouts  14.6 us
    dot_general x4, matrix products, dot(): return lax.dot_general(a, b, (dims, ((), ())), preferred_element_type=F32)  10.7 us
  transfers between devices with their start and end apart: 28, of which 20 were waited for; matrix products, arithmetic and copies ran while one was open for 8% of the time, Pallas kernels for 10%

profile of v2, /device:TPU:32, one launch (start us, length us, event | category | flops | bytes accessed | tf_op | source)
XLA Modules:
  0.0 239.8 jit_solution(13681190932677211505)
XLA Ops:
  3.7 10.9 %collective-permute-done.refs_2_ = s32[128,2]{1,0:T(8,128)S(1)} collective-permute-done((s32[128,2]{1,0:T(8,128)S(1)}, s32[128,2]{1,0:T(8,128)S(1)}, u32[]{:S(2)}, u32[]{:S(2)}) %collective-permute-start) | collective-permute-done | bytes 1056 | tf_op jit(solution)/shard_map/ppermute | solution.py:16
  19.4 7.2 %all-to-all-start = ((bf16[16,24,1792]{2,1,0:T(8,128)(2,1)}), bf16[16,24,1792]{2,1,0:T(8,128)(2,1)S(1)}, u32[]{:S(2)}, u32[]{:S(2)}) async-start(bf16[16,24,1792]{2,1,0:T(8,128)(2,1)} %bitcast.3), calls=%async_computation | async-start | bytes 2752512 | tf_op jit(solution)/shard_map/all_to_all | solution.py:248
  28.7 9.1 %collective-permute-done.1 = f32[128,2]{0,1:T(2,128)S(1)} collective-permute-done((f32[128,2]{0,1:T(2,128)S(1)}, f32[128,2]{0,1:T(2,128)S(1)}, u32[]{:S(2)}, u32[]{:S(2)}) %collective-permute-start.1) | collective-permute-done | bytes 1056 | tf_op jit(solution)/shard_map/ppermute | solution.py:16
  41.4 5.7 %all-to-all-done = bf16[16,24,1792]{2,1,0:T(8,128)(2,1)S(1)} async-done(((bf16[16,24,1792]{2,1,0:T(8,128)(2,1)}), bf16[16,24,1792]{2,1,0:T(8,128)(2,1)S(1)}, u32[]{:S(2)}, u32[]{:S(2)}) %all-to-all-start) | async-done | bytes 1376288 | tf_op jit(solution)/shard_map/all_to_all | solution.py:248
  47.1 4.5 %all-to-all-start.1 = ((bf16[16,24,1792]{2,1,0:T(8,128)(2,1)}), bf16[16,24,1792]{2,1,0:T(8,128)(2,1)}, u32[]{:S(2)}, u32[]{:S(2)}) async-start(bf16[16,24,1792]{2,1,0:T(8,128)(2,1)} %bitcast.81), calls=%async_computation.1 | async-start | bytes 2752512 | tf_op jit(solution)/shard_map/all_to_all | solution.py:248
  54.9 5.2 %shard_map.121 = (f32[2,192,1024]{2,1,0:T(8,128)S(1)}, bf16[2,192,1024]{2,1,0:T(8,128)(2,1)}, bf16[2,2,192,1792]{3,2,1,0:T(8,128)(2,1)S(1)}) custom-call(s32[2]{0:T(128)S(1)} %pad_add_fusion._.refs_0_, bf16[384,1792]{1,0:T(8,128)(2,1)S(1)} %bitcast.80, bf16[192,1792]{1,0:T(8,128)(2,1)S(1)} %collective-permute-done.4.refs_2_, ...), custom_call_target="tpu_custom_call" | custom-call | flops 1000 | bytes 1000 | tf_op jit(solution)/shard_map/pallas_call | solution.py:42
  62.8 3.3 %collective-permute-start.9 = (bf16[2,192,1024]{2,1,0:T(8,128)(2,1)}, bf16[2,192,1024]{2,1,0:T(8,128)(2,1)}, u32[]{:S(2)}, u32[]{:S(2)}) collective-permute-start(bf16[2,192,1024]{2,1,0:T(8,128)(2,1)} %get-tuple-element.39), channel_id=1, source_target_pairs={{0,1},{1,0},{2,3},{3,2},{4,7},{7,4},{5,6},{6,5},{8,9},{9,8},{10,11... | collective-permute-start | bytes 2359304 | tf_op jit(solution)/shard_map/ppermute | solution.py:24
  66.1 3.9 %all-to-all-done.1 = bf16[16,24,1792]{2,1,0:T(8,128)(2,1)} async-done(((bf16[16,24,1792]{2,1,0:T(8,128)(2,1)}), bf16[16,24,1792]{2,1,0:T(8,128)(2,1)}, u32[]{:S(2)}, u32[]{:S(2)}) %all-to-all-start.1) | async-done | bytes 1376288 | tf_op jit(solution)/shard_map/all_to_all | solution.py:248
  74.6 3.5 %shard_map.122 = (f32[2,192,512]{2,1,0:T(8,128)S(1)}, bf16[2,192,512]{2,1,0:T(8,128)(2,1)S(1)}, bf16[2,2,192,1792]{3,2,1,0:T(8,128)(2,1)S(1)}) custom-call(s32[2]{0:T(128)S(1)} %pad_add_fusion._.refs_0_, bf16[384,1792]{1,0:T(8,128)(2,1)} %bitcast.6.refs_1_, bf16[192,1792]{1,0:T(8,128)(2,1)S(1)} %collective-permute-done.6.refs_2_, ...), custom_call_target="tpu_custom_call" | custom-call | flops 1000 | bytes 1000 | tf_op jit(solution)/shard_map/pallas_call | solution.py:42
  78.1 3.3 %collective-permute-start.8 = (bf16[2,192,512]{2,1,0:T(8,128)(2,1)S(1)}, bf16[2,192,512]{2,1,0:T(8,128)(2,1)S(1)}, u32[]{:S(2)}, u32[]{:S(2)}) collective-permute-start(bf16[2,192,512]{2,1,0:T(8,128)(2,1)S(1)} %get-tuple-element.42), channel_id=1, source_target_pairs={{0,1},{1,0},{2,3},{3,2},{4,7},{7,4},{5,6},{6,5},{8,9},{9,8},{10,11... | collective-permute-start | bytes 1179656 | tf_op jit(solution)/shard_map/ppermute | solution.py:24
  86.0 7.5 %collective-permute-start.10 = (bf16[192,1024]{1,0:T(8,128)(2,1)S(1)}, bf16[192,1024]{1,0:T(8,128)(2,1)S(1)}, u32[]{:S(2)}, u32[]{:S(2)}) collective-permute-start(bf16[192,1024]{1,0:T(8,128)(2,1)S(1)} %fusion.18), channel_id=1, source_target_pairs={{0,3},{3,0},{1,2},{2,1},{4,5},{5,4},{6,7},{7,6},{8,11},{11,8},{9,1... | collective-permute-start | bytes 1179656 | tf_op jit(solution)/shard_map/ppermute | solution.py:24
  93.5 3.3 %collective-permute-done.8 = bf16[2,192,512]{2,1,0:T(8,128)(2,1)S(1)} collective-permute-done((bf16[2,192,512]{2,1,0:T(8,128)(2,1)S(1)}, bf16[2,192,512]{2,1,0:T(8,128)(2,1)S(1)}, u32[]{:S(2)}, u32[]{:S(2)}) %collective-permute-start.8) | collective-permute-done | bytes 393248 | tf_op jit(solution)/shard_map/ppermute | solution.py:24
  96.9 9.0 %collective-permute-done.10 = bf16[192,1024]{1,0:T(8,128)(2,1)S(1)} collective-permute-done((bf16[192,1024]{1,0:T(8,128)(2,1)S(1)}, bf16[192,1024]{1,0:T(8,128)(2,1)S(1)}, u32[]{:S(2)}, u32[]{:S(2)}) %collective-permute-start.10) | collective-permute-done | bytes 393248 | tf_op jit(solution)/shard_map/ppermute | solution.py:24
  106.3 11.5 %collective-permute-done.11 = bf16[2,192,512]{2,1,0:T(8,128)(2,1)S(1)} collective-permute-done((bf16[2,192,512]{2,1,0:T(8,128)(2,1)S(1)}, bf16[2,192,512]{2,1,0:T(8,128)(2,1)S(1)}, u32[]{:S(2)}, u32[]{:S(2)}) %collective-permute-start.11) | collective-permute-done | bytes 393248 | tf_op jit(solution)/shard_map/ppermute | solution.py:24
  121.3 10.2 %collective-permute-done.14 = bf16[2,192,512]{2,1,0:T(8,128)(2,1)S(1)} collective-permute-done((bf16[2,192,512]{2,1,0:T(8,128)(2,1)S(1)}, bf16[2,192,512]{2,1,0:T(8,128)(2,1)S(1)}, u32[]{:S(2)}, u32[]{:S(2)}) %collective-permute-start.14) | collective-permute-done | bytes 393248 | tf_op jit(solution)/shard_map/ppermute | solution.py:24
  133.6 4.4 %collective-permute-done.12 = bf16[2,192,512]{2,1,0:T(8,128)(2,1)S(1)} collective-permute-done((bf16[2,192,512]{2,1,0:T(8,128)(2,1)S(1)}, bf16[2,192,512]{2,1,0:T(8,128)(2,1)S(1)}, u32[]{:S(2)}, u32[]{:S(2)}) %collective-permute-start.12) | collective-permute-done | bytes 393248 | tf_op jit(solution)/shard_map/ppermute | solution.py:24
  138.1 3.9 %collective-permute-start.13 = (bf16[4,192,512]{2,1,0:T(8,128)(2,1)S(1)}, bf16[4,192,512]{2,1,0:T(8,128)(2,1)}, u32[]{:S(2)}, u32[]{:S(2)}) collective-permute-start(bf16[4,192,512]{2,1,0:T(8,128)(2,1)S(1)} %pad_maximum_fusion.refs_1_), channel_id=1, source_target_pairs={{0,3},{3,0},{1,2},{2,1},{4,5},{5,4},{6,7},{7,6},{8,11},{11,8},{9,1... | collective-permute-start | bytes 2359304 | tf_op jit(solution)/shard_map/ppermute | solution.py:24
  144.5 26.0 %all-to-all-start.2 = ((bf16[16,24,1792]{2,1,0:T(8,128)(2,1)}), bf16[16,24,1792]{2,1,0:T(8,128)(2,1)}, u32[]{:S(2)}, u32[]{:S(2)}) async-start(bf16[16,24,1792]{2,1,0:T(8,128)(2,1)} %bitcast.82), calls=%async_computation.2 | async-start | bytes 2752512 | tf_op jit(solution)/shard_map/all_to_all | solution.py:248
  172.1 4.0 %shard_map.126 = (bf16[192,1792]{1,0:T(8,128)(2,1)}, bf16[192,1792]{1,0:T(8,128)(2,1)}) custom-call(s32[2]{0:T(128)S(1)} %pad_add_fusion._.refs_0_, bf16[4,192,512]{2,1,0:T(8,128)(2,1)S(1)} %pad_maximum_fusion.refs_1_, bf16[4,192,512]{2,1,0:T(8,128)(2,1)} %collective-permute-done.13.refs_2_, bf16[1792,512]{1,0:T(8,128)(2,1)S(1)} %bitcast.73, ...), custom_call_target="tpu_custom_call" | custom-call | flops 1000 | bytes 1000 | tf_op jit(solution)/shard_map/pallas_call | solution.py:42
  179.5 6.1 %all-to-all-done.2 = bf16[16,24,1792]{2,1,0:T(8,128)(2,1)} async-done(((bf16[16,24,1792]{2,1,0:T(8,128)(2,1)}), bf16[16,24,1792]{2,1,0:T(8,128)(2,1)}, u32[]{:S(2)}, u32[]{:S(2)}) %all-to-all-start.2) | async-done | bytes 1376288 | tf_op jit(solution)/shard_map/all_to_all | solution.py:248
  192.3 3.2 %shard_map.127 = bf16[384,1792]{1,0:T(8,128)(2,1)S(1)} custom-call(s32[2]{0:T(128)S(1)} %pad_add_fusion._.refs_0_, bf16[4,192,512]{2,1,0:T(8,128)(2,1)S(1)} %pad_maximum_fusion.refs_1_, bf16[4,192,512]{2,1,0:T(8,128)(2,1)} %collective-permute-done.13.refs_2_, bf16[1792,512]{1,0:T(8,128)(2,1)S(1)} %bitcast.74, bf16[1792,512]{1,0:T(8,128)(2,1)S(1)} %bitcast.77, ...), custom_call_target="tpu_custom_call" | custom-call | flops 1000 | bytes 1000 | tf_op jit(solution)/shard_map/pallas_call | solution.py:42
  196.6 9.0 %all-to-all-start.3 = ((bf16[16,24,1792]{2,1,0:T(8,128)(2,1)}), bf16[16,24,1792]{2,1,0:T(8,128)(2,1)}, u32[]{:S(2)}, u32[]{:S(2)}) async-start(bf16[16,24,1792]{2,1,0:T(8,128)(2,1)} %bitcast.83), calls=%async_computation.3 | async-start | bytes 2752512 | tf_op jit(solution)/shard_map/all_to_all | solution.py:248
  222.4 5.0 %all-to-all-done.3 = bf16[16,24,1792]{2,1,0:T(8,128)(2,1)} async-done(((bf16[16,24,1792]{2,1,0:T(8,128)(2,1)}), bf16[16,24,1792]{2,1,0:T(8,128)(2,1)}, u32[]{:S(2)}, u32[]{:S(2)}) %all-to-all-start.3) | async-done | bytes 1376288 | tf_op jit(solution)/shard_map/all_to_all | solution.py:248
  233.2 5.7 %collective-permute-done.23 = bf16[128,1792]{1,0:T(8,128)(2,1)S(1)} collective-permute-done((bf16[128,1792]{1,0:T(8,128)(2,1)S(1)}, bf16[128,1792]{1,0:T(8,128)(2,1)S(1)}, u32[]{:S(2)}, u32[]{:S(2)}) %collective-permute-start.23) | collective-permute-done | bytes 458784 | tf_op jit(solution)/shard_map/ppermute | solution.py:16
  (128 shorter events, 73.3 us)
Async XLA Ops:
  0.6 14.5 %collective-permute-start.2 = (bf16[128,1792]{1,0:T(8,128)(2,1)}, bf16[128,1792]{1,0:T(8,128)(2,1)S(1)}, u32[]{:S(2)}, u32[]{:S(2)}) collective-permute-start(bf16[128,1792]{1,0:T(8,128)(2,1)} %mine.4), channel_id=1, source_target_pairs={{0,128},{128,0},{1,129},{129,1},{2,130},{130,2},{3,131},{131,3},{4... | collective-permute-start | bytes 1376264 | tf_op jit(solution)/shard_map/ppermute | solution.py:16
  3.3 11.2 %collective-permute-start = (s32[128,2]{1,0:T(8,128)S(1)}, s32[128,2]{1,0:T(8,128)S(1)}, u32[]{:S(2)}, u32[]{:S(2)}) collective-permute-start(s32[128,2]{1,0:T(8,128)S(1)} %copy.19.refs_1_), channel_id=1, source_target_pairs={{0,128},{128,0},{1,129},{129,1},{2,130},{130,2},{3,131},{131,3},{4... | collective-permute-start | bytes 3080 | tf_op jit(solution)/shard_map/ppermute | solution.py:16
  19.4 27.6 %all-to-all-start = ((bf16[16,24,1792]{2,1,0:T(8,128)(2,1)}), bf16[16,24,1792]{2,1,0:T(8,128)(2,1)S(1)}, u32[]{:S(2)}, u32[]{:S(2)}) async-start(bf16[16,24,1792]{2,1,0:T(8,128)(2,1)} %bitcast.3), calls=%async_computation | async-start | bytes 2752512 | tf_op jit(solution)/shard_map/all_to_all | solution.py:248
  26.6 11.4 %collective-permute-start.3 = (bf16[128,1792]{1,0:T(8,128)(2,1)S(1)}, bf16[128,1792]{1,0:T(8,128)(2,1)S(1)}, u32[]{:S(2)}, u32[]{:S(2)}) collective-permute-start(bf16[128,1792]{1,0:T(8,128)(2,1)S(1)} %copy-done.11), channel_id=1, source_target_pairs={{0,128},{128,0},{1,129},{129,1},{2,130},{130,2},{3,131},{131,3},{4... | collective-permute-start | bytes 1376264 | tf_op jit(solution)/shard_map/ppermute | solution.py:16
  27.0 10.9 %collective-permute-start.1 = (f32[128,2]{0,1:T(2,128)S(1)}, f32[128,2]{0,1:T(2,128)S(1)}, u32[]{:S(2)}, u32[]{:S(2)}) collective-permute-start(f32[128,2]{0,1:T(2,128)S(1)} %copy-done.26), channel_id=1, source_target_pairs={{0,128},{128,0},{1,129},{129,1},{2,130},{130,2},{3,131},{131,3},{4... | collective-permute-start | bytes 3080 | tf_op jit(solution)/shard_map/ppermute | solution.py:16
  47.1 22.9 %all-to-all-start.1 = ((bf16[16,24,1792]{2,1,0:T(8,128)(2,1)}), bf16[16,24,1792]{2,1,0:T(8,128)(2,1)}, u32[]{:S(2)}, u32[]{:S(2)}) async-start(bf16[16,24,1792]{2,1,0:T(8,128)(2,1)} %bitcast.81), calls=%async_computation.1 | async-start | bytes 2752512 | tf_op jit(solution)/shard_map/all_to_all | solution.py:248
  62.8 21.7 %collective-permute-start.9 = (bf16[2,192,1024]{2,1,0:T(8,128)(2,1)}, bf16[2,192,1024]{2,1,0:T(8,128)(2,1)}, u32[]{:S(2)}, u32[]{:S(2)}) collective-permute-start(bf16[2,192,1024]{2,1,0:T(8,128)(2,1)} %get-tuple-element.39), channel_id=1, source_target_pairs={{0,1},{1,0},{2,3},{3,2},{4,7},{7,4},{5,6},{6,5},{8,9},{9,8},{10,11... | collective-permute-start | bytes 2359304 | tf_op jit(solution)/shard_map/ppermute | solution.py:24
  78.1 18.7 %collective-permute-start.8 = (bf16[2,192,512]{2,1,0:T(8,128)(2,1)S(1)}, bf16[2,192,512]{2,1,0:T(8,128)(2,1)S(1)}, u32[]{:S(2)}, u32[]{:S(2)}) collective-permute-start(bf16[2,192,512]{2,1,0:T(8,128)(2,1)S(1)} %get-tuple-element.42), channel_id=1, source_target_pairs={{0,1},{1,0},{2,3},{3,2},{4,7},{7,4},{5,6},{6,5},{8,9},{9,8},{10,11... | collective-permute-start | bytes 1179656 | tf_op jit(solution)/shard_map/ppermute | solution.py:24
  86.0 20.0 %collective-permute-start.10 = (bf16[192,1024]{1,0:T(8,128)(2,1)S(1)}, bf16[192,1024]{1,0:T(8,128)(2,1)S(1)}, u32[]{:S(2)}, u32[]{:S(2)}) collective-permute-start(bf16[192,1024]{1,0:T(8,128)(2,1)S(1)} %fusion.18), channel_id=1, source_target_pairs={{0,3},{3,0},{1,2},{2,1},{4,5},{5,4},{6,7},{7,6},{8,11},{11,8},{9,1... | collective-permute-start | bytes 1179656 | tf_op jit(solution)/shard_map/ppermute | solution.py:24
  106.2 11.6 %collective-permute-start.11 = (bf16[2,192,512]{2,1,0:T(8,128)(2,1)S(1)}, bf16[2,192,512]{2,1,0:T(8,128)(2,1)S(1)}, u32[]{:S(2)}, u32[]{:S(2)}) collective-permute-start(bf16[2,192,512]{2,1,0:T(8,128)(2,1)S(1)} %pad_maximum_fusion.2), channel_id=1, source_target_pairs={{0,3},{3,0},{1,2},{2,1},{4,5},{5,4},{6,7},{7,6},{8,11},{11,8},{9,1... | collective-permute-start | bytes 1179656 | tf_op jit(solution)/shard_map/ppermute | solution.py:24
  117.9 13.5 %collective-permute-start.14 = (bf16[2,192,512]{2,1,0:T(8,128)(2,1)S(1)}, bf16[2,192,512]{2,1,0:T(8,128)(2,1)S(1)}, u32[]{:S(2)}, u32[]{:S(2)}) collective-permute-start(bf16[2,192,512]{2,1,0:T(8,128)(2,1)S(1)} %pad_maximum_fusion.4), channel_id=1, source_target_pairs={{0,1},{1,0},{2,3},{3,2},{4,7},{7,4},{5,6},{6,5},{8,9},{9,8},{10,11... | collective-permute-start | bytes 1179656 | tf_op jit(solution)/shard_map/ppermute | solution.py:24
  119.8 18.3 %collective-permute-start.12 = (bf16[2,192,512]{2,1,0:T(8,128)(2,1)S(1)}, bf16[2,192,512]{2,1,0:T(8,128)(2,1)S(1)}, u32[]{:S(2)}, u32[]{:S(2)}) collective-permute-start(bf16[2,192,512]{2,1,0:T(8,128)(2,1)S(1)} %pad_maximum_fusion.3), channel_id=1, source_target_pairs={{0,1},{1,0},{2,3},{3,2},{4,7},{7,4},{5,6},{6,5},{8,9},{9,8},{10,11... | collective-permute-start | bytes 1179656 | tf_op jit(solution)/shard_map/ppermute | solution.py:24
  132.9 9.0 %collective-permute-start.15 = (bf16[192,1792]{1,0:T(8,128)(2,1)S(1)}, bf16[192,1792]{1,0:T(8,128)(2,1)S(1)}, u32[]{:S(2)}, u32[]{:S(2)}) collective-permute-start(bf16[192,1792]{1,0:T(8,128)(2,1)S(1)} %get-tuple-element.45), channel_id=1, source_target_pairs={{0,4},{4,0},{1,5},{5,1},{2,6},{6,2},{3,7},{7,3},{8,12},{12,8},{9,1... | collective-permute-start | bytes 2064392 | tf_op jit(solution)/shard_map/ppermute | solution.py:16
  133.5 8.5 %collective-permute-start.16 = (bf16[192,1792]{1,0:T(8,128)(2,1)S(1)}, bf16[192,1792]{1,0:T(8,128)(2,1)S(1)}, u32[]{:S(2)}, u32[]{:S(2)}) collective-permute-start(bf16[192,1792]{1,0:T(8,128)(2,1)S(1)} %get-tuple-element.46), channel_id=1, source_target_pairs={{0,4},{4,0},{1,5},{5,1},{2,6},{6,2},{3,7},{7,3},{8,12},{12,8},{9,1... | collective-permute-start | bytes 2064392 | tf_op jit(solution)/shard_map/ppermute | solution.py:16
  138.1 32.5 %collective-permute-start.13 = (bf16[4,192,512]{2,1,0:T(8,128)(2,1)S(1)}, bf16[4,192,512]{2,1,0:T(8,128)(2,1)}, u32[]{:S(2)}, u32[]{:S(2)}) collective-permute-start(bf16[4,192,512]{2,1,0:T(8,128)(2,1)S(1)} %pad_maximum_fusion.refs_1_), channel_id=1, source_target_pairs={{0,3},{3,0},{1,2},{2,1},{4,5},{5,4},{6,7},{7,6},{8,11},{11,8},{9,1... | collective-permute-start | bytes 2359304 | tf_op jit(solution)/shard_map/ppermute | solution.py:24
  144.5 41.1 %all-to-all-start.2 = ((bf16[16,24,1792]{2,1,0:T(8,128)(2,1)}), bf16[16,24,1792]{2,1,0:T(8,128)(2,1)}, u32[]{:S(2)}, u32[]{:S(2)}) async-start(bf16[16,24,1792]{2,1,0:T(8,128)(2,1)} %bitcast.82), calls=%async_computation.2 | async-start | bytes 2752512 | tf_op jit(solution)/shard_map/all_to_all | solution.py:248
  176.1 16.2 %collective-permute-start.17 = (bf16[192,1792]{1,0:T(8,128)(2,1)}, bf16[192,1792]{1,0:T(8,128)(2,1)}, u32[]{:S(2)}, u32[]{:S(2)}) collective-permute-start(bf16[192,1792]{1,0:T(8,128)(2,1)} %get-tuple-element.49), channel_id=1, source_target_pairs={{0,4},{4,0},{1,5},{5,1},{2,6},{6,2},{3,7},{7,3},{8,12},{12,8},{9,1... | collective-permute-start | bytes 2064392 | tf_op jit(solution)/shard_map/ppermute | solution.py:16
  176.1 16.2 %collective-permute-start.18 = (bf16[192,1792]{1,0:T(8,128)(2,1)}, bf16[192,1792]{1,0:T(8,128)(2,1)}, u32[]{:S(2)}, u32[]{:S(2)}) collective-permute-start(bf16[192,1792]{1,0:T(8,128)(2,1)} %get-tuple-element.50), channel_id=1, source_target_pairs={{0,4},{4,0},{1,5},{5,1},{2,6},{6,2},{3,7},{7,3},{8,12},{12,8},{9,1... | collective-permute-start | bytes 2064392 | tf_op jit(solution)/shard_map/ppermute | solution.py:16
  192.3 39.1 %collective-permute-start.19 = (bf16[128,1792]{1,0:T(8,128)(2,1)S(1)}, bf16[128,1792]{1,0:T(8,128)(2,1)}, u32[]{:S(2)}, u32[]{:S(2)}) collective-permute-start(bf16[128,1792]{1,0:T(8,128)(2,1)S(1)} %get-tuple-element.51), channel_id=1, source_target_pairs={{0,128},{128,0},{1,129},{129,1},{2,130},{130,2},{3,131},{131,3},{4... | collective-permute-start | bytes 1376264 | tf_op jit(solution)/shard_map/ppermute | solution.py:16
  196.6 30.8 %all-to-all-start.3 = ((bf16[16,24,1792]{2,1,0:T(8,128)(2,1)}), bf16[16,24,1792]{2,1,0:T(8,128)(2,1)}, u32[]{:S(2)}, u32[]{:S(2)}) async-start(bf16[16,24,1792]{2,1,0:T(8,128)(2,1)} %bitcast.83), calls=%async_computation.3 | async-start | bytes 2752512 | tf_op jit(solution)/shard_map/all_to_all | solution.py:248
  205.7 4.4 %collective-permute-start.20 = (f32[2,128]{0,1:T(8,128)S(1)}, f32[2,128]{0,1:T(8,128)S(1)}, u32[]{:S(2)}, u32[]{:S(2)}) collective-permute-start(f32[2,128]{0,1:T(8,128)S(1)} %slice.108), channel_id=1, source_target_pairs={{0,128},{128,0},{1,129},{129,1},{2,130},{130,2},{3,131},{131,3},{4... | collective-permute-start | bytes 3080 | tf_op jit(solution)/shard_map/ppermute | solution.py:16
  210.0 5.3 %collective-permute-start.21 = (f32[2,128]{0,1:T(8,128)S(1)}, f32[2,128]{0,1:T(8,128)S(1)}, u32[]{:S(2)}, u32[]{:S(2)}) collective-permute-start(f32[2,128]{0,1:T(8,128)S(1)} %slice_add_fusion.2), channel_id=1, source_target_pairs={{0,1},{1,0},{2,3},{3,2},{4,7},{7,4},{5,6},{6,5},{8,9},{9,8},{10,11... | collective-permute-start | bytes 3080 | tf_op jit(solution)/shard_map/ppermute | solution.py:24
  215.3 6.5 %collective-permute-start.22 = (f32[2,128]{0,1:T(8,128)S(1)}, f32[2,128]{0,1:T(8,128)S(1)}, u32[]{:S(2)}, u32[]{:S(2)}) collective-permute-start(f32[2,128]{0,1:T(8,128)S(1)} %add.58), channel_id=1, source_target_pairs={{0,3},{3,0},{1,2},{2,1},{4,5},{5,4},{6,7},{7,6},{8,11},{11,8},{9,1... | collective-permute-start | bytes 3080 | tf_op jit(solution)/shard_map/ppermute | solution.py:24
  229.5 9.4 %collective-permute-start.23 = (bf16[128,1792]{1,0:T(8,128)(2,1)S(1)}, bf16[128,1792]{1,0:T(8,128)(2,1)S(1)}, u32[]{:S(2)}, u32[]{:S(2)}) collective-permute-start(bf16[128,1792]{1,0:T(8,128)(2,1)S(1)} %slice.159), channel_id=1, source_target_pairs={{0,128},{128,0},{1,129},{129,1},{2,130},{130,2},{3,131},{131,3},{4... | collective-permute-start | bytes 1376264 | tf_op jit(solution)/shard_map/ppermute | solution.py:16
  (31 other events, 167.3 us)

commit v3 on v2

--- a/solution.py
+++ b/solution.py
@@ -147,7 +147,7 @@
     )
 
 
-def slots_kernel(chips, capacity, planes, z_ref, route_mine, route_peer, local, assign):
+def slots_kernel(chips, capacity, planes, z_ref, route_mine, route_peer, local, assign, turned):
     tokens = route_mine.shape[0]
     slots = assign.shape[1]
     lanes = lax.broadcasted_iota(jnp.int32, (tokens, 128), 1)
@@ -168,11 +168,12 @@
             local[block * tokens : (block + 1) * tokens, k : k + 1] = slot
             chosen = chosen + (slot == places).astype(F32)
         assign[block * tokens : (block + 1) * tokens, :] = chosen.astype(BF)
-
-
-def rows_kernel(_, assign, mine, peer, out):
+        turned[:, block * tokens : (block + 1) * tokens] = chosen.T.astype(BF)
+
+
+def rows_kernel(_, turned, mine, peer, out):
     tokens = mine.shape[0]
-    rows = dot(assign[:tokens], mine[...], TN) + dot(assign[tokens:], peer[...], TN)
+    rows = dot(turned[:, :tokens], mine[...], NN) + dot(turned[:, tokens:], peer[...], NN)
     out[...] = rows.astype(BF)
 
 
@@ -232,11 +233,12 @@
     tok_peer = swap(tokens, "z")
     cot_peer = swap(tie(cotangent, tok_peer), "z")
     prob = jnp.concatenate([probs, probs_peer], 0)
-    local, assign = local_call(
+    local, assign, turned = local_call(
         lambda *refs: slots_kernel(chips, capacity, planes, *refs),
         [
             jax.ShapeDtypeStruct((planes * tok_rows, top_count), jnp.int32),
             jax.ShapeDtypeStruct((planes * tok_rows, slots), BF),
+            jax.ShapeDtypeStruct((slots, planes * tok_rows), BF),
         ],
         z_index.astype(jnp.int32)[None],
         route,
@@ -256,7 +258,7 @@
     def collect(sent):
         return sent, [swap(sent[: slots // 2], "core"), swap(sent[slots // 2 :], "core")]
 
-    tok_sent = exchange(local_call(rows_kernel, rows_shape, code, assign, tokens, tok_peer))
+    tok_sent = exchange(local_call(rows_kernel, rows_shape, code, turned, tokens, tok_peer))
     cot_rows = local_call(cot_rows_kernel, rows_shape, code, local, prob, cotangent, cot_peer)
     cot_sent = exchange(tie(cot_rows, tok_sent))
     in_mine, in_other = collect(tie(tok_sent, cot_rows))
@@ -281,15 +283,16 @@
     hidden = (jax.nn.silu(gate) * up).astype(BF)
 
     hidden_cot = keep_c + got_c.astype(F32)
-    got = cross(jnp.stack([hidden_cot[1].astype(BF), hidden]), SECOND)
-    hidden_cot = hidden_cot[0] + got[0].astype(F32)
-    hidden = jnp.stack([hidden, got[1]])
+    hidden = jnp.stack([hidden, cross(hidden, FIRST)])
+    got = cross(hidden_cot[1].astype(BF), SECOND)
+    hidden_cot = hidden_cot[0] + got.astype(F32)
     sig = jax.nn.sigmoid(gate)
     gate_cot = (hidden_cot * up * sig * (1.0 + gate * (1.0 - sig))).astype(BF)
     up_cot = (hidden_cot * gate * sig).astype(BF)
 
     own = jnp.stack([gate_cot, up_cot])
-    hidden = jnp.concatenate([hidden, cross(hidden, FIRST)], 0)
+    got = cross(hidden, SECOND)
+    hidden = jnp.stack([hidden[0], got[0], hidden[1], got[1]])
     got = cross(own, FIRST)
 
     def send_back(kernel, pieces, weights, after=None):
@@ -319,7 +322,7 @@
         cotangent,
         cot_peer,
     )
-    in_back = send_back(in_rows_kernel, (near, far), (w_gate, w_up), (out_peer, grad_down))
+    in_back = send_back(in_rows_kernel, (near, far), (w_gate, w_up), grad_down)
     returned_in = exchange(in_back)
     near, far, out_mine, grad_p = tie((near, far, out_mine, grad_p), in_back)
 

time: 241 us -> 224 us (0.929)
  starting transfers between devices: 80.5 us -> 62.1 us
  waiting for transfers between devices: 98.1 us -> 104 us
  local copies, waits for them, and re-layouts: 17.7 us -> 13.8 us
    all_to_all x4, starting transfers between devices: 46.7 us -> 28.4 us  [exchange(): lax.all_to_all(rows.reshape(chips, planes * capacity, quarter), ('x', 'y'...]
    all_to_all x4, waiting for transfers between devices: 20.7 us -> 9.61 us  [exchange(): lax.all_to_all(rows.reshape(chips, planes * capacity, quarter), ('x', 'y'...]
    ppermute x9 -> x10, waiting for transfers between devices: 45.5 us -> 55.8 us  [cross(): return lax.ppermute(value, ('core', 'tensor'), step)]
    ppermute x15, waiting for transfers between devices: 31.9 us -> 38.9 us  [swap(): return lax.ppermute(value, axis, PAIR)]
    unnamed x56 -> x50, local copies, waits for them, and re-layouts: 14.6 us -> 10.7 us
    ppermute x9 -> x10, starting transfers between devices: 23.2 us -> 24.8 us  [cross(): return lax.ppermute(value, ('core', 'tensor'), step)]
  transfers between devices with their start and end apart: 28 -> 29, of which waited for: 20 -> 21; matrix products, arithmetic and copies ran while one was open for 8% -> 8% of each run, Pallas kernels for 10% -> 10%
where the time goes in v3:
time: 224 us; the launch traced here: 221 us
  waiting for transfers between devices  104 us (46%)
  starting transfers between devices  62.1 us (28%)
  Pallas kernels  25.3 us (11%)
  local copies, waits for them, and re-layouts  13.8 us (6%)
  matrix products  10.5 us (5%)
  other arithmetic  3.85 us (2%)
    ppermute x10, waiting for transfers between devices, cross(): return lax.ppermute(value, ('core', 'tensor'), step)  55.8 us
    ppermute x15, waiting for transfers between devices, swap(): return lax.ppermute(value, axis, PAIR)  38.9 us
    all_to_all x4, starting transfers between devices, exchange(): lax.all_to_all(rows.reshape(chips, planes * capacity, quarter), ('x', 'y'...  28.4 us
    pallas_call x10, Pallas kernels, local_call(): pl.pallas_call(kernel, in_specs=[pl.BlockSpec(memory_space=pltpu.SMEM)] +...  25.3 us
    ppermute x10, starting transfers between devices, cross(): return lax.ppermute(value, ('core', 'tensor'), step)  24.8 us
    unnamed x50, local copies, waits for them, and re-layouts  10.7 us
    dot_general x4, matrix products, dot(): return lax.dot_general(a, b, (dims, ((), ())), preferred_element_type=F32)  10.5 us
    all_to_all x4, waiting for transfers between devices, exchange(): lax.all_to_all(rows.reshape(chips, planes * capacity, quarter), ('x', 'y'...  9.61 us
  transfers between devices with their start and end apart: 29, of which 21 were waited for; matrix products, arithmetic and copies ran while one was open for 8% of the time, Pallas kernels for 10%

profile of v3, /device:TPU:32, one launch (start us, length us, event | category | flops | bytes accessed | tf_op | source)
XLA Modules:
  0.0 220.9 jit_solution(9082381567901273257)
XLA Ops:
  3.7 10.9 %collective-permute-done.refs_2_ = s32[128,2]{1,0:T(8,128)S(1)} collective-permute-done((s32[128,2]{1,0:T(8,128)S(1)}, s32[128,2]{1,0:T(8,128)S(1)}, u32[]{:S(2)}, u32[]{:S(2)}) %collective-permute-start) | collective-permute-done | bytes 1056 | tf_op jit(solution)/shard_map/ppermute | solution.py:16
  19.5 7.2 %all-to-all-start = ((bf16[16,24,1792]{2,1,0:T(8,128)(2,1)}), bf16[16,24,1792]{2,1,0:T(8,128)(2,1)S(1)}, u32[]{:S(2)}, u32[]{:S(2)}) async-start(bf16[16,24,1792]{2,1,0:T(8,128)(2,1)} %bitcast.3), calls=%async_computation | async-start | bytes 2752512 | tf_op jit(solution)/shard_map/all_to_all | solution.py:250
  28.8 9.1 %collective-permute-done.1 = f32[128,2]{0,1:T(2,128)S(1)} collective-permute-done((f32[128,2]{0,1:T(2,128)S(1)}, f32[128,2]{0,1:T(2,128)S(1)}, u32[]{:S(2)}, u32[]{:S(2)}) %collective-permute-start.1) | collective-permute-done | bytes 1056 | tf_op jit(solution)/shard_map/ppermute | solution.py:16
  41.4 5.7 %all-to-all-done = bf16[16,24,1792]{2,1,0:T(8,128)(2,1)S(1)} async-done(((bf16[16,24,1792]{2,1,0:T(8,128)(2,1)}), bf16[16,24,1792]{2,1,0:T(8,128)(2,1)S(1)}, u32[]{:S(2)}, u32[]{:S(2)}) %all-to-all-start) | async-done | bytes 1376288 | tf_op jit(solution)/shard_map/all_to_all | solution.py:250
  47.1 4.5 %all-to-all-start.1 = ((bf16[16,24,1792]{2,1,0:T(8,128)(2,1)}), bf16[16,24,1792]{2,1,0:T(8,128)(2,1)}, u32[]{:S(2)}, u32[]{:S(2)}) async-start(bf16[16,24,1792]{2,1,0:T(8,128)(2,1)} %bitcast.85), calls=%async_computation.1 | async-start | bytes 2752512 | tf_op jit(solution)/shard_map/all_to_all | solution.py:250
  55.0 5.2 %shard_map.121 = (f32[2,192,1024]{2,1,0:T(8,128)S(1)}, bf16[2,192,1024]{2,1,0:T(8,128)(2,1)}, bf16[2,2,192,1792]{3,2,1,0:T(8,128)(2,1)S(1)}) custom-call(s32[2]{0:T(128)S(1)} %pad_add_fusion._.refs_0_, bf16[384,1792]{1,0:T(8,128)(2,1)S(1)} %bitcast.84, bf16[192,1792]{1,0:T(8,128)(2,1)S(1)} %collective-permute-done.4.refs_2_, ...), custom_call_target="tpu_custom_call" | custom-call | flops 1000 | bytes 1000 | tf_op jit(solution)/shard_map/pallas_call | solution.py:42
  62.8 3.3 %collective-permute-start.10 = (bf16[2,192,1024]{2,1,0:T(8,128)(2,1)}, bf16[2,192,1024]{2,1,0:T(8,128)(2,1)}, u32[]{:S(2)}, u32[]{:S(2)}) collective-permute-start(bf16[2,192,1024]{2,1,0:T(8,128)(2,1)} %get-tuple-element.40), channel_id=1, source_target_pairs={{0,1},{1,0},{2,3},{3,2},{4,7},{7,4},{5,6},{6,5},{8,9},{9,8},{10,11... | collective-permute-start | bytes 2359304 | tf_op jit(solution)/shard_map/ppermute | solution.py:24
  66.1 3.9 %all-to-all-done.1 = bf16[16,24,1792]{2,1,0:T(8,128)(2,1)} async-done(((bf16[16,24,1792]{2,1,0:T(8,128)(2,1)}), bf16[16,24,1792]{2,1,0:T(8,128)(2,1)}, u32[]{:S(2)}, u32[]{:S(2)}) %all-to-all-start.1) | async-done | bytes 1376288 | tf_op jit(solution)/shard_map/all_to_all | solution.py:250
  74.7 3.4 %shard_map.122 = (f32[2,192,512]{2,1,0:T(8,128)S(1)}, bf16[2,192,512]{2,1,0:T(8,128)(2,1)S(1)}, bf16[2,2,192,1792]{3,2,1,0:T(8,128)(2,1)S(1)}) custom-call(s32[2]{0:T(128)S(1)} %pad_add_fusion._.refs_0_, bf16[384,1792]{1,0:T(8,128)(2,1)} %bitcast.6.refs_1_, bf16[192,1792]{1,0:T(8,128)(2,1)S(1)} %collective-permute-done.6.refs_2_, ...), custom_call_target="tpu_custom_call" | custom-call | flops 1000 | bytes 1000 | tf_op jit(solution)/shard_map/pallas_call | solution.py:42
  78.1 3.4 %collective-permute-start.8 = (bf16[2,192,512]{2,1,0:T(8,128)(2,1)S(1)}, bf16[2,192,512]{2,1,0:T(8,128)(2,1)S(1)}, u32[]{:S(2)}, u32[]{:S(2)}) collective-permute-start(bf16[2,192,512]{2,1,0:T(8,128)(2,1)S(1)} %get-tuple-element.43), channel_id=1, source_target_pairs={{0,1},{1,0},{2,3},{3,2},{4,7},{7,4},{5,6},{6,5},{8,9},{9,8},{10,11... | collective-permute-start | bytes 1179656 | tf_op jit(solution)/shard_map/ppermute | solution.py:24
  81.5 3.1 %collective-permute-done.10 = bf16[2,192,1024]{2,1,0:T(8,128)(2,1)} collective-permute-done((bf16[2,192,1024]{2,1,0:T(8,128)(2,1)}, bf16[2,192,1024]{2,1,0:T(8,128)(2,1)}, u32[]{:S(2)}, u32[]{:S(2)}) %collective-permute-start.10) | collective-permute-done | bytes 786464 | tf_op jit(solution)/shard_map/ppermute | solution.py:24
  86.0 7.5 %collective-permute-start.11 = (bf16[192,1024]{1,0:T(8,128)(2,1)S(1)}, bf16[192,1024]{1,0:T(8,128)(2,1)S(1)}, u32[]{:S(2)}, u32[]{:S(2)}) collective-permute-start(bf16[192,1024]{1,0:T(8,128)(2,1)S(1)} %fusion.18), channel_id=1, source_target_pairs={{0,3},{3,0},{1,2},{2,1},{4,5},{5,4},{6,7},{7,6},{8,11},{11,8},{9,1... | collective-permute-start | bytes 1179656 | tf_op jit(solution)/shard_map/ppermute | solution.py:24
  93.5 3.3 %collective-permute-done.8 = bf16[2,192,512]{2,1,0:T(8,128)(2,1)S(1)} collective-permute-done((bf16[2,192,512]{2,1,0:T(8,128)(2,1)S(1)}, bf16[2,192,512]{2,1,0:T(8,128)(2,1)S(1)}, u32[]{:S(2)}, u32[]{:S(2)}) %collective-permute-start.8) | collective-permute-done | bytes 393248 | tf_op jit(solution)/shard_map/ppermute | solution.py:24
  97.0 9.8 %collective-permute-done.11 = bf16[192,1024]{1,0:T(8,128)(2,1)S(1)} collective-permute-done((bf16[192,1024]{1,0:T(8,128)(2,1)S(1)}, bf16[192,1024]{1,0:T(8,128)(2,1)S(1)}, u32[]{:S(2)}, u32[]{:S(2)}) %collective-permute-start.11) | collective-permute-done | bytes 393248 | tf_op jit(solution)/shard_map/ppermute | solution.py:24
  109.6 6.3 %collective-permute-done.14 = bf16[192,512]{1,0:T(8,128)(2,1)S(1)} collective-permute-done((bf16[192,512]{1,0:T(8,128)(2,1)S(1)}, bf16[192,512]{1,0:T(8,128)(2,1)S(1)}, u32[]{:S(2)}, u32[]{:S(2)}) %collective-permute-start.14) | collective-permute-done | bytes 196640 | tf_op jit(solution)/shard_map/ppermute | solution.py:24
  116.0 3.9 %collective-permute-start.15 = (bf16[2,192,512]{2,1,0:T(8,128)(2,1)S(1)}, bf16[2,192,512]{2,1,0:T(8,128)(2,1)S(1)}, u32[]{:S(2)}, u32[]{:S(2)}) collective-permute-start(bf16[2,192,512]{2,1,0:T(8,128)(2,1)S(1)} %pad_maximum_fusion.3), channel_id=1, source_target_pairs={{0,3},{3,0},{1,2},{2,1},{4,5},{5,4},{6,7},{7,6},{8,11},{11,8},{9,1... | collective-permute-start | bytes 1179656 | tf_op jit(solution)/shard_map/ppermute | solution.py:24
  119.9 3.5 %collective-permute-start.12 = (bf16[2,192,512]{2,1,0:T(8,128)(2,1)S(1)}, bf16[2,192,512]{2,1,0:T(8,128)(2,1)S(1)}, u32[]{:S(2)}, u32[]{:S(2)}) collective-permute-start(bf16[2,192,512]{2,1,0:T(8,128)(2,1)S(1)} %pad_maximum_fusion.2), channel_id=1, source_target_pairs={{0,1},{1,0},{2,3},{3,2},{4,7},{7,4},{5,6},{6,5},{8,9},{9,8},{10,11... | collective-permute-start | bytes 1179656 | tf_op jit(solution)/shard_map/ppermute | solution.py:24
  123.4 12.9 %collective-permute-done.15 = bf16[2,192,512]{2,1,0:T(8,128)(2,1)S(1)} collective-permute-done((bf16[2,192,512]{2,1,0:T(8,128)(2,1)S(1)}, bf16[2,192,512]{2,1,0:T(8,128)(2,1)S(1)}, u32[]{:S(2)}, u32[]{:S(2)}) %collective-permute-start.15) | collective-permute-done | bytes 393248 | tf_op jit(solution)/shard_map/ppermute | solution.py:24
  143.6 8.9 %all-to-all-start.2 = ((bf16[16,24,1792]{2,1,0:T(8,128)(2,1)}), bf16[16,24,1792]{2,1,0:T(8,128)(2,1)}, u32[]{:S(2)}, u32[]{:S(2)}) async-start(bf16[16,24,1792]{2,1,0:T(8,128)(2,1)} %bitcast.86), calls=%async_computation.2 | async-start | bytes 2752512 | tf_op jit(solution)/shard_map/all_to_all | solution.py:250
  152.5 8.7 %collective-permute-done.13.refs_2_ = bf16[4,192,512]{2,1,0:T(8,128)(2,1)} collective-permute-done((bf16[4,192,512]{2,1,0:T(8,128)(2,1)S(1)}, bf16[4,192,512]{2,1,0:T(8,128)(2,1)}, u32[]{:S(2)}, u32[]{:S(2)}) %collective-permute-start.13) | collective-permute-done | bytes 786464 | tf_op jit(solution)/shard_map/ppermute | solution.py:24
  162.7 2.9 %shard_map.126 = (bf16[192,1792]{1,0:T(8,128)(2,1)S(1)}, bf16[192,1792]{1,0:T(8,128)(2,1)S(1)}) custom-call(s32[2]{0:T(128)S(1)} %pad_add_fusion._.refs_0_, bf16[4,192,512]{2,1,0:T(8,128)(2,1)S(1)} %pad_maximum_fusion.refs_1_, bf16[4,192,512]{2,1,0:T(8,128)(2,1)} %collective-permute-done.13.refs_2_, bf16[1792,512]{1,0:T(8,128)(2,1)S(1)} %bitcast.77, ...), custom_call_target="tpu_custom_call" | custom-call | flops 1000 | bytes 1000 | tf_op jit(solution)/shard_map/pallas_call | solution.py:42
  173.1 7.8 %all-to-all-start.3 = ((bf16[16,24,1792]{2,1,0:T(8,128)(2,1)}), bf16[16,24,1792]{2,1,0:T(8,128)(2,1)}, u32[]{:S(2)}, u32[]{:S(2)}) async-start(bf16[16,24,1792]{2,1,0:T(8,128)(2,1)} %bitcast.87), calls=%async_computation.3 | async-start | bytes 2752512 | tf_op jit(solution)/shard_map/all_to_all | solution.py:250
  192.1 7.6 %collective-permute-done.22 = f32[2,128]{0,1:T(8,128)S(1)} collective-permute-done((f32[2,128]{0,1:T(8,128)S(1)}, f32[2,128]{0,1:T(8,128)S(1)}, u32[]{:S(2)}, u32[]{:S(2)}) %collective-permute-start.22) | collective-permute-done | bytes 1056 | tf_op jit(solution)/shard_map/ppermute | solution.py:24
  209.8 10.3 %collective-permute-done.24 = bf16[128,1792]{1,0:T(8,128)(2,1)S(1)} collective-permute-done((bf16[128,1792]{1,0:T(8,128)(2,1)S(1)}, bf16[128,1792]{1,0:T(8,128)(2,1)S(1)}, u32[]{:S(2)}, u32[]{:S(2)}) %collective-permute-start.24) | collective-permute-done | bytes 458784 | tf_op jit(solution)/shard_map/ppermute | solution.py:16
  (122 shorter events, 66.8 us)
Async XLA Ops:
  0.6 15.3 %collective-permute-start.2 = (bf16[128,1792]{1,0:T(8,128)(2,1)}, bf16[128,1792]{1,0:T(8,128)(2,1)S(1)}, u32[]{:S(2)}, u32[]{:S(2)}) collective-permute-start(bf16[128,1792]{1,0:T(8,128)(2,1)} %mine.4), channel_id=1, source_target_pairs={{0,128},{128,0},{1,129},{129,1},{2,130},{130,2},{3,131},{131,3},{4... | collective-permute-start | bytes 1376264 | tf_op jit(solution)/shard_map/ppermute | solution.py:16
  3.3 11.2 %collective-permute-start = (s32[128,2]{1,0:T(8,128)S(1)}, s32[128,2]{1,0:T(8,128)S(1)}, u32[]{:S(2)}, u32[]{:S(2)}) collective-permute-start(s32[128,2]{1,0:T(8,128)S(1)} %copy.19.refs_1_), channel_id=1, source_target_pairs={{0,128},{128,0},{1,129},{129,1},{2,130},{130,2},{3,131},{131,3},{4... | collective-permute-start | bytes 3080 | tf_op jit(solution)/shard_map/ppermute | solution.py:16
  19.5 27.6 %all-to-all-start = ((bf16[16,24,1792]{2,1,0:T(8,128)(2,1)}), bf16[16,24,1792]{2,1,0:T(8,128)(2,1)S(1)}, u32[]{:S(2)}, u32[]{:S(2)}) async-start(bf16[16,24,1792]{2,1,0:T(8,128)(2,1)} %bitcast.3), calls=%async_computation | async-start | bytes 2752512 | tf_op jit(solution)/shard_map/all_to_all | solution.py:250
  26.7 11.4 %collective-permute-start.3 = (bf16[128,1792]{1,0:T(8,128)(2,1)S(1)}, bf16[128,1792]{1,0:T(8,128)(2,1)S(1)}, u32[]{:S(2)}, u32[]{:S(2)}) collective-permute-start(bf16[128,1792]{1,0:T(8,128)(2,1)S(1)} %copy-done.10), channel_id=1, source_target_pairs={{0,128},{128,0},{1,129},{129,1},{2,130},{130,2},{3,131},{131,3},{4... | collective-permute-start | bytes 1376264 | tf_op jit(solution)/shard_map/ppermute | solution.py:16
  27.0 10.9 %collective-permute-start.1 = (f32[128,2]{0,1:T(2,128)S(1)}, f32[128,2]{0,1:T(2,128)S(1)}, u32[]{:S(2)}, u32[]{:S(2)}) collective-permute-start(f32[128,2]{0,1:T(2,128)S(1)} %copy-done.23), channel_id=1, source_target_pairs={{0,128},{128,0},{1,129},{129,1},{2,130},{130,2},{3,131},{131,3},{4... | collective-permute-start | bytes 3080 | tf_op jit(solution)/shard_map/ppermute | solution.py:16
  47.1 22.9 %all-to-all-start.1 = ((bf16[16,24,1792]{2,1,0:T(8,128)(2,1)}), bf16[16,24,1792]{2,1,0:T(8,128)(2,1)}, u32[]{:S(2)}, u32[]{:S(2)}) async-start(bf16[16,24,1792]{2,1,0:T(8,128)(2,1)} %bitcast.85), calls=%async_computation.1 | async-start | bytes 2752512 | tf_op jit(solution)/shard_map/all_to_all | solution.py:250
  62.8 21.7 %collective-permute-start.10 = (bf16[2,192,1024]{2,1,0:T(8,128)(2,1)}, bf16[2,192,1024]{2,1,0:T(8,128)(2,1)}, u32[]{:S(2)}, u32[]{:S(2)}) collective-permute-start(bf16[2,192,1024]{2,1,0:T(8,128)(2,1)} %get-tuple-element.40), channel_id=1, source_target_pairs={{0,1},{1,0},{2,3},{3,2},{4,7},{7,4},{5,6},{6,5},{8,9},{9,8},{10,11... | collective-permute-start | bytes 2359304 | tf_op jit(solution)/shard_map/ppermute | solution.py:24
  71.6 3.1 %collective-permute-start.7 = (bf16[192,1792]{1,0:T(8,128)(2,1)S(1)}, bf16[192,1792]{1,0:T(8,128)(2,1)S(1)}, u32[]{:S(2)}, u32[]{:S(2)}) collective-permute-start(bf16[192,1792]{1,0:T(8,128)(2,1)S(1)} %get-tuple-element.78), channel_id=1, source_target_pairs={{0,4},{4,0},{1,5},{5,1},{2,6},{6,2},{3,7},{7,3},{8,12},{12,8},{9,1... | collective-permute-start | bytes 2064392 | tf_op jit(solution)/shard_map/ppermute | solution.py:16
  78.1 18.6 %collective-permute-start.8 = (bf16[2,192,512]{2,1,0:T(8,128)(2,1)S(1)}, bf16[2,192,512]{2,1,0:T(8,128)(2,1)S(1)}, u32[]{:S(2)}, u32[]{:S(2)}) collective-permute-start(bf16[2,192,512]{2,1,0:T(8,128)(2,1)S(1)} %get-tuple-element.43), channel_id=1, source_target_pairs={{0,1},{1,0},{2,3},{3,2},{4,7},{7,4},{5,6},{6,5},{8,9},{9,8},{10,11... | collective-permute-start | bytes 1179656 | tf_op jit(solution)/shard_map/ppermute | solution.py:24
  86.0 20.8 %collective-permute-start.11 = (bf16[192,1024]{1,0:T(8,128)(2,1)S(1)}, bf16[192,1024]{1,0:T(8,128)(2,1)S(1)}, u32[]{:S(2)}, u32[]{:S(2)}) collective-permute-start(bf16[192,1024]{1,0:T(8,128)(2,1)S(1)} %fusion.18), channel_id=1, source_target_pairs={{0,3},{3,0},{1,2},{2,1},{4,5},{5,4},{6,7},{7,6},{8,11},{11,8},{9,1... | collective-permute-start | bytes 1179656 | tf_op jit(solution)/shard_map/ppermute | solution.py:24
  96.9 12.0 %collective-permute-start.9 = (bf16[192,512]{1,0:T(8,128)(2,1)S(1)}, bf16[192,512]{1,0:T(8,128)(2,1)S(1)}, u32[]{:S(2)}, u32[]{:S(2)}) collective-permute-start(bf16[192,512]{1,0:T(8,128)(2,1)S(1)} %fusion.20), channel_id=1, source_target_pairs={{0,3},{3,0},{1,2},{2,1},{4,5},{5,4},{6,7},{7,6},{8,11},{11,8},{9,1... | collective-permute-start | bytes 589832 | tf_op jit(solution)/shard_map/ppermute | solution.py:24
  109.2 6.8 %collective-permute-start.14 = (bf16[192,512]{1,0:T(8,128)(2,1)S(1)}, bf16[192,512]{1,0:T(8,128)(2,1)S(1)}, u32[]{:S(2)}, u32[]{:S(2)}) collective-permute-start(bf16[192,512]{1,0:T(8,128)(2,1)S(1)} %get-tuple-element.90), channel_id=1, source_target_pairs={{0,1},{1,0},{2,3},{3,2},{4,7},{7,4},{5,6},{6,5},{8,9},{9,8},{10,11... | collective-permute-start | bytes 589832 | tf_op jit(solution)/shard_map/ppermute | solution.py:24
  116.0 20.3 %collective-permute-start.15 = (bf16[2,192,512]{2,1,0:T(8,128)(2,1)S(1)}, bf16[2,192,512]{2,1,0:T(8,128)(2,1)S(1)}, u32[]{:S(2)}, u32[]{:S(2)}) collective-permute-start(bf16[2,192,512]{2,1,0:T(8,128)(2,1)S(1)} %pad_maximum_fusion.3), channel_id=1, source_target_pairs={{0,3},{3,0},{1,2},{2,1},{4,5},{5,4},{6,7},{7,6},{8,11},{11,8},{9,1... | collective-permute-start | bytes 1179656 | tf_op jit(solution)/shard_map/ppermute | solution.py:24
  119.9 18.5 %collective-permute-start.12 = (bf16[2,192,512]{2,1,0:T(8,128)(2,1)S(1)}, bf16[2,192,512]{2,1,0:T(8,128)(2,1)S(1)}, u32[]{:S(2)}, u32[]{:S(2)}) collective-permute-start(bf16[2,192,512]{2,1,0:T(8,128)(2,1)S(1)} %pad_maximum_fusion.2), channel_id=1, source_target_pairs={{0,1},{1,0},{2,3},{3,2},{4,7},{7,4},{5,6},{6,5},{8,9},{9,8},{10,11... | collective-permute-start | bytes 1179656 | tf_op jit(solution)/shard_map/ppermute | solution.py:24
  138.5 22.7 %collective-permute-start.13 = (bf16[4,192,512]{2,1,0:T(8,128)(2,1)S(1)}, bf16[4,192,512]{2,1,0:T(8,128)(2,1)}, u32[]{:S(2)}, u32[]{:S(2)}) collective-permute-start(bf16[4,192,512]{2,1,0:T(8,128)(2,1)S(1)} %pad_maximum_fusion.refs_1_), channel_id=1, source_target_pairs={{0,3},{3,0},{1,2},{2,1},{4,5},{5,4},{6,7},{7,6},{8,11},{11,8},{9,1... | collective-permute-start | bytes 2359304 | tf_op jit(solution)/shard_map/ppermute | solution.py:24
  143.6 29.5 %all-to-all-start.2 = ((bf16[16,24,1792]{2,1,0:T(8,128)(2,1)}), bf16[16,24,1792]{2,1,0:T(8,128)(2,1)}, u32[]{:S(2)}, u32[]{:S(2)}) async-start(bf16[16,24,1792]{2,1,0:T(8,128)(2,1)} %bitcast.86), calls=%async_computation.2 | async-start | bytes 2752512 | tf_op jit(solution)/shard_map/all_to_all | solution.py:250
  165.6 3.5 %collective-permute-start.18 = (bf16[192,1792]{1,0:T(8,128)(2,1)S(1)}, bf16[192,1792]{1,0:T(8,128)(2,1)S(1)}, u32[]{:S(2)}, u32[]{:S(2)}) collective-permute-start(bf16[192,1792]{1,0:T(8,128)(2,1)S(1)} %get-tuple-element.50), channel_id=1, source_target_pairs={{0,4},{4,0},{1,5},{5,1},{2,6},{6,2},{3,7},{7,3},{8,12},{12,8},{9,1... | collective-permute-start | bytes 2064392 | tf_op jit(solution)/shard_map/ppermute | solution.py:16
  165.7 3.4 %collective-permute-start.19 = (bf16[192,1792]{1,0:T(8,128)(2,1)S(1)}, bf16[192,1792]{1,0:T(8,128)(2,1)S(1)}, u32[]{:S(2)}, u32[]{:S(2)}) collective-permute-start(bf16[192,1792]{1,0:T(8,128)(2,1)S(1)} %get-tuple-element.51), channel_id=1, source_target_pairs={{0,4},{4,0},{1,5},{5,1},{2,6},{6,2},{3,7},{7,3},{8,12},{12,8},{9,1... | collective-permute-start | bytes 2064392 | tf_op jit(solution)/shard_map/ppermute | solution.py:16
  173.1 33.7 %all-to-all-start.3 = ((bf16[16,24,1792]{2,1,0:T(8,128)(2,1)}), bf16[16,24,1792]{2,1,0:T(8,128)(2,1)}, u32[]{:S(2)}, u32[]{:S(2)}) async-start(bf16[16,24,1792]{2,1,0:T(8,128)(2,1)} %bitcast.87), calls=%async_computation.3 | async-start | bytes 2752512 | tf_op jit(solution)/shard_map/all_to_all | solution.py:250
  183.7 5.1 %collective-permute-start.21 = (f32[2,128]{0,1:T(8,128)S(1)}, f32[2,128]{0,1:T(8,128)S(1)}, u32[]{:S(2)}, u32[]{:S(2)}) collective-permute-start(f32[2,128]{0,1:T(8,128)S(1)} %slice.108), channel_id=1, source_target_pairs={{0,128},{128,0},{1,129},{129,1},{2,130},{130,2},{3,131},{131,3},{4... | collective-permute-start | bytes 3080 | tf_op jit(solution)/shard_map/ppermute | solution.py:16
  184.3 24.6 %collective-permute-start.20 = (bf16[128,1792]{1,0:T(8,128)(2,1)S(1)}, bf16[128,1792]{1,0:T(8,128)(2,1)S(1)}, u32[]{:S(2)}, u32[]{:S(2)}) collective-permute-start(bf16[128,1792]{1,0:T(8,128)(2,1)S(1)} %get-tuple-element.58), channel_id=1, source_target_pairs={{0,128},{128,0},{1,129},{129,1},{2,130},{130,2},{3,131},{131,3},{4... | collective-permute-start | bytes 1376264 | tf_op jit(solution)/shard_map/ppermute | solution.py:16
  188.7 10.9 %collective-permute-start.22 = (f32[2,128]{0,1:T(8,128)S(1)}, f32[2,128]{0,1:T(8,128)S(1)}, u32[]{:S(2)}, u32[]{:S(2)}) collective-permute-start(f32[2,128]{0,1:T(8,128)S(1)} %slice_add_fusion.1), channel_id=1, source_target_pairs={{0,1},{1,0},{2,3},{3,2},{4,7},{7,4},{5,6},{6,5},{8,9},{9,8},{10,11... | collective-permute-start | bytes 3080 | tf_op jit(solution)/shard_map/ppermute | solution.py:24
  199.7 6.5 %collective-permute-start.23 = (f32[2,128]{0,1:T(8,128)S(1)}, f32[2,128]{0,1:T(8,128)S(1)}, u32[]{:S(2)}, u32[]{:S(2)}) collective-permute-start(f32[2,128]{0,1:T(8,128)S(1)} %add.54), channel_id=1, source_target_pairs={{0,3},{3,0},{1,2},{2,1},{4,5},{5,4},{6,7},{7,6},{8,11},{11,8},{9,1... | collective-permute-start | bytes 3080 | tf_op jit(solution)/shard_map/ppermute | solution.py:24
  208.8 11.3 %collective-permute-start.24 = (bf16[128,1792]{1,0:T(8,128)(2,1)S(1)}, bf16[128,1792]{1,0:T(8,128)(2,1)S(1)}, u32[]{:S(2)}, u32[]{:S(2)}) collective-permute-start(bf16[128,1792]{1,0:T(8,128)(2,1)S(1)} %slice.155), channel_id=1, source_target_pairs={{0,128},{128,0},{1,129},{129,1},{2,130},{130,2},{3,131},{131,3},{4... | collective-permute-start | bytes 1376264 | tf_op jit(solution)/shard_map/ppermute | solution.py:16
  (29 other events, 164.1 us)

commit v4 on v3

--- a/solution.py
+++ b/solution.py
@@ -49,37 +49,37 @@
     )(code, *args)
 
 
-def shuffled(value, bit):
-    half = value.shape[0] // 2
-    return [(part ^ bit, value[part * half : (part + 1) * half]) for part in range(2)]
-
-
 def first_kernel(product, count, code, mine, top, bottom, *refs):
     weights, (keep, away, rel) = refs[:count], refs[count:]
-
-    def half_of_rows(step, rows):
-        for place, part in shuffled(rows, code[1]):
-            rel[step, place] = part
+    block, quarter = top.shape
+
+    @pl.loop(0, 2)
+    def _(step):
+        @pl.when(step == code[0])
+        def _():
+            for part in range(2):
+                rel[step, part ^ code[1]] = mine[part * block : (part + 1) * block, :]
+
+        @pl.when(step != code[0])
+        def _():
+            for part, rows in enumerate((top, bottom)):
+                rel[step, part ^ code[1]] = rows[...]
+
         column = 0
         for weight in weights:
-            value = product(rows, weight[...])
+            value = product(rel[step].reshape(2 * block, quarter), weight[...])
             width = value.shape[1]
-            for place, part in shuffled(value, code[1]):
-
-                @pl.when(step == 0)
-                def _():
-                    keep[place, :, column : column + width] = part
-
-                @pl.when(step == 1)
-                def _():
-                    away[place, :, column : column + width] = part.astype(BF)
+            value = value.reshape(2, block, width)
+
+            @pl.when(step == 0)
+            def _():
+                keep[:, :, column : column + width] = value
+
+            @pl.when(step == 1)
+            def _():
+                away[:, :, column : column + width] = value.astype(BF)
 
             column += width
-
-    @pl.loop(0, 2)
-    def _(step):
-        other = jnp.concatenate([top[...], bottom[...]], 0)
-        half_of_rows(step, jnp.where((step ^ code[0]) == 0, mine[...], other))
 
 
 def first_products(product, code, mine, other, weights, width):
@@ -103,14 +103,22 @@
     half = value.shape[0] // 2
     for j in range(2):
         part = value[j * half : (j + 1) * half]
-        if theirs:
+        if len(outs) == 1 and not theirs:
+            outs[0][j * half : (j + 1) * half, :] = part
+        elif theirs:
             outs[0][j * half : (j + 1) * half, :] = (part + theirs[j][...].astype(F32)).astype(BF)
         else:
             outs[j][...] = part.astype(BF)
 
 
+def add_kernel(_, mine, top, bottom, out):
+    half = top.shape[0]
+    out[:half, :] = (mine[:half, :] + top[...].astype(F32)).astype(BF)
+    out[half:, :] = (mine[half:, :] + bottom[...].astype(F32)).astype(BF)
+
+
 def out_rows_kernel(side, code, hidden, w_down, *refs):
-    theirs, outs = refs[:2], refs[2:]
+    theirs, outs = refs[:-1], refs[-1:]
     if side == 1:
         theirs, outs = (), refs
     parts = [hidden[2 * (side ^ code[0]) + (j ^ code[1])] for j in range(2)]
@@ -119,7 +127,7 @@
 
 
 def in_rows_kernel(side, code, near, far, w_gate, w_up, *refs):
-    theirs, outs = refs[:2], refs[2:]
+    theirs, outs = refs[:-1], refs[-1:]
     if side == 1:
         theirs, outs = (), refs
     place = side ^ code[0]
@@ -135,7 +143,7 @@
 def last_products(kernel, code, pieces, weights, quarter, theirs):
     side = 1 if theirs is None else 0
     rows = pieces[0].shape[1]
-    whole_shape = jax.ShapeDtypeStruct((2 * rows, quarter), BF)
+    whole_shape = jax.ShapeDtypeStruct((2 * rows, quarter), BF if theirs else F32)
     half_shape = jax.ShapeDtypeStruct((rows, quarter), BF)
     return local_call(
         lambda *refs: kernel(side, *refs),
@@ -172,9 +180,10 @@
 
 
 def rows_kernel(_, turned, mine, peer, out):
-    tokens = mine.shape[0]
-    rows = dot(turned[:, :tokens], mine[...], NN) + dot(turned[:, tokens:], peer[...], NN)
-    out[...] = rows.astype(BF)
+    every = jnp.concatenate([mine[...], peer[...]], 0)
+    width = min(256, every.shape[1])
+    for at in range(0, every.shape[1], width):
+        out[:, at : at + width] = dot(turned[...], every[:, at : at + width], NN).astype(BF)
 
 
 def picks_of(local, k, first, last, slots):
@@ -278,13 +287,16 @@
     gate_up = keep + tie(got, away_c).astype(F32)
     got = cross(gate_up[1].astype(BF), SECOND)
 
-    gate_up = gate_up[0] + got.astype(F32)
+    hidden_cot = keep_c + got_c.astype(F32)
+    away_c = hidden_cot[1].astype(BF)
+    gate_up = gate_up[0] + tie(got, away_c).astype(F32)
     gate, up = gate_up[:, :half], gate_up[:, half:]
     hidden = (jax.nn.silu(gate) * up).astype(BF)
 
-    hidden_cot = keep_c + got_c.astype(F32)
-    hidden = jnp.stack([hidden, cross(hidden, FIRST)])
-    got = cross(hidden_cot[1].astype(BF), SECOND)
+    got_h = cross(hidden, FIRST)
+    got = cross(away_c, SECOND)
+    got, got_h = lax.optimization_barrier((got, got_h))
+    hidden = jnp.stack([hidden, got_h])
     hidden_cot = hidden_cot[0] + got.astype(F32)
     sig = jax.nn.sigmoid(gate)
     gate_cot = (hidden_cot * up * sig * (1.0 + gate * (1.0 - sig))).astype(BF)
@@ -322,19 +334,18 @@
         cotangent,
         cot_peer,
     )
-    in_back = send_back(in_rows_kernel, (near, far), (w_gate, w_up), grad_down)
+    far = tie(far, grad_down)
+    away_in = last_products(in_rows_kernel, code, (near, far), (w_gate, w_up), quarter, None)
+    theirs_in = [swap(part, "core") for part in away_in]
+    mine_in = last_products(in_rows_kernel, code, (near, far), (w_gate, w_up), quarter, ())
+    in_back = local_call(
+        add_kernel, jax.ShapeDtypeStruct((slots, quarter), BF), code, mine_in, *tie(theirs_in, mine_in)
+    )
     returned_in = exchange(in_back)
     near, far, out_mine, grad_p = tie((near, far, out_mine, grad_p), in_back)
 
-    moe_out = (out_mine + swap(out_peer, "z").astype(F32)).astype(BF)
-    grad_p = grad_p.T
-    grad_p = grad_p[:, :tok_rows] + swap(grad_p[:, tok_rows:], "z")
-    grad_p = grad_p + cross(grad_p, FIRST)
-    grad_p = grad_p + cross(grad_p, SECOND)
-
-    tok_part = dot(assign, returned_in, NN)
-    grad_tokens = (tok_part[:tok_rows] + swap(tok_part[tok_rows:].astype(BF), "z").astype(F32)).astype(BF)
-
+    out_theirs = swap(out_peer, "z")
+    moe_out = (out_mine + out_theirs.astype(F32)).astype(BF)
     rows_in = rows_in.reshape(2 * slots, quarter)
 
     def all_rows(kind):
@@ -343,6 +354,15 @@
 
     grad_gate = dot(rows_in, all_rows(0), TN).astype(BF)
     grad_up = dot(rows_in, all_rows(1), TN).astype(BF)
+    grad_p = grad_p.T
+    theirs = tie(swap(grad_p[:, tok_rows:], "z"), (grad_gate, grad_up))
+    grad_p = grad_p[:, :tok_rows] + theirs
+    grad_p = tie(grad_p + cross(grad_p, FIRST), out_theirs)
+    grad_p = grad_p + cross(grad_p, SECOND)
+
+    tok_part = dot(assign, returned_in, NN)
+    grad_tokens = (tok_part[:tok_rows] + swap(tok_part[tok_rows:].astype(BF), "z").astype(F32)).astype(BF)
+
     return (moe_out, grad_p.T, grad_tokens, grad_gate[None], grad_up[None], grad_down[None])
 
 

time: 224 us -> 214 us (0.955); the launches traced: 221 us -> 213 us
  starting transfers between devices: 62.1 us -> 54.9 us
  local copies, waits for them, and re-layouts: 13.8 us -> 11.1 us
    ppermute x10, starting transfers between devices: 24.8 us -> 19 us  [cross(): return lax.ppermute(value, ('core', 'tensor'), step)]
    all_to_all x4, waiting for transfers between devices: 9.61 us -> 14.6 us  [exchange(): lax.all_to_all(rows.reshape(chips, planes * capacity, quarter), ('x', 'y'...]
    ppermute x10, waiting for transfers between devices: 55.8 us -> 51.2 us  [cross(): return lax.ppermute(value, ('core', 'tensor'), step)]
    all_to_all x4, starting transfers between devices: 28.4 us -> 25.2 us  [exchange(): lax.all_to_all(rows.reshape(chips, planes * capacity, quarter), ('x', 'y'...]
    unnamed x50, local copies, waits for them, and re-layouts: 10.7 us -> 8.04 us
    pallas_call x10 -> x11, Pallas kernels: 25.3 us -> 26 us  [local_call(): pl.pallas_call(kernel, in_specs=[pl.BlockSpec(memory_space=pltpu.SMEM)] +...]
  transfers between devices with their start and end apart: 29 -> 29, of which waited for: 21 -> 21; matrix products, arithmetic and copies ran while one was open for 8% -> 9% of each run, Pallas kernels for 10% -> 11%
where the time goes in v4:
time: 214 us; the launch traced here: 213 us
  waiting for transfers between devices  105 us (49%)
  starting transfers between devices  54.9 us (26%)
  Pallas kernels  26 us (12%)
  matrix products  12.6 us (6%)
  local copies, waits for them, and re-layouts  11.1 us (5%)
  other arithmetic  2.95 us (1%)
    ppermute x10, waiting for transfers between devices, cross(): return lax.ppermute(value, ('core', 'tensor'), step)  51.2 us
    ppermute x15, waiting for transfers between devices, swap(): return lax.ppermute(value, axis, PAIR)  38.7 us
    pallas_call x11, Pallas kernels, local_call(): pl.pallas_call(kernel, in_specs=[pl.BlockSpec(memory_space=pltpu.SMEM)] +...  26 us
    all_to_all x4, starting transfers between devices, exchange(): lax.all_to_all(rows.reshape(chips, planes * capacity, quarter), ('x', 'y'...  25.2 us
    ppermute x10, starting transfers between devices, cross(): return lax.ppermute(value, ('core', 'tensor'), step)  19 us
    all_to_all x4, waiting for transfers between devices, exchange(): lax.all_to_all(rows.reshape(chips, planes * capacity, quarter), ('x', 'y'...  14.6 us
    dot_general x4, matrix products, dot(): return lax.dot_general(a, b, (dims, ((), ())), preferred_element_type=F32)  12.6 us
    ppermute x15, starting transfers between devices, swap(): return lax.ppermute(value, axis, PAIR)  10.7 us
  transfers between devices with their start and end apart: 29, of which 21 were waited for; matrix products, arithmetic and copies ran while one was open for 9% of the time, Pallas kernels for 11%

profile of v4, /device:TPU:32, one launch (start us, length us, event | category | flops | bytes accessed | tf_op | source)
XLA Modules:
  0.0 213.2 jit_solution(17862232049652586262)
XLA Ops:
  3.7 10.9 %collective-permute-done.refs_2_ = s32[128,2]{1,0:T(8,128)S(1)} collective-permute-done((s32[128,2]{1,0:T(8,128)S(1)}, s32[128,2]{1,0:T(8,128)S(1)}, u32[]{:S(2)}, u32[]{:S(2)}) %collective-permute-start) | collective-permute-done | bytes 1056 | tf_op jit(solution)/shard_map/ppermute | solution.py:16
  19.1 7.2 %all-to-all-start = ((bf16[16,24,1792]{2,1,0:T(8,128)(2,1)}), bf16[16,24,1792]{2,1,0:T(8,128)(2,1)S(1)}, u32[]{:S(2)}, u32[]{:S(2)}) async-start(bf16[16,24,1792]{2,1,0:T(8,128)(2,1)} %bitcast.3), calls=%async_computation | async-start | bytes 2752512 | tf_op jit(solution)/shard_map/all_to_all | solution.py:259
  28.4 9.1 %collective-permute-done.1 = f32[128,2]{0,1:T(2,128)S(1)} collective-permute-done((f32[128,2]{0,1:T(2,128)S(1)}, f32[128,2]{0,1:T(2,128)S(1)}, u32[]{:S(2)}, u32[]{:S(2)}) %collective-permute-start.1) | collective-permute-done | bytes 1056 | tf_op jit(solution)/shard_map/ppermute | solution.py:16
  41.1 5.7 %all-to-all-done = bf16[16,24,1792]{2,1,0:T(8,128)(2,1)S(1)} async-done(((bf16[16,24,1792]{2,1,0:T(8,128)(2,1)}), bf16[16,24,1792]{2,1,0:T(8,128)(2,1)S(1)}, u32[]{:S(2)}, u32[]{:S(2)}) %all-to-all-start) | async-done | bytes 1376288 | tf_op jit(solution)/shard_map/all_to_all | solution.py:259
  46.8 4.5 %all-to-all-start.1 = ((bf16[16,24,1792]{2,1,0:T(8,128)(2,1)}), bf16[16,24,1792]{2,1,0:T(8,128)(2,1)}, u32[]{:S(2)}, u32[]{:S(2)}) async-start(bf16[16,24,1792]{2,1,0:T(8,128)(2,1)} %bitcast.85), calls=%async_computation.1 | async-start | bytes 2752512 | tf_op jit(solution)/shard_map/all_to_all | solution.py:259
  54.6 5.3 %shard_map.121 = (f32[2,192,1024]{2,1,0:T(8,128)S(1)}, bf16[2,192,1024]{2,1,0:T(8,128)(2,1)}, bf16[2,2,192,1792]{3,2,1,0:T(8,128)(2,1)S(1)}) custom-call(s32[2]{0:T(128)S(1)} %pad_add_fusion._.refs_0_, bf16[384,1792]{1,0:T(8,128)(2,1)S(1)} %bitcast.83, bf16[192,1792]{1,0:T(8,128)(2,1)S(1)} %collective-permute-done.4.refs_2_, ...), custom_call_target="tpu_custom_call" | custom-call | flops 1000 | bytes 1000 | tf_op jit(solution)/shard_map/pallas_call | solution.py:42
  62.6 3.3 %collective-permute-start.10 = (bf16[2,192,1024]{2,1,0:T(8,128)(2,1)}, bf16[2,192,1024]{2,1,0:T(8,128)(2,1)S(1)}, u32[]{:S(2)}, u32[]{:S(2)}) collective-permute-start(bf16[2,192,1024]{2,1,0:T(8,128)(2,1)} %get-tuple-element.46), channel_id=1, source_target_pairs={{0,1},{1,0},{2,3},{3,2},{4,7},{7,4},{5,6},{6,5},{8,9},{9,8},{10,11... | collective-permute-start | bytes 2359304 | tf_op jit(solution)/shard_map/ppermute | solution.py:24
  65.8 3.9 %all-to-all-done.1 = bf16[16,24,1792]{2,1,0:T(8,128)(2,1)} async-done(((bf16[16,24,1792]{2,1,0:T(8,128)(2,1)}), bf16[16,24,1792]{2,1,0:T(8,128)(2,1)}, u32[]{:S(2)}, u32[]{:S(2)}) %all-to-all-start.1) | async-done | bytes 1376288 | tf_op jit(solution)/shard_map/all_to_all | solution.py:259
  74.3 3.6 %shard_map.122 = (f32[2,192,512]{2,1,0:T(8,128)S(1)}, bf16[2,192,512]{2,1,0:T(8,128)(2,1)S(1)}, bf16[2,2,192,1792]{3,2,1,0:T(8,128)(2,1)S(1)}) custom-call(s32[2]{0:T(128)S(1)} %pad_add_fusion._.refs_0_, bf16[384,1792]{1,0:T(8,128)(2,1)} %bitcast.6.refs_1_, bf16[192,1792]{1,0:T(8,128)(2,1)S(1)} %collective-permute-done.6.refs_2_, ...), custom_call_target="tpu_custom_call" | custom-call | flops 1000 | bytes 1000 | tf_op jit(solution)/shard_map/pallas_call | solution.py:42
  77.9 3.4 %collective-permute-start.8 = (bf16[2,192,512]{2,1,0:T(8,128)(2,1)S(1)}, bf16[2,192,512]{2,1,0:T(8,128)(2,1)S(1)}, u32[]{:S(2)}, u32[]{:S(2)}) collective-permute-start(bf16[2,192,512]{2,1,0:T(8,128)(2,1)S(1)} %get-tuple-element.49), channel_id=1, source_target_pairs={{0,1},{1,0},{2,3},{3,2},{4,7},{7,4},{5,6},{6,5},{8,9},{9,8},{10,11... | collective-permute-start | bytes 1179656 | tf_op jit(solution)/shard_map/ppermute | solution.py:24
  81.3 3.1 %collective-permute-done.10 = bf16[2,192,1024]{2,1,0:T(8,128)(2,1)S(1)} collective-permute-done((bf16[2,192,1024]{2,1,0:T(8,128)(2,1)}, bf16[2,192,1024]{2,1,0:T(8,128)(2,1)S(1)}, u32[]{:S(2)}, u32[]{:S(2)}) %collective-permute-start.10) | collective-permute-done | bytes 786464 | tf_op jit(solution)/shard_map/ppermute | solution.py:24
  84.7 7.2 %collective-permute-start.11 = (bf16[192,1024]{1,0:T(8,128)(2,1)S(1)}, bf16[192,1024]{1,0:T(8,128)(2,1)S(1)}, u32[]{:S(2)}, u32[]{:S(2)}) collective-permute-start(bf16[192,1024]{1,0:T(8,128)(2,1)S(1)} %fusion.16), channel_id=1, source_target_pairs={{0,3},{3,0},{1,2},{2,1},{4,5},{5,4},{6,7},{7,6},{8,11},{11,8},{9,1... | collective-permute-start | bytes 1179656 | tf_op jit(solution)/shard_map/ppermute | solution.py:24
  91.9 8.9 %collective-permute-done.8 = bf16[2,192,512]{2,1,0:T(8,128)(2,1)S(1)} collective-permute-done((bf16[2,192,512]{2,1,0:T(8,128)(2,1)S(1)}, bf16[2,192,512]{2,1,0:T(8,128)(2,1)S(1)}, u32[]{:S(2)}, u32[]{:S(2)}) %collective-permute-start.8) | collective-permute-done | bytes 393248 | tf_op jit(solution)/shard_map/ppermute | solution.py:24
  101.2 5.0 %collective-permute-done.11 = bf16[192,1024]{1,0:T(8,128)(2,1)S(1)} collective-permute-done((bf16[192,1024]{1,0:T(8,128)(2,1)S(1)}, bf16[192,1024]{1,0:T(8,128)(2,1)S(1)}, u32[]{:S(2)}, u32[]{:S(2)}) %collective-permute-start.11) | collective-permute-done | bytes 393248 | tf_op jit(solution)/shard_map/ppermute | solution.py:24
  106.7 8.1 %collective-permute-done.12 = bf16[192,512]{1,0:T(8,128)(2,1)S(1)} collective-permute-done((bf16[192,512]{1,0:T(8,128)(2,1)S(1)}, bf16[192,512]{1,0:T(8,128)(2,1)S(1)}, u32[]{:S(2)}, u32[]{:S(2)}) %collective-permute-start.12) | collective-permute-done | bytes 196640 | tf_op jit(solution)/shard_map/ppermute | solution.py:24
  118.2 16.2 %collective-permute-done.15 = bf16[2,192,512]{2,1,0:T(8,128)(2,1)S(1)} collective-permute-done((bf16[2,192,512]{2,1,0:T(8,128)(2,1)S(1)}, bf16[2,192,512]{2,1,0:T(8,128)(2,1)S(1)}, u32[]{:S(2)}, u32[]{:S(2)}) %collective-permute-start.15) | collective-permute-done | bytes 393248 | tf_op jit(solution)/shard_map/ppermute | solution.py:24
  141.7 8.9 %all-to-all-start.2 = ((bf16[16,24,1792]{2,1,0:T(8,128)(2,1)}), bf16[16,24,1792]{2,1,0:T(8,128)(2,1)S(1)}, u32[]{:S(2)}, u32[]{:S(2)}) async-start(bf16[16,24,1792]{2,1,0:T(8,128)(2,1)} %bitcast.86), calls=%async_computation.2 | async-start | bytes 2752512 | tf_op jit(solution)/shard_map/all_to_all | solution.py:259
  150.6 4.8 %convolution_convert_fusion.2 = bf16[512,1792]{1,0:T(8,128)(2,1)} fusion(bf16[768,512]{1,0:T(8,128)(2,1)S(1)} %bitcast.81, bf16[768,1792]{1,0:T(8,128)(2,1)} %bitcast.87), kind=kOutput, calls=%fused_computation.2 | convolution fusion | flops 1410203648 | bytes 5373952 | tf_op jit(solution)/shard_map/dot_general | solution.py:32
  155.4 4.0 %collective-permute-done.14.refs_2_ = bf16[4,192,512]{2,1,0:T(8,128)(2,1)} collective-permute-done((bf16[4,192,512]{2,1,0:T(8,128)(2,1)S(1)}, bf16[4,192,512]{2,1,0:T(8,128)(2,1)}, u32[]{:S(2)}, u32[]{:S(2)}) %collective-permute-start.14) | collective-permute-done | bytes 786464 | tf_op jit(solution)/shard_map/ppermute | solution.py:24
  167.4 5.0 %all-to-all-done.2 = bf16[16,24,1792]{2,1,0:T(8,128)(2,1)S(1)} async-done(((bf16[16,24,1792]{2,1,0:T(8,128)(2,1)}), bf16[16,24,1792]{2,1,0:T(8,128)(2,1)S(1)}, u32[]{:S(2)}, u32[]{:S(2)}) %all-to-all-start.2) | async-done | bytes 1376288 | tf_op jit(solution)/shard_map/all_to_all | solution.py:259
  172.4 4.6 %all-to-all-start.3 = ((bf16[16,24,1792]{2,1,0:T(8,128)(2,1)}), bf16[16,24,1792]{2,1,0:T(8,128)(2,1)}, u32[]{:S(2)}, u32[]{:S(2)}) async-start(bf16[16,24,1792]{2,1,0:T(8,128)(2,1)} %bitcast.33), calls=%async_computation.3 | async-start | bytes 2752512 | tf_op jit(solution)/shard_map/all_to_all | solution.py:259
  188.3 3.8 %collective-permute-done.21 = f32[2,128]{0,1:T(8,128)S(1)} collective-permute-done((f32[2,128]{0,1:T(8,128)S(1)}, f32[2,128]{0,1:T(8,128)S(1)}, u32[]{:S(2)}, u32[]{:S(2)}) %collective-permute-start.21) | collective-permute-done | bytes 1056 | tf_op jit(solution)/shard_map/ppermute | solution.py:16
  192.2 5.2 %collective-permute-done.22 = f32[2,128]{0,1:T(8,128)S(1)} collective-permute-done((f32[2,128]{0,1:T(8,128)S(1)}, f32[2,128]{0,1:T(8,128)S(1)}, u32[]{:S(2)}, u32[]{:S(2)}) %collective-permute-start.22) | collective-permute-done | bytes 1056 | tf_op jit(solution)/shard_map/ppermute | solution.py:24
  205.2 7.2 %collective-permute-done.24 = bf16[128,1792]{1,0:T(8,128)(2,1)S(1)} collective-permute-done((bf16[128,1792]{1,0:T(8,128)(2,1)S(1)}, bf16[128,1792]{1,0:T(8,128)(2,1)S(1)}, u32[]{:S(2)}, u32[]{:S(2)}) %collective-permute-start.24) | collective-permute-done | bytes 458784 | tf_op jit(solution)/shard_map/ppermute | solution.py:16
  (125 shorter events, 63.4 us)
Async XLA Ops:
  0.6 15.3 %collective-permute-start.2 = (bf16[128,1792]{1,0:T(8,128)(2,1)}, bf16[128,1792]{1,0:T(8,128)(2,1)S(1)}, u32[]{:S(2)}, u32[]{:S(2)}) collective-permute-start(bf16[128,1792]{1,0:T(8,128)(2,1)} %mine.4), channel_id=1, source_target_pairs={{0,128},{128,0},{1,129},{129,1},{2,130},{130,2},{3,131},{131,3},{4... | collective-permute-start | bytes 1376264 | tf_op jit(solution)/shard_map/ppermute | solution.py:16
  3.3 11.2 %collective-permute-start = (s32[128,2]{1,0:T(8,128)S(1)}, s32[128,2]{1,0:T(8,128)S(1)}, u32[]{:S(2)}, u32[]{:S(2)}) collective-permute-start(s32[128,2]{1,0:T(8,128)S(1)} %copy.19.refs_1_), channel_id=1, source_target_pairs={{0,128},{128,0},{1,129},{129,1},{2,130},{130,2},{3,131},{131,3},{4... | collective-permute-start | bytes 3080 | tf_op jit(solution)/shard_map/ppermute | solution.py:16
  19.1 27.6 %all-to-all-start = ((bf16[16,24,1792]{2,1,0:T(8,128)(2,1)}), bf16[16,24,1792]{2,1,0:T(8,128)(2,1)S(1)}, u32[]{:S(2)}, u32[]{:S(2)}) async-start(bf16[16,24,1792]{2,1,0:T(8,128)(2,1)} %bitcast.3), calls=%async_computation | async-start | bytes 2752512 | tf_op jit(solution)/shard_map/all_to_all | solution.py:259
  26.3 11.4 %collective-permute-start.3 = (bf16[128,1792]{1,0:T(8,128)(2,1)S(1)}, bf16[128,1792]{1,0:T(8,128)(2,1)S(1)}, u32[]{:S(2)}, u32[]{:S(2)}) collective-permute-start(bf16[128,1792]{1,0:T(8,128)(2,1)S(1)} %copy-done.8), channel_id=1, source_target_pairs={{0,128},{128,0},{1,129},{129,1},{2,130},{130,2},{3,131},{131,3},{4... | collective-permute-start | bytes 1376264 | tf_op jit(solution)/shard_map/ppermute | solution.py:16
  26.7 10.9 %collective-permute-start.1 = (f32[128,2]{0,1:T(2,128)S(1)}, f32[128,2]{0,1:T(2,128)S(1)}, u32[]{:S(2)}, u32[]{:S(2)}) collective-permute-start(f32[128,2]{0,1:T(2,128)S(1)} %copy-done.23), channel_id=1, source_target_pairs={{0,128},{128,0},{1,129},{129,1},{2,130},{130,2},{3,131},{131,3},{4... | collective-permute-start | bytes 3080 | tf_op jit(solution)/shard_map/ppermute | solution.py:16
  46.8 22.9 %all-to-all-start.1 = ((bf16[16,24,1792]{2,1,0:T(8,128)(2,1)}), bf16[16,24,1792]{2,1,0:T(8,128)(2,1)}, u32[]{:S(2)}, u32[]{:S(2)}) async-start(bf16[16,24,1792]{2,1,0:T(8,128)(2,1)} %bitcast.85), calls=%async_computation.1 | async-start | bytes 2752512 | tf_op jit(solution)/shard_map/all_to_all | solution.py:259
  62.6 21.8 %collective-permute-start.10 = (bf16[2,192,1024]{2,1,0:T(8,128)(2,1)}, bf16[2,192,1024]{2,1,0:T(8,128)(2,1)S(1)}, u32[]{:S(2)}, u32[]{:S(2)}) collective-permute-start(bf16[2,192,1024]{2,1,0:T(8,128)(2,1)} %get-tuple-element.46), channel_id=1, source_target_pairs={{0,1},{1,0},{2,3},{3,2},{4,7},{7,4},{5,6},{6,5},{8,9},{9,8},{10,11... | collective-permute-start | bytes 2359304 | tf_op jit(solution)/shard_map/ppermute | solution.py:24
  71.2 3.1 %collective-permute-start.6 = (bf16[192,1792]{1,0:T(8,128)(2,1)S(1)}, bf16[192,1792]{1,0:T(8,128)(2,1)S(1)}, u32[]{:S(2)}, u32[]{:S(2)}) collective-permute-start(bf16[192,1792]{1,0:T(8,128)(2,1)S(1)} %get-tuple-element.91), channel_id=1, source_target_pairs={{0,4},{4,0},{1,5},{5,1},{2,6},{6,2},{3,7},{7,3},{8,12},{12,8},{9,1... | collective-permute-start | bytes 2064392 | tf_op jit(solution)/shard_map/ppermute | solution.py:16
  77.9 22.9 %collective-permute-start.8 = (bf16[2,192,512]{2,1,0:T(8,128)(2,1)S(1)}, bf16[2,192,512]{2,1,0:T(8,128)(2,1)S(1)}, u32[]{:S(2)}, u32[]{:S(2)}) collective-permute-start(bf16[2,192,512]{2,1,0:T(8,128)(2,1)S(1)} %get-tuple-element.49), channel_id=1, source_target_pairs={{0,1},{1,0},{2,3},{3,2},{4,7},{7,4},{5,6},{6,5},{8,9},{9,8},{10,11... | collective-permute-start | bytes 1179656 | tf_op jit(solution)/shard_map/ppermute | solution.py:24
  84.7 21.6 %collective-permute-start.11 = (bf16[192,1024]{1,0:T(8,128)(2,1)S(1)}, bf16[192,1024]{1,0:T(8,128)(2,1)S(1)}, u32[]{:S(2)}, u32[]{:S(2)}) collective-permute-start(bf16[192,1024]{1,0:T(8,128)(2,1)S(1)} %fusion.16), channel_id=1, source_target_pairs={{0,3},{3,0},{1,2},{2,1},{4,5},{5,4},{6,7},{7,6},{8,11},{11,8},{9,1... | collective-permute-start | bytes 1179656 | tf_op jit(solution)/shard_map/ppermute | solution.py:24
  100.9 13.9 %collective-permute-start.9 = (bf16[192,512]{1,0:T(8,128)(2,1)S(1)}, bf16[192,512]{1,0:T(8,128)(2,1)S(1)}, u32[]{:S(2)}, u32[]{:S(2)}) collective-permute-start(bf16[192,512]{1,0:T(8,128)(2,1)S(1)} %fusion.18), channel_id=1, source_target_pairs={{0,3},{3,0},{1,2},{2,1},{4,5},{5,4},{6,7},{7,6},{8,11},{11,8},{9,1... | collective-permute-start | bytes 589832 | tf_op jit(solution)/shard_map/ppermute | solution.py:24
  106.5 8.3 %collective-permute-start.12 = (bf16[192,512]{1,0:T(8,128)(2,1)S(1)}, bf16[192,512]{1,0:T(8,128)(2,1)S(1)}, u32[]{:S(2)}, u32[]{:S(2)}) collective-permute-start(bf16[192,512]{1,0:T(8,128)(2,1)S(1)} %multiply_convert_fusion.2), channel_id=1, source_target_pairs={{0,1},{1,0},{2,3},{3,2},{4,7},{7,4},{5,6},{6,5},{8,9},{9,8},{10,11... | collective-permute-start | bytes 589832 | tf_op jit(solution)/shard_map/ppermute | solution.py:24
  114.8 19.6 %collective-permute-start.15 = (bf16[2,192,512]{2,1,0:T(8,128)(2,1)S(1)}, bf16[2,192,512]{2,1,0:T(8,128)(2,1)S(1)}, u32[]{:S(2)}, u32[]{:S(2)}) collective-permute-start(bf16[2,192,512]{2,1,0:T(8,128)(2,1)S(1)} %pad_maximum_fusion.3), channel_id=1, source_target_pairs={{0,3},{3,0},{1,2},{2,1},{4,5},{5,4},{6,7},{7,6},{8,11},{11,8},{9,1... | collective-permute-start | bytes 1179656 | tf_op jit(solution)/shard_map/ppermute | solution.py:24
  115.2 21.4 %collective-permute-start.13 = (bf16[2,192,512]{2,1,0:T(8,128)(2,1)S(1)}, bf16[2,192,512]{2,1,0:T(8,128)(2,1)S(1)}, u32[]{:S(2)}, u32[]{:S(2)}) collective-permute-start(bf16[2,192,512]{2,1,0:T(8,128)(2,1)S(1)} %pad_maximum_fusion.2), channel_id=1, source_target_pairs={{0,1},{1,0},{2,3},{3,2},{4,7},{7,4},{5,6},{6,5},{8,9},{9,8},{10,11... | collective-permute-start | bytes 1179656 | tf_op jit(solution)/shard_map/ppermute | solution.py:24
  136.6 22.7 %collective-permute-start.14 = (bf16[4,192,512]{2,1,0:T(8,128)(2,1)S(1)}, bf16[4,192,512]{2,1,0:T(8,128)(2,1)}, u32[]{:S(2)}, u32[]{:S(2)}) collective-permute-start(bf16[4,192,512]{2,1,0:T(8,128)(2,1)S(1)} %pad_maximum_fusion.refs_1_), channel_id=1, source_target_pairs={{0,3},{3,0},{1,2},{2,1},{4,5},{5,4},{6,7},{7,6},{8,11},{11,8},{9,1... | collective-permute-start | bytes 2359304 | tf_op jit(solution)/shard_map/ppermute | solution.py:24
  141.7 30.7 %all-to-all-start.2 = ((bf16[16,24,1792]{2,1,0:T(8,128)(2,1)}), bf16[16,24,1792]{2,1,0:T(8,128)(2,1)S(1)}, u32[]{:S(2)}, u32[]{:S(2)}) async-start(bf16[16,24,1792]{2,1,0:T(8,128)(2,1)} %bitcast.86), calls=%async_computation.2 | async-start | bytes 2752512 | tf_op jit(solution)/shard_map/all_to_all | solution.py:259
  162.1 3.4 %collective-permute-start.18 = (bf16[192,1792]{1,0:T(8,128)(2,1)S(1)}, bf16[192,1792]{1,0:T(8,128)(2,1)S(1)}, u32[]{:S(2)}, u32[]{:S(2)}) collective-permute-start(bf16[192,1792]{1,0:T(8,128)(2,1)S(1)} %get-tuple-element.63), channel_id=1, source_target_pairs={{0,4},{4,0},{1,5},{5,1},{2,6},{6,2},{3,7},{7,3},{8,12},{12,8},{9,1... | collective-permute-start | bytes 2064392 | tf_op jit(solution)/shard_map/ppermute | solution.py:16
  162.2 3.3 %collective-permute-start.19 = (bf16[192,1792]{1,0:T(8,128)(2,1)S(1)}, bf16[192,1792]{1,0:T(8,128)(2,1)S(1)}, u32[]{:S(2)}, u32[]{:S(2)}) collective-permute-start(bf16[192,1792]{1,0:T(8,128)(2,1)S(1)} %get-tuple-element.64), channel_id=1, source_target_pairs={{0,4},{4,0},{1,5},{5,1},{2,6},{6,2},{3,7},{7,3},{8,12},{12,8},{9,1... | collective-permute-start | bytes 2064392 | tf_op jit(solution)/shard_map/ppermute | solution.py:16
  172.4 26.4 %all-to-all-start.3 = ((bf16[16,24,1792]{2,1,0:T(8,128)(2,1)}), bf16[16,24,1792]{2,1,0:T(8,128)(2,1)}, u32[]{:S(2)}, u32[]{:S(2)}) async-start(bf16[16,24,1792]{2,1,0:T(8,128)(2,1)} %bitcast.33), calls=%async_computation.3 | async-start | bytes 2752512 | tf_op jit(solution)/shard_map/all_to_all | solution.py:259
  179.0 18.4 %collective-permute-start.20 = (bf16[128,1792]{1,0:T(8,128)(2,1)S(1)}, bf16[128,1792]{1,0:T(8,128)(2,1)S(1)}, u32[]{:S(2)}, u32[]{:S(2)}) collective-permute-start(bf16[128,1792]{1,0:T(8,128)(2,1)S(1)} %get-tuple-element.68), channel_id=1, source_target_pairs={{0,128},{128,0},{1,129},{129,1},{2,130},{130,2},{3,131},{131,3},{4... | collective-permute-start | bytes 1376264 | tf_op jit(solution)/shard_map/ppermute | solution.py:16
  179.1 13.0 %collective-permute-start.21 = (f32[2,128]{0,1:T(8,128)S(1)}, f32[2,128]{0,1:T(8,128)S(1)}, u32[]{:S(2)}, u32[]{:S(2)}) collective-permute-start(f32[2,128]{0,1:T(8,128)S(1)} %slice.108), channel_id=1, source_target_pairs={{0,128},{128,0},{1,129},{129,1},{2,130},{130,2},{3,131},{131,3},{4... | collective-permute-start | bytes 3080 | tf_op jit(solution)/shard_map/ppermute | solution.py:16
  192.1 5.3 %collective-permute-start.22 = (f32[2,128]{0,1:T(8,128)S(1)}, f32[2,128]{0,1:T(8,128)S(1)}, u32[]{:S(2)}, u32[]{:S(2)}) collective-permute-start(f32[2,128]{0,1:T(8,128)S(1)} %slice_add_fusion.1), channel_id=1, source_target_pairs={{0,1},{1,0},{2,3},{3,2},{4,7},{7,4},{5,6},{6,5},{8,9},{9,8},{10,11... | collective-permute-start | bytes 3080 | tf_op jit(solution)/shard_map/ppermute | solution.py:24
  197.4 7.1 %collective-permute-start.23 = (f32[2,128]{0,1:T(8,128)S(1)}, f32[2,128]{0,1:T(8,128)S(1)}, u32[]{:S(2)}, u32[]{:S(2)}) collective-permute-start(f32[2,128]{0,1:T(8,128)S(1)} %add.54), channel_id=1, source_target_pairs={{0,3},{3,0},{1,2},{2,1},{4,5},{5,4},{6,7},{7,6},{8,11},{11,8},{9,1... | collective-permute-start | bytes 3080 | tf_op jit(solution)/shard_map/ppermute | solution.py:24
  201.0 11.4 %collective-permute-start.24 = (bf16[128,1792]{1,0:T(8,128)(2,1)S(1)}, bf16[128,1792]{1,0:T(8,128)(2,1)S(1)}, u32[]{:S(2)}, u32[]{:S(2)}) collective-permute-start(bf16[128,1792]{1,0:T(8,128)(2,1)S(1)} %slice.155), channel_id=1, source_target_pairs={{0,128},{128,0},{1,129},{129,1},{2,130},{130,2},{3,131},{131,3},{4... | collective-permute-start | bytes 1376264 | tf_op jit(solution)/shard_map/ppermute | solution.py:16
  (29 other events, 175.6 us)

commit v5 on v4

--- a/solution.py
+++ b/solution.py
@@ -357,12 +357,14 @@
     grad_p = grad_p.T
     theirs = tie(swap(grad_p[:, tok_rows:], "z"), (grad_gate, grad_up))
     grad_p = grad_p[:, :tok_rows] + theirs
-    grad_p = tie(grad_p + cross(grad_p, FIRST), out_theirs)
+    grad_p = tie(grad_p, out_theirs)
+    got_p = cross(grad_p, FIRST)
+
+    tok_part = dot(assign, returned_in, NN)
+    tok_away = tok_part[tok_rows:].astype(BF)
+    grad_tokens = (tok_part[:tok_rows] + swap(tok_away, "z").astype(F32)).astype(BF)
+    grad_p = grad_p + tie(got_p, tok_away)
     grad_p = grad_p + cross(grad_p, SECOND)
-
-    tok_part = dot(assign, returned_in, NN)
-    grad_tokens = (tok_part[:tok_rows] + swap(tok_part[tok_rows:].astype(BF), "z").astype(F32)).astype(BF)
-
     return (moe_out, grad_p.T, grad_tokens, grad_gate[None], grad_up[None], grad_down[None])
 
 

time: 214 us -> 214 us (level)
  waiting for transfers between devices: 105 us -> 102 us
    all_to_all x4, waiting for transfers between devices: 14.6 us -> 20.6 us  [exchange(): lax.all_to_all(rows.reshape(chips, planes * capacity, quarter), ('x', 'y'...]
    ppermute x15, waiting for transfers between devices: 38.7 us -> 33.1 us  [swap(): return lax.ppermute(value, axis, PAIR)]
    ppermute x10, waiting for transfers between devices: 51.2 us -> 48.6 us  [cross(): return lax.ppermute(value, ('core', 'tensor'), step)]
where the time goes in v5:
time: 214 us; the launch traced here: 212 us
  waiting for transfers between devices  102 us (48%)
  starting transfers between devices  54.8 us (26%)
  Pallas kernels  26 us (12%)
  matrix products  12.6 us (6%)
  local copies, waits for them, and re-layouts  11.1 us (5%)
  other arithmetic  3.79 us (2%)
    ppermute x10, waiting for transfers between devices, cross(): return lax.ppermute(value, ('core', 'tensor'), step)  48.6 us
    ppermute x15, waiting for transfers between devices, swap(): return lax.ppermute(value, axis, PAIR)  33.1 us
    pallas_call x11, Pallas kernels, local_call(): pl.pallas_call(kernel, in_specs=[pl.BlockSpec(memory_space=pltpu.SMEM)] +...  26 us
    all_to_all x4, starting transfers between devices, exchange(): lax.all_to_all(rows.reshape(chips, planes * capacity, quarter), ('x', 'y'...  25.2 us
    ppermute x10, starting transfers between devices, cross(): return lax.ppermute(value, ('core', 'tensor'), step)  20.7 us
    all_to_all x4, waiting for transfers between devices, exchange(): lax.all_to_all(rows.reshape(chips, planes * capacity, quarter), ('x', 'y'...  20.6 us
    dot_general x4, matrix products, dot(): return lax.dot_general(a, b, (dims, ((), ())), preferred_element_type=F32)  12.6 us
    ppermute x15, starting transfers between devices, swap(): return lax.ppermute(value, axis, PAIR)  8.93 us
  transfers between devices with their start and end apart: 29, of which 21 were waited for; matrix products, arithmetic and copies ran while one was open for 9% of the time, Pallas kernels for 11%

profile of v5, /device:TPU:32, one launch (start us, length us, event | category | flops | bytes accessed | tf_op | source)
XLA Modules:
  0.0 211.8 jit_solution(13152019042857239010)
XLA Ops:
  3.7 10.9 %collective-permute-done.refs_2_ = s32[128,2]{1,0:T(8,128)S(1)} collective-permute-done((s32[128,2]{1,0:T(8,128)S(1)}, s32[128,2]{1,0:T(8,128)S(1)}, u32[]{:S(2)}, u32[]{:S(2)}) %collective-permute-start) | collective-permute-done | bytes 1056 | tf_op jit(solution)/shard_map/ppermute | solution.py:16
  19.1 7.2 %all-to-all-start = ((bf16[16,24,1792]{2,1,0:T(8,128)(2,1)}), bf16[16,24,1792]{2,1,0:T(8,128)(2,1)S(1)}, u32[]{:S(2)}, u32[]{:S(2)}) async-start(bf16[16,24,1792]{2,1,0:T(8,128)(2,1)} %bitcast.3), calls=%async_computation | async-start | bytes 2752512 | tf_op jit(solution)/shard_map/all_to_all | solution.py:259
  28.4 9.1 %collective-permute-done.1 = f32[128,2]{0,1:T(2,128)S(1)} collective-permute-done((f32[128,2]{0,1:T(2,128)S(1)}, f32[128,2]{0,1:T(2,128)S(1)}, u32[]{:S(2)}, u32[]{:S(2)}) %collective-permute-start.1) | collective-permute-done | bytes 1056 | tf_op jit(solution)/shard_map/ppermute | solution.py:16
  41.1 5.7 %all-to-all-done = bf16[16,24,1792]{2,1,0:T(8,128)(2,1)S(1)} async-done(((bf16[16,24,1792]{2,1,0:T(8,128)(2,1)}), bf16[16,24,1792]{2,1,0:T(8,128)(2,1)S(1)}, u32[]{:S(2)}, u32[]{:S(2)}) %all-to-all-start) | async-done | bytes 1376288 | tf_op jit(solution)/shard_map/all_to_all | solution.py:259
  46.8 4.5 %all-to-all-start.1 = ((bf16[16,24,1792]{2,1,0:T(8,128)(2,1)}), bf16[16,24,1792]{2,1,0:T(8,128)(2,1)}, u32[]{:S(2)}, u32[]{:S(2)}) async-start(bf16[16,24,1792]{2,1,0:T(8,128)(2,1)} %bitcast.85), calls=%async_computation.1 | async-start | bytes 2752512 | tf_op jit(solution)/shard_map/all_to_all | solution.py:259
  54.6 5.3 %shard_map.121 = (f32[2,192,1024]{2,1,0:T(8,128)S(1)}, bf16[2,192,1024]{2,1,0:T(8,128)(2,1)}, bf16[2,2,192,1792]{3,2,1,0:T(8,128)(2,1)S(1)}) custom-call(s32[2]{0:T(128)S(1)} %pad_add_fusion._.refs_0_, bf16[384,1792]{1,0:T(8,128)(2,1)S(1)} %bitcast.83, bf16[192,1792]{1,0:T(8,128)(2,1)S(1)} %collective-permute-done.4.refs_2_, ...), custom_call_target="tpu_custom_call" | custom-call | flops 1000 | bytes 1000 | tf_op jit(solution)/shard_map/pallas_call | solution.py:42
  62.6 3.3 %collective-permute-start.10 = (bf16[2,192,1024]{2,1,0:T(8,128)(2,1)}, bf16[2,192,1024]{2,1,0:T(8,128)(2,1)S(1)}, u32[]{:S(2)}, u32[]{:S(2)}) collective-permute-start(bf16[2,192,1024]{2,1,0:T(8,128)(2,1)} %get-tuple-element.47), channel_id=1, source_target_pairs={{0,1},{1,0},{2,3},{3,2},{4,7},{7,4},{5,6},{6,5},{8,9},{9,8},{10,11... | collective-permute-start | bytes 2359304 | tf_op jit(solution)/shard_map/ppermute | solution.py:24
  65.8 3.9 %all-to-all-done.1 = bf16[16,24,1792]{2,1,0:T(8,128)(2,1)} async-done(((bf16[16,24,1792]{2,1,0:T(8,128)(2,1)}), bf16[16,24,1792]{2,1,0:T(8,128)(2,1)}, u32[]{:S(2)}, u32[]{:S(2)}) %all-to-all-start.1) | async-done | bytes 1376288 | tf_op jit(solution)/shard_map/all_to_all | solution.py:259
  74.3 3.6 %shard_map.122 = (f32[2,192,512]{2,1,0:T(8,128)S(1)}, bf16[2,192,512]{2,1,0:T(8,128)(2,1)S(1)}, bf16[2,2,192,1792]{3,2,1,0:T(8,128)(2,1)S(1)}) custom-call(s32[2]{0:T(128)S(1)} %pad_add_fusion._.refs_0_, bf16[384,1792]{1,0:T(8,128)(2,1)} %bitcast.6.refs_1_, bf16[192,1792]{1,0:T(8,128)(2,1)S(1)} %collective-permute-done.6.refs_2_, ...), custom_call_target="tpu_custom_call" | custom-call | flops 1000 | bytes 1000 | tf_op jit(solution)/shard_map/pallas_call | solution.py:42
  77.9 3.4 %collective-permute-start.8 = (bf16[2,192,512]{2,1,0:T(8,128)(2,1)S(1)}, bf16[2,192,512]{2,1,0:T(8,128)(2,1)S(1)}, u32[]{:S(2)}, u32[]{:S(2)}) collective-permute-start(bf16[2,192,512]{2,1,0:T(8,128)(2,1)S(1)} %get-tuple-element.50), channel_id=1, source_target_pairs={{0,1},{1,0},{2,3},{3,2},{4,7},{7,4},{5,6},{6,5},{8,9},{9,8},{10,11... | collective-permute-start | bytes 1179656 | tf_op jit(solution)/shard_map/ppermute | solution.py:24
  84.7 7.2 %collective-permute-start.11 = (bf16[192,1024]{1,0:T(8,128)(2,1)S(1)}, bf16[192,1024]{1,0:T(8,128)(2,1)S(1)}, u32[]{:S(2)}, u32[]{:S(2)}) collective-permute-start(bf16[192,1024]{1,0:T(8,128)(2,1)S(1)} %fusion.16), channel_id=1, source_target_pairs={{0,3},{3,0},{1,2},{2,1},{4,5},{5,4},{6,7},{7,6},{8,11},{11,8},{9,1... | collective-permute-start | bytes 1179656 | tf_op jit(solution)/shard_map/ppermute | solution.py:24
  91.9 8.9 %collective-permute-done.8 = bf16[2,192,512]{2,1,0:T(8,128)(2,1)S(1)} collective-permute-done((bf16[2,192,512]{2,1,0:T(8,128)(2,1)S(1)}, bf16[2,192,512]{2,1,0:T(8,128)(2,1)S(1)}, u32[]{:S(2)}, u32[]{:S(2)}) %collective-permute-start.8) | collective-permute-done | bytes 393248 | tf_op jit(solution)/shard_map/ppermute | solution.py:24
  101.2 5.0 %collective-permute-done.11 = bf16[192,1024]{1,0:T(8,128)(2,1)S(1)} collective-permute-done((bf16[192,1024]{1,0:T(8,128)(2,1)S(1)}, bf16[192,1024]{1,0:T(8,128)(2,1)S(1)}, u32[]{:S(2)}, u32[]{:S(2)}) %collective-permute-start.11) | collective-permute-done | bytes 393248 | tf_op jit(solution)/shard_map/ppermute | solution.py:24
  106.7 8.1 %collective-permute-done.12 = bf16[192,512]{1,0:T(8,128)(2,1)S(1)} collective-permute-done((bf16[192,512]{1,0:T(8,128)(2,1)S(1)}, bf16[192,512]{1,0:T(8,128)(2,1)S(1)}, u32[]{:S(2)}, u32[]{:S(2)}) %collective-permute-start.12) | collective-permute-done | bytes 196640 | tf_op jit(solution)/shard_map/ppermute | solution.py:24
  118.2 16.2 %collective-permute-done.15 = bf16[2,192,512]{2,1,0:T(8,128)(2,1)S(1)} collective-permute-done((bf16[2,192,512]{2,1,0:T(8,128)(2,1)S(1)}, bf16[2,192,512]{2,1,0:T(8,128)(2,1)S(1)}, u32[]{:S(2)}, u32[]{:S(2)}) %collective-permute-start.15) | collective-permute-done | bytes 393248 | tf_op jit(solution)/shard_map/ppermute | solution.py:24
  141.7 8.9 %all-to-all-start.2 = ((bf16[16,24,1792]{2,1,0:T(8,128)(2,1)}), bf16[16,24,1792]{2,1,0:T(8,128)(2,1)S(1)}, u32[]{:S(2)}, u32[]{:S(2)}) async-start(bf16[16,24,1792]{2,1,0:T(8,128)(2,1)} %bitcast.86), calls=%async_computation.2 | async-start | bytes 2752512 | tf_op jit(solution)/shard_map/all_to_all | solution.py:259
  150.6 4.8 %convolution_convert_fusion.2 = bf16[512,1792]{1,0:T(8,128)(2,1)} fusion(bf16[768,512]{1,0:T(8,128)(2,1)S(1)} %bitcast.81, bf16[768,1792]{1,0:T(8,128)(2,1)} %bitcast.87), kind=kOutput, calls=%fused_computation.2 | convolution fusion | flops 1410203648 | bytes 5373952 | tf_op jit(solution)/shard_map/dot_general | solution.py:32
  155.4 4.0 %collective-permute-done.14.refs_2_ = bf16[4,192,512]{2,1,0:T(8,128)(2,1)} collective-permute-done((bf16[4,192,512]{2,1,0:T(8,128)(2,1)S(1)}, bf16[4,192,512]{2,1,0:T(8,128)(2,1)}, u32[]{:S(2)}, u32[]{:S(2)}) %collective-permute-start.14) | collective-permute-done | bytes 786464 | tf_op jit(solution)/shard_map/ppermute | solution.py:24
  167.4 5.0 %all-to-all-done.2 = bf16[16,24,1792]{2,1,0:T(8,128)(2,1)S(1)} async-done(((bf16[16,24,1792]{2,1,0:T(8,128)(2,1)}), bf16[16,24,1792]{2,1,0:T(8,128)(2,1)S(1)}, u32[]{:S(2)}, u32[]{:S(2)}) %all-to-all-start.2) | async-done | bytes 1376288 | tf_op jit(solution)/shard_map/all_to_all | solution.py:259
  172.4 4.6 %all-to-all-start.3 = ((bf16[16,24,1792]{2,1,0:T(8,128)(2,1)}), bf16[16,24,1792]{2,1,0:T(8,128)(2,1)}, u32[]{:S(2)}, u32[]{:S(2)}) async-start(bf16[16,24,1792]{2,1,0:T(8,128)(2,1)} %bitcast.32), calls=%async_computation.3 | async-start | bytes 2752512 | tf_op jit(solution)/shard_map/all_to_all | solution.py:259
  188.3 3.8 %collective-permute-done.21 = f32[2,128]{0,1:T(8,128)S(1)} collective-permute-done((f32[2,128]{0,1:T(8,128)S(1)}, f32[2,128]{0,1:T(8,128)S(1)}, u32[]{:S(2)}, u32[]{:S(2)}) %collective-permute-start.21) | collective-permute-done | bytes 1056 | tf_op jit(solution)/shard_map/ppermute | solution.py:16
  192.2 6.1 %all-to-all-done.3 = bf16[16,24,1792]{2,1,0:T(8,128)(2,1)} async-done(((bf16[16,24,1792]{2,1,0:T(8,128)(2,1)}), bf16[16,24,1792]{2,1,0:T(8,128)(2,1)}, u32[]{:S(2)}, u32[]{:S(2)}) %all-to-all-start.3) | async-done | bytes 1376288 | tf_op jit(solution)/shard_map/all_to_all | solution.py:259
  201.4 3.2 %collective-permute-start.23 = (f32[2,128]{0,1:T(8,128)S(1)}, f32[2,128]{0,1:T(8,128)S(1)}, u32[]{:S(2)}, u32[]{:S(2)}) collective-permute-start(f32[2,128]{0,1:T(8,128)S(1)} %add.54), channel_id=1, source_target_pairs={{0,3},{3,0},{1,2},{2,1},{4,5},{5,4},{6,7},{7,6},{8,11},{11,8},{9,1... | collective-permute-start | bytes 3080 | tf_op jit(solution)/shard_map/ppermute | solution.py:24
  205.4 3.4 %collective-permute-done.23 = f32[2,128]{0,1:T(8,128)S(1)} collective-permute-done((f32[2,128]{0,1:T(8,128)S(1)}, f32[2,128]{0,1:T(8,128)S(1)}, u32[]{:S(2)}, u32[]{:S(2)}) %collective-permute-start.23) | collective-permute-done | bytes 1056 | tf_op jit(solution)/shard_map/ppermute | solution.py:24
  (125 shorter events, 64.8 us)
Async XLA Ops:
  0.6 15.3 %collective-permute-start.2 = (bf16[128,1792]{1,0:T(8,128)(2,1)}, bf16[128,1792]{1,0:T(8,128)(2,1)S(1)}, u32[]{:S(2)}, u32[]{:S(2)}) collective-permute-start(bf16[128,1792]{1,0:T(8,128)(2,1)} %mine.4), channel_id=1, source_target_pairs={{0,128},{128,0},{1,129},{129,1},{2,130},{130,2},{3,131},{131,3},{4... | collective-permute-start | bytes 1376264 | tf_op jit(solution)/shard_map/ppermute | solution.py:16
  3.3 11.2 %collective-permute-start = (s32[128,2]{1,0:T(8,128)S(1)}, s32[128,2]{1,0:T(8,128)S(1)}, u32[]{:S(2)}, u32[]{:S(2)}) collective-permute-start(s32[128,2]{1,0:T(8,128)S(1)} %copy.19.refs_1_), channel_id=1, source_target_pairs={{0,128},{128,0},{1,129},{129,1},{2,130},{130,2},{3,131},{131,3},{4... | collective-permute-start | bytes 3080 | tf_op jit(solution)/shard_map/ppermute | solution.py:16
  19.1 27.6 %all-to-all-start = ((bf16[16,24,1792]{2,1,0:T(8,128)(2,1)}), bf16[16,24,1792]{2,1,0:T(8,128)(2,1)S(1)}, u32[]{:S(2)}, u32[]{:S(2)}) async-start(bf16[16,24,1792]{2,1,0:T(8,128)(2,1)} %bitcast.3), calls=%async_computation | async-start | bytes 2752512 | tf_op jit(solution)/shard_map/all_to_all | solution.py:259
  26.3 11.4 %collective-permute-start.3 = (bf16[128,1792]{1,0:T(8,128)(2,1)S(1)}, bf16[128,1792]{1,0:T(8,128)(2,1)S(1)}, u32[]{:S(2)}, u32[]{:S(2)}) collective-permute-start(bf16[128,1792]{1,0:T(8,128)(2,1)S(1)} %copy-done.8), channel_id=1, source_target_pairs={{0,128},{128,0},{1,129},{129,1},{2,130},{130,2},{3,131},{131,3},{4... | collective-permute-start | bytes 1376264 | tf_op jit(solution)/shard_map/ppermute | solution.py:16
  26.7 10.9 %collective-permute-start.1 = (f32[128,2]{0,1:T(2,128)S(1)}, f32[128,2]{0,1:T(2,128)S(1)}, u32[]{:S(2)}, u32[]{:S(2)}) collective-permute-start(f32[128,2]{0,1:T(2,128)S(1)} %copy-done.23), channel_id=1, source_target_pairs={{0,128},{128,0},{1,129},{129,1},{2,130},{130,2},{3,131},{131,3},{4... | collective-permute-start | bytes 3080 | tf_op jit(solution)/shard_map/ppermute | solution.py:16
  46.8 22.9 %all-to-all-start.1 = ((bf16[16,24,1792]{2,1,0:T(8,128)(2,1)}), bf16[16,24,1792]{2,1,0:T(8,128)(2,1)}, u32[]{:S(2)}, u32[]{:S(2)}) async-start(bf16[16,24,1792]{2,1,0:T(8,128)(2,1)} %bitcast.85), calls=%async_computation.1 | async-start | bytes 2752512 | tf_op jit(solution)/shard_map/all_to_all | solution.py:259
  62.6 21.8 %collective-permute-start.10 = (bf16[2,192,1024]{2,1,0:T(8,128)(2,1)}, bf16[2,192,1024]{2,1,0:T(8,128)(2,1)S(1)}, u32[]{:S(2)}, u32[]{:S(2)}) collective-permute-start(bf16[2,192,1024]{2,1,0:T(8,128)(2,1)} %get-tuple-element.47), channel_id=1, source_target_pairs={{0,1},{1,0},{2,3},{3,2},{4,7},{7,4},{5,6},{6,5},{8,9},{9,8},{10,11... | collective-permute-start | bytes 2359304 | tf_op jit(solution)/shard_map/ppermute | solution.py:24
  77.9 22.9 %collective-permute-start.8 = (bf16[2,192,512]{2,1,0:T(8,128)(2,1)S(1)}, bf16[2,192,512]{2,1,0:T(8,128)(2,1)S(1)}, u32[]{:S(2)}, u32[]{:S(2)}) collective-permute-start(bf16[2,192,512]{2,1,0:T(8,128)(2,1)S(1)} %get-tuple-element.50), channel_id=1, source_target_pairs={{0,1},{1,0},{2,3},{3,2},{4,7},{7,4},{5,6},{6,5},{8,9},{9,8},{10,11... | collective-permute-start | bytes 1179656 | tf_op jit(solution)/shard_map/ppermute | solution.py:24
  84.7 21.6 %collective-permute-start.11 = (bf16[192,1024]{1,0:T(8,128)(2,1)S(1)}, bf16[192,1024]{1,0:T(8,128)(2,1)S(1)}, u32[]{:S(2)}, u32[]{:S(2)}) collective-permute-start(bf16[192,1024]{1,0:T(8,128)(2,1)S(1)} %fusion.16), channel_id=1, source_target_pairs={{0,3},{3,0},{1,2},{2,1},{4,5},{5,4},{6,7},{7,6},{8,11},{11,8},{9,1... | collective-permute-start | bytes 1179656 | tf_op jit(solution)/shard_map/ppermute | solution.py:24
  100.9 13.9 %collective-permute-start.9 = (bf16[192,512]{1,0:T(8,128)(2,1)S(1)}, bf16[192,512]{1,0:T(8,128)(2,1)S(1)}, u32[]{:S(2)}, u32[]{:S(2)}) collective-permute-start(bf16[192,512]{1,0:T(8,128)(2,1)S(1)} %fusion.18), channel_id=1, source_target_pairs={{0,3},{3,0},{1,2},{2,1},{4,5},{5,4},{6,7},{7,6},{8,11},{11,8},{9,1... | collective-permute-start | bytes 589832 | tf_op jit(solution)/shard_map/ppermute | solution.py:24
  106.5 8.3 %collective-permute-start.12 = (bf16[192,512]{1,0:T(8,128)(2,1)S(1)}, bf16[192,512]{1,0:T(8,128)(2,1)S(1)}, u32[]{:S(2)}, u32[]{:S(2)}) collective-permute-start(bf16[192,512]{1,0:T(8,128)(2,1)S(1)} %multiply_convert_fusion.2), channel_id=1, source_target_pairs={{0,1},{1,0},{2,3},{3,2},{4,7},{7,4},{5,6},{6,5},{8,9},{9,8},{10,11... | collective-permute-start | bytes 589832 | tf_op jit(solution)/shard_map/ppermute | solution.py:24
  114.8 19.6 %collective-permute-start.15 = (bf16[2,192,512]{2,1,0:T(8,128)(2,1)S(1)}, bf16[2,192,512]{2,1,0:T(8,128)(2,1)S(1)}, u32[]{:S(2)}, u32[]{:S(2)}) collective-permute-start(bf16[2,192,512]{2,1,0:T(8,128)(2,1)S(1)} %pad_maximum_fusion.3), channel_id=1, source_target_pairs={{0,3},{3,0},{1,2},{2,1},{4,5},{5,4},{6,7},{7,6},{8,11},{11,8},{9,1... | collective-permute-start | bytes 1179656 | tf_op jit(solution)/shard_map/ppermute | solution.py:24
  115.2 21.4 %collective-permute-start.13 = (bf16[2,192,512]{2,1,0:T(8,128)(2,1)S(1)}, bf16[2,192,512]{2,1,0:T(8,128)(2,1)S(1)}, u32[]{:S(2)}, u32[]{:S(2)}) collective-permute-start(bf16[2,192,512]{2,1,0:T(8,128)(2,1)S(1)} %pad_maximum_fusion.2), channel_id=1, source_target_pairs={{0,1},{1,0},{2,3},{3,2},{4,7},{7,4},{5,6},{6,5},{8,9},{9,8},{10,11... | collective-permute-start | bytes 1179656 | tf_op jit(solution)/shard_map/ppermute | solution.py:24
  136.1 3.1 %collective-permute-start.17 = (bf16[192,1792]{1,0:T(8,128)(2,1)S(1)}, bf16[192,1792]{1,0:T(8,128)(2,1)S(1)}, u32[]{:S(2)}, u32[]{:S(2)}) collective-permute-start(bf16[192,1792]{1,0:T(8,128)(2,1)S(1)} %get-tuple-element.58), channel_id=1, source_target_pairs={{0,4},{4,0},{1,5},{5,1},{2,6},{6,2},{3,7},{7,3},{8,12},{12,8},{9,1... | collective-permute-start | bytes 2064392 | tf_op jit(solution)/shard_map/ppermute | solution.py:16
  136.6 22.7 %collective-permute-start.14 = (bf16[4,192,512]{2,1,0:T(8,128)(2,1)S(1)}, bf16[4,192,512]{2,1,0:T(8,128)(2,1)}, u32[]{:S(2)}, u32[]{:S(2)}) collective-permute-start(bf16[4,192,512]{2,1,0:T(8,128)(2,1)S(1)} %pad_maximum_fusion.refs_1_), channel_id=1, source_target_pairs={{0,3},{3,0},{1,2},{2,1},{4,5},{5,4},{6,7},{7,6},{8,11},{11,8},{9,1... | collective-permute-start | bytes 2359304 | tf_op jit(solution)/shard_map/ppermute | solution.py:24
  141.7 30.7 %all-to-all-start.2 = ((bf16[16,24,1792]{2,1,0:T(8,128)(2,1)}), bf16[16,24,1792]{2,1,0:T(8,128)(2,1)S(1)}, u32[]{:S(2)}, u32[]{:S(2)}) async-start(bf16[16,24,1792]{2,1,0:T(8,128)(2,1)} %bitcast.86), calls=%async_computation.2 | async-start | bytes 2752512 | tf_op jit(solution)/shard_map/all_to_all | solution.py:259
  162.1 3.4 %collective-permute-start.18 = (bf16[192,1792]{1,0:T(8,128)(2,1)S(1)}, bf16[192,1792]{1,0:T(8,128)(2,1)S(1)}, u32[]{:S(2)}, u32[]{:S(2)}) collective-permute-start(bf16[192,1792]{1,0:T(8,128)(2,1)S(1)} %get-tuple-element.64), channel_id=1, source_target_pairs={{0,4},{4,0},{1,5},{5,1},{2,6},{6,2},{3,7},{7,3},{8,12},{12,8},{9,1... | collective-permute-start | bytes 2064392 | tf_op jit(solution)/shard_map/ppermute | solution.py:16
  162.2 3.3 %collective-permute-start.19 = (bf16[192,1792]{1,0:T(8,128)(2,1)S(1)}, bf16[192,1792]{1,0:T(8,128)(2,1)S(1)}, u32[]{:S(2)}, u32[]{:S(2)}) collective-permute-start(bf16[192,1792]{1,0:T(8,128)(2,1)S(1)} %get-tuple-element.65), channel_id=1, source_target_pairs={{0,4},{4,0},{1,5},{5,1},{2,6},{6,2},{3,7},{7,3},{8,12},{12,8},{9,1... | collective-permute-start | bytes 2064392 | tf_op jit(solution)/shard_map/ppermute | solution.py:16
  172.4 25.8 %all-to-all-start.3 = ((bf16[16,24,1792]{2,1,0:T(8,128)(2,1)}), bf16[16,24,1792]{2,1,0:T(8,128)(2,1)}, u32[]{:S(2)}, u32[]{:S(2)}) async-start(bf16[16,24,1792]{2,1,0:T(8,128)(2,1)} %bitcast.32), calls=%async_computation.3 | async-start | bytes 2752512 | tf_op jit(solution)/shard_map/all_to_all | solution.py:259
  179.0 13.1 %collective-permute-start.20 = (bf16[128,1792]{1,0:T(8,128)(2,1)S(1)}, bf16[128,1792]{1,0:T(8,128)(2,1)S(1)}, u32[]{:S(2)}, u32[]{:S(2)}) collective-permute-start(bf16[128,1792]{1,0:T(8,128)(2,1)S(1)} %get-tuple-element.69), channel_id=1, source_target_pairs={{0,128},{128,0},{1,129},{129,1},{2,130},{130,2},{3,131},{131,3},{4... | collective-permute-start | bytes 1376264 | tf_op jit(solution)/shard_map/ppermute | solution.py:16
  179.1 13.0 %collective-permute-start.21 = (f32[2,128]{0,1:T(8,128)S(1)}, f32[2,128]{0,1:T(8,128)S(1)}, u32[]{:S(2)}, u32[]{:S(2)}) collective-permute-start(f32[2,128]{0,1:T(8,128)S(1)} %slice.108), channel_id=1, source_target_pairs={{0,128},{128,0},{1,129},{129,1},{2,130},{130,2},{3,131},{131,3},{4... | collective-permute-start | bytes 3080 | tf_op jit(solution)/shard_map/ppermute | solution.py:16
  192.1 8.4 %collective-permute-start.22 = (f32[2,128]{0,1:T(8,128)S(1)}, f32[2,128]{0,1:T(8,128)}, u32[]{:S(2)}, u32[]{:S(2)}) collective-permute-start(f32[2,128]{0,1:T(8,128)S(1)} %slice_add_fusion.1), channel_id=1, source_target_pairs={{0,1},{1,0},{2,3},{3,2},{4,7},{7,4},{5,6},{6,5},{8,9},{9,8},{10,11... | collective-permute-start | bytes 3080 | tf_op jit(solution)/shard_map/ppermute | solution.py:24
  200.4 10.6 %collective-permute-start.24 = (bf16[128,1792]{1,0:T(8,128)(2,1)S(1)}, bf16[128,1792]{1,0:T(8,128)(2,1)S(1)}, u32[]{:S(2)}, u32[]{:S(2)}) collective-permute-start(bf16[128,1792]{1,0:T(8,128)(2,1)S(1)} %slice.155), channel_id=1, source_target_pairs={{0,128},{128,0},{1,129},{129,1},{2,130},{130,2},{3,131},{131,3},{4... | collective-permute-start | bytes 1376264 | tf_op jit(solution)/shard_map/ppermute | solution.py:16
  201.4 7.4 %collective-permute-start.23 = (f32[2,128]{0,1:T(8,128)S(1)}, f32[2,128]{0,1:T(8,128)S(1)}, u32[]{:S(2)}, u32[]{:S(2)}) collective-permute-start(f32[2,128]{0,1:T(8,128)S(1)} %add.54), channel_id=1, source_target_pairs={{0,3},{3,0},{1,2},{2,1},{4,5},{5,4},{6,7},{7,6},{8,11},{11,8},{9,1... | collective-permute-start | bytes 3080 | tf_op jit(solution)/shard_map/ppermute | solution.py:24
  (29 other events, 177.4 us)
